TPU v7x, 32 devices: a whole 2x2x4 slice. The times are simulated.
32 devices in a mesh: groups: 2 (over x), blk: 16 (over z, y, core).
Axes of the slice: x: 2, y: 2, z: 4, core: 2. Of those that a mesh axis runs over, the one named last changes fastest.
Arguments:
- queries: bfloat16 [16384, 1536], P(('groups', 'blk')), parts along dimension 0, may hold values from -8 to 8
- key_rows: bfloat16 [16384, 1536], P(('groups', 'blk')), parts along dimension 0, may hold values from -8 to 8
- value_rows: bfloat16 [16384, 1536], P(('groups', 'blk')), parts along dimension 0, may hold values from -24 to 24
- block_mask: int32 [64, 20], P('blk'), may hold values from 0 to 1, as said below
- out_weight: bfloat16 [1536, 3072], P(None, 'blk'), may hold values from -0.5 to 0.5
Outputs:
- projected: bfloat16 [16384, 3072], P(('groups', 'blk')), parts along dimension 0
There are 2 independent parts, one for each index of `groups`. A program takes and returns all parts, laid end to end along the dimension named above; an argument that names none is the same for every part. Nothing has to cross between parts.
Inputs may be any that keep to these rules, and one draw needn't show every extreme that they name: `block_mask`: entry [b, (d + 2) * 4 + j] is 1 if query block b may attend key block j of the slab d slabs after its own in cyclic order (before it for negative d). A slab's own blocks are always admitted. For d = 2 and d = -2, the query blocks of one slab together admit exactly 2 of that slab's key blocks, in every draw.
All inputs are finite; a program needn't handle non-finite values.
Results may differ from a plain program's by a relative error of at most 0.009.
Values may be sent and summed in bfloat16 or wider, within the bound.
No kernel may reach another device: no remote copies, remote signals or barrier semaphores. Data moves between devices by JAX's collectives and lax.ppermute only.
A program may use at most 192 MiB of HBM per device.

v0:
```python
import math

import jax
import jax.numpy as jnp
from jax import lax
from jax.sharding import PartitionSpec as P

HEADS = 12
BLOCK = 128
RADIUS = 2


neg_large = -1e30


def shifted(value, axis, steps):
    count = lax.axis_size(axis)
    pairs = [(source, (source + steps) % count) for source in range(count)]
    return lax.ppermute(value, axis, pairs)


def absorb(carried, queries, key_part, value_part, allowed):
    run_max, run_sum, accumulated = carried
    tok_rows = queries.shape[0]
    head_count = HEADS
    head_size = queries.shape[1] // head_count
    key_count = key_part.shape[0]
    block_len = BLOCK
    query_heads = queries.reshape(tok_rows, head_count, head_size)
    key_heads = key_part.reshape(key_count, head_count, head_size)
    value_heads = value_part.reshape(key_count, head_count, head_size)
    scores = jnp.einsum(
        "qhe,khe->hqk", query_heads, key_heads, preferred_element_type=jnp.float32
    ) * (1.0 / math.sqrt(head_size))
    shaped = scores.reshape(
        head_count, tok_rows // block_len, block_len, key_count // block_len, block_len
    )
    keeping = (allowed > 0)[None, :, None, :, None]
    shaped = jnp.where(keeping, shaped, neg_large)
    new_max = jnp.maximum(run_max, jnp.max(shaped, axis=(3, 4)).reshape(head_count, tok_rows))
    level = new_max.reshape(head_count, tok_rows // block_len, block_len)[:, :, :, None, None]
    weights = jnp.where(keeping, jnp.exp(shaped - level), 0.0)
    factor = jnp.exp(run_max - new_max)
    run_sum = run_sum * factor + jnp.sum(weights, axis=(3, 4)).reshape(head_count, tok_rows)
    rounded_probs = weights.reshape(head_count, tok_rows, key_count).astype(jnp.bfloat16)
    update = jnp.einsum(
        "hqk,khe->qhe", rounded_probs, value_heads, preferred_element_type=jnp.float32
    )
    accumulated = accumulated * jnp.transpose(factor)[:, :, None] + update
    return (new_max, run_sum, accumulated)


def local(queries, key_rows, value_rows, block_mask, out_weight):
    tok_rows, feat_width = queries.shape
    head_count = HEADS
    radius = RADIUS
    per_slab = tok_rows // BLOCK
    key_value = jnp.stack((key_rows, value_rows))

    def columns(offset):
        return block_mask[:, (offset + radius) * per_slab : (offset + radius + 1) * per_slab]

    carried = (
        jnp.full((head_count, tok_rows), neg_large, jnp.float32),
        jnp.zeros((head_count, tok_rows), jnp.float32),
        jnp.zeros((tok_rows, head_count, feat_width // head_count), jnp.float32),
    )
    carried = absorb(carried, queries, key_rows, value_rows, columns(0))
    for direction in (1, -1):
        offset = direction
        arrived = shifted(key_value, "blk", -offset)
        carried = absorb(carried, queries, arrived[0], arrived[1], columns(offset))
    far_count = per_slab // 2
    blocked = key_value.reshape(2, per_slab, BLOCK, feat_width)
    for direction in (1, -1):
        offset = direction * radius
        wanted = columns(offset)
        used_any = jnp.max(wanted, axis=0)
        ranking = jnp.argsort((1 - used_any) * per_slab + jnp.arange(per_slab, dtype=jnp.int32))
        picked = ranking[:far_count]
        requests = shifted(picked, "blk", offset)
        chosen = jnp.take(blocked, requests, axis=1).reshape(2, far_count * BLOCK, feat_width)
        arrived = shifted(chosen, "blk", -offset)
        carried = absorb(carried, queries, arrived[0], arrived[1], jnp.take(wanted, picked, axis=1))
    run_max, run_sum, accumulated = carried
    attention = (
        (accumulated / jnp.transpose(run_sum)[:, :, None])
        .reshape(tok_rows, feat_width)
        .astype(jnp.bfloat16)
    )
    result = jnp.dot(
        attention,
        lax.all_gather(out_weight, "blk", axis=1, tiled=True),
        preferred_element_type=jnp.float32,
    )
    return result.astype(jnp.bfloat16)


def solution(mesh):
    in_specs = (
        P(("groups", "blk"), None),
        P(("groups", "blk"), None),
        P(("groups", "blk"), None),
        P("blk", None),
        P(None, "blk"),
    )
    out_specs = P(("groups", "blk"), None)
    return jax.shard_map(local, mesh=mesh, in_specs=in_specs, out_specs=out_specs, check_vma=False)
```

profile of v0, /device:TPU:0, one launch (start us, length us, event | category | flops | bytes accessed | tf_op | source)
XLA Modules:
  0.0 286.2 jit_solution(4080492890166236329)
XLA Ops:
  6.5 1.7 copy.82
  8.3 1.7 copy.86
  10.0 2.1 pad_maximum_fusion
  12.6 5.0 %collective-permute-start = (bf16[2,512,1536]{1,2,0:T(8,128)(2,1)}, bf16[2,512,1536]{1,2,0:T(8,128)(2,1)}, u32[]{:S(2)}, u32[]{:S(2)}) collective-permute-start(bf16[2,512,1536]{1,2,0:T(8,128)(2,1)} %pad_maximum_fusion), channel_id=1, source_target_pairs={{0,15},{1,0},{2,1},{3,2},{4,3},{5,4},{6,5},{7,6},{8,7},{9,8},{10,9... | collective-permute-start | bytes 9437192 | tf_op jit(solution)/shard_map/ppermute | solution.py:19
  18.4 2.3 collective-permute-start.4
  22.5 1.7 copy.81
  24.4 3.8 %pad_maximum_fusion.1 = bf16[2,4,128,1536]{3,2,1,0:T(8,128)(2,1)} fusion(bf16[1,4,128,1536]{3,2,1,0:T(8,128)(2,1)} %bitcast.263, bf16[1,4,128,1536]{3,2,1,0:T(8,128)(2,1)} %bitcast.264), kind=kLoop, calls=%fused_computation.39 | loop fusion | flops 1572864 | bytes 6291456 | tf_op jit(solution)/shard_map/stack | solution.py:58
  28.8 114.3 %collective-permute-done.4 = s32[2]{0:T(128)S(1)} collective-permute-done((s32[2]{0:T(128)S(1)}, s32[2]{0:T(128)S(1)}, u32[]{:S(2)}, u32[]{:S(2)}) %collective-permute-start.4) | collective-permute-done | bytes 40 | tf_op jit(solution)/shard_map/ppermute | solution.py:19
  143.1 3.7 %gather_fusion.3 = bf16[2,2,128,1536]{3,2,1,0:T(8,128)(2,1)} fusion(bf16[2,4,128,1536]{3,2,1,0:T(8,128)(2,1)} %pad_maximum_fusion.1, s32[1024]{0:T(1024)S(1)} %pad_clamp_fusion), kind=kCustom, calls=%fused_computation.3.clone | custom fusion | bytes 3145736 | tf_op jit(solution)/shard_map/jit(_take)/gather | solution.py:82
  146.8 1.6 select_bitcast_fusion
  149.7 3.7 %gather_fusion.1 = bf16[2,2,128,1536]{3,2,1,0:T(8,128)(2,1)} fusion(bf16[2,4,128,1536]{3,2,1,0:T(8,128)(2,1)} %pad_maximum_fusion.1, s32[1024]{0:T(1024)S(1)} %pad_clamp_fusion.2), kind=kCustom, calls=%fused_computation.1.clone | custom fusion | bytes 3145736 | tf_op jit(solution)/shard_map/jit(_take)/gather | solution.py:82
  153.4 1.6 select_bitcast_fusion.1
  156.3 4.7 %collective-permute-start.3 = (bf16[2,256,1536]{2,1,0:T(8,128)(2,1)}, bf16[2,256,1536]{2,1,0:T(8,128)(2,1)}, u32[]{:S(2)}, u32[]{:S(2)}) collective-permute-start(bf16[2,256,1536]{2,1,0:T(8,128)(2,1)} %bitcast.21), channel_id=1, source_target_pairs={{0,14},{1,15},{2,0},{3,1},{4,2},{5,3},{6,4},{7,5},{8,6},{9,7},{10,... | collective-permute-start | bytes 4718600 | tf_op jit(solution)/shard_map/ppermute | solution.py:19
  164.1 7.5 %fusion = (f32[12,512]{1,0:T(8,128)}, f32[12,512,512]{1,2,0:T(8,128)}) fusion(pred[512,512]{0,1:T(8,128)(4,1)S(1)} %bitcast.274, bf16[512,12,128]{0,2,1:T(8,128)(2,1)S(1)} %bitcast.252, bf16[512,12,128]{0,2,1:T(8,128)(2,1)S(1)} %bitcast.262), kind=kOutput, calls=%fused_computation.10 | convolution fusion | flops 814737408 | bytes 16015360 | tf_op jit(solution)/shard_map/qhe,khe->hqk/dot_general | solution.py:32
  171.6 16.1 %collective-permute-done.5 = bf16[2,256,1536]{2,1,0:T(8,128)(2,1)} collective-permute-done((bf16[2,256,1536]{2,1,0:T(8,128)(2,1)}, bf16[2,256,1536]{2,1,0:T(8,128)(2,1)}, u32[]{:S(2)}, u32[]{:S(2)}) %collective-permute-start.5) | collective-permute-done | bytes 1572896 | tf_op jit(solution)/shard_map/ppermute | solution.py:19
  187.7 2.4 fusion.75
  190.3 2.6 fusion.76
  194.4 2.3 copy.103
  196.7 2.3 copy.110
  201.6 5.5 %fusion.74 = (bf16[1,512,1536]{1,2,0:T(8,128)(2,1)}, bf16[1,512,1536]{1,2,0:T(8,128)(2,1)S(1)}) fusion(bf16[2,512,1536]{1,2,0:T(8,128)(2,1)} %collective-permute-done.1), kind=kLoop, calls=%fused_computation.129 | loop fusion | bytes 6291456 | tf_op jit(solution)/shard_map/slice | solution.py:72
  207.1 3.2 %fusion.73 = (bf16[1,512,1536]{1,2,0:T(8,128)(2,1)}, bf16[1,512,1536]{1,2,0:T(8,128)(2,1)S(1)}) fusion(bf16[2,512,1536]{1,2,0:T(8,128)(2,1)} %collective-permute-done), kind=kLoop, calls=%fused_computation.128 | loop fusion | bytes 6291456 | tf_op jit(solution)/shard_map/slice | solution.py:72
  210.3 2.3 fusion.2
  212.7 7.0 %fusion.1 = (f32[12,512]{1,0:T(8,128)S(1)}, f32[12,512,512]{2,1,0:T(8,128)}) fusion(pred[512,512]{0,1:T(8,128)(4,1)S(1)} %bitcast.277, bf16[512,12,128]{0,2,1:T(8,128)(2,1)S(1)} %bitcast.268, bf16[512,12,128]{0,2,1:T(8,128)(2,1)S(1)} %bitcast.256), kind=kOutput, calls=%fused_computation.11 | convolution fusion | flops 814737408 | bytes 16015360 | tf_op jit(solution)/shard_map/qhe,khe->hqk/dot_general | solution.py:32
  222.8 7.5 %fusion.5 = f32[12,512]{1,0:T(8,128)S(1)} fusion(f32[12,512,512]{2,1,0:T(8,128)} %get-tuple-element.48, f32[12,512]{1,0:T(8,128)S(1)} %get-tuple-element.20, pred[512,512]{0,1:T(8,128)(4,1)S(1)} %bitcast.278), kind=kLoop, calls=%fused_computation.15 | loop fusion | flops 15722496 | bytes 12894208 | tf_op jit(solution)/shard_map/reduce_sum | solution.py:44
  230.4 3.2 %fusion.7 = f32[12,512]{1,0:T(8,128)S(1)} fusion(f32[12,512,512]{2,1,0:T(8,128)S(1)} %get-tuple-element.46, f32[12,512]{1,0:T(8,128)S(1)} %get-tuple-element.19, pred[512,512]{0,1:T(8,128)(4,1)S(1)} %bitcast.272), kind=kLoop, calls=%fused_computation.17 | loop fusion | flops 15722496 | bytes 12894208 | tf_op jit(solution)/shard_map/reduce_sum | solution.py:44
  233.6 3.2 %fusion.3 = f32[12,512]{1,0:T(8,128)S(1)} fusion(f32[12,512,512]{1,2,0:T(8,128)S(1)} %bitcast.258, f32[12,512]{1,0:T(8,128)S(1)} %get-tuple-element.35, pred[512,512]{0,1:T(8,128)(4,1)S(1)} %bitcast.275), kind=kLoop, calls=%fused_computation.13 | loop fusion | flops 15722496 | bytes 12894208 | tf_op jit(solution)/shard_map/reduce_sum | solution.py:44
  236.9 3.7 %fusion.26 = f32[12,128,512]{2,1,0:T(8,128)} fusion(bf16[256,12,128]{0,2,1:T(8,128)(2,1)S(1)} %bitcast.292, f32[12,256,512]{2,1,0:T(8,128)S(1)} %bitcast.260, f32[12,512]{1,0:T(8,128)S(1)} %get-tuple-element.18, pred[512,256]{0,1:T(8,128)(4,1)S(1)} %bitcast.287), kind=kOutput, calls=%fused_computation.37 | convolution fusion | flops 410517504 | bytes 10379264 | tf_op jit(solution)/shard_map/hqk,khe->qhe/dot_general | solution.py:46
  240.6 9.9 %fusion.11 = f32[12,128,512]{2,1,0:T(8,128)} fusion(bf16[512,12,128]{0,2,1:T(8,128)(2,1)S(1)} %bitcast.281, f32[12,512,512]{2,1,0:T(8,128)} %get-tuple-element.48, f32[12,512]{1,0:T(8,128)S(1)} %get-tuple-element.20, pred[512,512]{0,1:T(8,128)(4,1)S(1)} %bitcast.279), kind=kOutput, calls=%fused_computation.24 | convolution fusion | flops 821035008 | bytes 17588224 | tf_op jit(solution)/shard_map/hqk,khe->qhe/dot_general | solution.py:46
  250.4 6.3 %fusion.9 = f32[12,128,512]{2,1,0:T(8,128)} fusion(bf16[512,12,128]{0,2,1:T(8,128)(2,1)} %bitcast.280, f32[12,512,512]{2,1,0:T(8,128)S(1)} %get-tuple-element.46, f32[12,512]{1,0:T(8,128)S(1)} %get-tuple-element.19, pred[512,512]{0,1:T(8,128)(4,1)S(1)} %bitcast.273), kind=kOutput, calls=%fused_computation.23 | convolution fusion | flops 821035008 | bytes 17588224 | tf_op jit(solution)/shard_map/hqk,khe->qhe/dot_general | solution.py:46
  256.8 4.8 %fusion.13 = f32[12,512,128]{1,2,0:T(8,128)} fusion(bf16[512,12,128]{0,2,1:T(8,128)(2,1)S(1)} %bitcast.266, f32[12,512,512]{1,2,0:T(8,128)S(1)} %bitcast.258, f32[12,512]{1,0:T(8,128)S(1)} %get-tuple-element.35, pred[512,512]{0,1:T(8,128)(4,1)S(1)} %bitcast.276), kind=kOutput, calls=%fused_computation.25 | convolution fusion | flops 821035008 | bytes 17588224 | tf_op jit(solution)/shard_map/hqk,khe->qhe/dot_general | solution.py:46
  261.6 7.5 %fusion.29 = bf16[512,12,128]{0,2,1:T(8,128)(2,1)S(1)} fusion(f32[12,128,512]{2,1,0:T(8,128)S(1)} %copy-done.14, f32[12,128,512]{2,1,0:T(8,128)} %fusion.9, f32[12,128,512]{2,1,0:T(8,128)S(1)} %copy-done.15, f32[12,512,128]{1,2,0:T(8,128)} %fusion.13, f32[512,12]{0,1:T(8,128)S(1)} %get-tuple-element.13, f32[512,12]{0,1:T(8,128)S(1)} %get-tuple-element.16, ...), kind=kOutput, calls=%fused_computation.42 | convolution fusion | flops 419168256 | bytes 21536768 | tf_op jit(solution)/shard_map/hqk,khe->qhe/dot_general | solution.py:46
  269.2 10.2 %convolution_convert_fusion = bf16[512,3072]{1,0:T(8,128)(2,1)} fusion(bf16[512,1536]{0,1:T(8,128)(2,1)S(1)} %bitcast.297, bf16[1536,3072]{0,1:T(8,128)(2,1)} %all-gather.2.cloned.1.call-done), kind=kOutput, calls=%fused_computation.31 | convolution fusion | flops 4833411072 | bytes 14155776 | tf_op jit(solution)/shard_map/dot_general | solution.py:91
  (100 shorter events, 16.8 us)
Async XLA Ops:
  6.5 11.1 %copy-start.13 = (s32[4,20]{1,0:T(4,128)S(1)}, s32[4,20]{1,0:T(4,128)}, u32[]{:S(2)}) copy-start(s32[4,20]{1,0:T(4,128)} %param.12) | copy-start | bytes 964
  6.5 262.6 %all-gather.2.cloned.1.call-start = ((), (), s32[]{:S(2)}) async-start(), calls=%async_computation | async-start | bytes 10027008 | tf_op jit(solution)/shard_map/all_gather | solution.py:93
  10.0 12.4 %copy-start.2 = (bf16[512,1536]{0,1:T(8,128)(2,1)}, bf16[512,1536]{0,1:T(8,128)(2,1)S(1)}, u32[]{:S(2)}) copy-start(bf16[512,1536]{0,1:T(8,128)(2,1)S(1)} %copy.86) | copy-start | bytes 4718596
  12.1 189.5 %collective-permute-start.1 = (bf16[2,512,1536]{1,2,0:T(8,128)(2,1)}, bf16[2,512,1536]{1,2,0:T(8,128)(2,1)}, u32[]{:S(2)}, u32[]{:S(2)}) collective-permute-start(bf16[2,512,1536]{1,2,0:T(8,128)(2,1)} %pad_maximum_fusion), channel_id=1, source_target_pairs={{0,1},{1,2},{2,3},{3,4},{4,5},{5,6},{6,7},{7,8},{8,9},{9,10},{10,1... | collective-permute-start | bytes 9437192 | tf_op jit(solution)/shard_map/ppermute | solution.py:19
  12.6 194.5 %collective-permute-start = (bf16[2,512,1536]{1,2,0:T(8,128)(2,1)}, bf16[2,512,1536]{1,2,0:T(8,128)(2,1)}, u32[]{:S(2)}, u32[]{:S(2)}) collective-permute-start(bf16[2,512,1536]{1,2,0:T(8,128)(2,1)} %pad_maximum_fusion), channel_id=1, source_target_pairs={{0,15},{1,0},{2,1},{3,2},{4,3},{5,4},{6,5},{7,6},{8,7},{9,8},{10,9... | collective-permute-start | bytes 9437192 | tf_op jit(solution)/shard_map/ppermute | solution.py:19
  18.4 124.6 %collective-permute-start.4 = (s32[2]{0:T(128)S(1)}, s32[2]{0:T(128)S(1)}, u32[]{:S(2)}, u32[]{:S(2)}) collective-permute-start(s32[2]{0:T(128)S(1)} %bitcast.296), channel_id=1, source_target_pairs={{0,14},{1,15},{2,0},{3,1},{4,2},{5,3},{6,4},{7,5},{8,6},{9,7},{10,... | collective-permute-start | bytes 32 | tf_op jit(solution)/shard_map/ppermute | solution.py:19
  21.5 128.2 %collective-permute-start.2 = (s32[2]{0:T(128)S(1)}, s32[2]{0:T(128)S(1)}, u32[]{:S(2)}, u32[]{:S(2)}) collective-permute-start(s32[2]{0:T(128)S(1)} %bitcast.295), channel_id=1, source_target_pairs={{0,2},{1,3},{2,4},{3,5},{4,6},{5,7},{6,8},{7,9},{8,10},{9,11},{10,... | collective-permute-start | bytes 32 | tf_op jit(solution)/shard_map/ppermute | solution.py:19
  149.7 38.0 %collective-permute-start.5 = (bf16[2,256,1536]{2,1,0:T(8,128)(2,1)}, bf16[2,256,1536]{2,1,0:T(8,128)(2,1)}, u32[]{:S(2)}, u32[]{:S(2)}) collective-permute-start(bf16[2,256,1536]{2,1,0:T(8,128)(2,1)} %bitcast.29), channel_id=1, source_target_pairs={{0,2},{1,3},{2,4},{3,5},{4,6},{5,7},{6,8},{7,9},{8,10},{9,11},{10,... | collective-permute-start | bytes 4718600 | tf_op jit(solution)/shard_map/ppermute | solution.py:19
  156.3 34.0 %collective-permute-start.3 = (bf16[2,256,1536]{2,1,0:T(8,128)(2,1)}, bf16[2,256,1536]{2,1,0:T(8,128)(2,1)}, u32[]{:S(2)}, u32[]{:S(2)}) collective-permute-start(bf16[2,256,1536]{2,1,0:T(8,128)(2,1)} %bitcast.21), channel_id=1, source_target_pairs={{0,14},{1,15},{2,0},{3,1},{4,2},{5,3},{6,4},{7,5},{8,6},{9,7},{10,... | collective-permute-start | bytes 4718600 | tf_op jit(solution)/shard_map/ppermute | solution.py:19
  164.1 7.5 %copy-start.4 = (pred[64,8,4,128]{3,1,2,0:T(8,128)(4,1)}, pred[64,8,4,128]{3,1,2,0:T(8,128)(4,1)S(1)}, u32[]{:S(2)}) copy-start(pred[64,8,4,128]{3,1,2,0:T(8,128)(4,1)S(1)} %copy.143) | copy-start | bytes 786436
  199.0 1.3 copy-start.9
  200.3 21.0 %copy-start = (f32[12,256,512]{2,1,0:T(8,128)}, f32[12,256,512]{2,1,0:T(8,128)S(1)}, u32[]{:S(2)}) copy-start(f32[12,256,512]{2,1,0:T(8,128)S(1)} %get-tuple-element.42) | copy-start | bytes 18874372
  201.6 18.1 %copy-start.1 = (f32[12,256,512]{2,1,0:T(8,128)}, f32[12,256,512]{2,1,0:T(8,128)S(1)}, u32[]{:S(2)}) copy-start(f32[12,256,512]{2,1,0:T(8,128)S(1)} %get-tuple-element.44) | copy-start | bytes 18874372
  210.3 2.3 copy-start.6
  212.6 7.0 %copy-start.12 = (f32[12,512]{1,0:T(8,128)S(1)}, f32[12,512]{1,0:T(8,128)}, u32[]{:S(2)}) copy-start(f32[12,512]{1,0:T(8,128)} %get-tuple-element.49) | copy-start | bytes 73732
  222.8 10.7 %slice-start = ((s8[12582912]{0:T(1024)(128)(4,1)}), s8[4194304]{0:T(1024)(128)(4,1)S(1)}, s32[]{:S(2)}) async-start(s8[12582912]{0:T(1024)(128)(4,1)} %bitcast.257), calls=%async_computation.1 | async-start | bytes 8388608
  222.8 10.7 %slice-start.1 = ((s8[12582912]{0:T(1024)(128)(4,1)}), s8[4194304]{0:T(1024)(128)(4,1)S(1)}, s32[]{:S(2)}) async-start(s8[12582912]{0:T(1024)(128)(4,1)} %bitcast.257), calls=%async_computation.2 | async-start | bytes 8388608
  230.3 3.2 %slice-start.2 = ((s8[12582912]{0:T(1024)(128)(4,1)}), s8[4194304]{0:T(1024)(128)(4,1)S(1)}, s32[]{:S(2)}) async-start(s8[12582912]{0:T(1024)(128)(4,1)} %bitcast.257), calls=%async_computation.3 | async-start | bytes 8388608
  230.3 3.2 %copy-start.5 = (pred[64,8,4,128]{3,1,2,0:T(8,128)(4,1)S(1)}, pred[64,8,4,128]{3,1,2,0:T(8,128)(4,1)}, u32[]{:S(2)}) copy-start(pred[64,8,4,128]{3,1,2,0:T(8,128)(4,1)} %copy-done.4) | copy-start | bytes 786436
  230.4 6.5 %slice-start.3 = ((s8[6291456]{0:T(1024)(128)(4,1)}), s8[4194304]{0:T(1024)(128)(4,1)S(1)}, s32[]{:S(2)}) async-start(s8[6291456]{0:T(1024)(128)(4,1)} %bitcast.259), calls=%async_computation.4 | async-start | bytes 8388608
  233.6 3.3 %slice-start.4 = ((s8[6291456]{0:T(1024)(128)(4,1)}), s8[2097152]{0:T(1024)(128)(4,1)S(1)}, s32[]{:S(2)}) async-start(s8[6291456]{0:T(1024)(128)(4,1)} %bitcast.259), calls=%async_computation.5 | async-start | bytes 4194304
  233.6 3.3 %copy-start.11 = (bf16[1,256,1536]{1,2,0:T(8,128)(2,1)S(1)}, bf16[1,256,1536]{1,2,0:T(8,128)(2,1)}, u32[]{:S(2)}) copy-start(bf16[1,256,1536]{1,2,0:T(8,128)(2,1)} %copy.103) | copy-start | bytes 2359300
  236.8 3.8 %copy-start.7 = (pred[64,8,4,128]{3,1,2,0:T(8,128)(4,1)S(1)}, pred[64,8,4,128]{3,1,2,0:T(8,128)(4,1)}, u32[]{:S(2)}) copy-start(pred[64,8,4,128]{3,1,2,0:T(8,128)(4,1)} %copy.142) | copy-start | bytes 786436
  236.8 3.7 %copy-start.8 = (bf16[1,512,1536]{1,2,0:T(8,128)(2,1)S(1)}, bf16[1,512,1536]{1,2,0:T(8,128)(2,1)}, u32[]{:S(2)}) copy-start(bf16[1,512,1536]{1,2,0:T(8,128)(2,1)} %get-tuple-element.25) | copy-start | bytes 4718596
  250.4 6.3 %copy-start.3 = (bf16[512,1536]{0,1:T(8,128)(2,1)S(1)}, bf16[512,1536]{0,1:T(8,128)(2,1)}, u32[]{:S(2)}) copy-start(bf16[512,1536]{0,1:T(8,128)(2,1)} %copy-done.2) | copy-start | bytes 4718596
  256.7 4.9 %copy-start.10 = (bf16[1,256,1536]{1,2,0:T(8,128)(2,1)S(1)}, bf16[1,256,1536]{1,2,0:T(8,128)(2,1)}, u32[]{:S(2)}) copy-start(bf16[1,256,1536]{1,2,0:T(8,128)(2,1)} %copy.110) | copy-start | bytes 2359300
  256.7 4.9 %copy-start.14 = (f32[12,128,512]{2,1,0:T(8,128)S(1)}, f32[12,128,512]{2,1,0:T(8,128)}, u32[]{:S(2)}) copy-start(f32[12,128,512]{2,1,0:T(8,128)} %fusion.26) | copy-start | bytes 9437188
  256.7 4.9 %copy-start.15 = (f32[12,128,512]{2,1,0:T(8,128)S(1)}, f32[12,128,512]{2,1,0:T(8,128)}, u32[]{:S(2)}) copy-start(f32[12,128,512]{2,1,0:T(8,128)} %fusion.11) | copy-start | bytes 9437188
Sparse Core Ops, SparseCore 0:
  21.6 126.1 all-gather.1
where the time goes:
time: 288 us; the launch traced here: 286 us
  waiting for transfers between devices  130 us (45%)
  matrix products  61.9 us (21%)
  local copies, waits for them, and re-layouts  39.5 us (14%)
  other arithmetic  28.1 us (10%)
  between operations  13.9 us (5%)
  starting transfers between devices  12.5 us (4%)
    ppermute x6, waiting for transfers between devices, shifted(): return lax.ppermute(value, axis, pairs)  130 us
    dot_general x5, matrix products, absorb(): jnp.einsum('hqk,khe->qhe', rounded_probs, value_heads, preferred_element_...  32.2 us
    dot_general x5, matrix products, absorb(): jnp.einsum('qhe,khe->hqk', query_heads, key_heads, preferred_element_type...  19.4 us
    reduce_sum x5, other arithmetic, absorb(): jnp.sum(weights, axis=(3, 4)).reshape(head_count, tok_rows)  16.9 us
    ppermute x6, starting transfers between devices, shifted(): return lax.ppermute(value, axis, pairs)  12.5 us
    dot_general x1, matrix products, local(): jnp.dot(attention, lax.all_gather(out_weight, 'blk', axis=1, tiled=True),...  10.2 us
    slice x2, local copies, waits for them, and re-layouts, local(): carried = absorb(carried, queries, arrived[0], arrived[1], columns(offset))  8.67 us
    gather x2, local copies, waits for them, and re-layouts, local(): jnp.take(blocked, requests, axis=1)  7.43 us
  transfers between devices with their start and end apart: 7, of which 2 were waited for; matrix products, arithmetic and copies ran while one was open for 40% of the time, Pallas kernels for 0%

commit v1 on v0

v1 whole, which is shorter than its diff:
```python
import math

import jax
import jax.numpy as jnp
from jax import lax
from jax.experimental import pallas as pl
from jax.experimental.pallas import tpu as pltpu
from jax.sharding import PartitionSpec as P

HEADS = 12
BLOCK = 128
RADIUS = 2
PARTS = 4

neg_large = -1e30
VMEM_LIMIT = 48 * 1024 * 1024


def moved(value, dest, count):
    return lax.ppermute(value, "blk", [(s, dest(s)) for s in range(count)])


def moved_all(value, groups, count, dest):
    pairs = []
    for g in range(groups):
        for s in range(count):
            tg, ts = dest(g, s)
            pairs.append((g * count + s, tg * count + ts))
    return lax.ppermute(value, ("groups", "blk"), pairs)


def other_core(s):
    return s ^ 1


def other_chip(s):
    return s ^ 2


def near_cross(count):
    def dest(s):
        row, place = s // 4 * 4, s % 4
        return ((row + 1), (row + 4), (row - 1), (row + 2))[place] % count

    return dest


def far_cross(count):
    def dest(s):
        return (s + (4 if s % 4 < 2 else -4)) % count

    return dest


def far_request(count):
    def dest(s):
        return (s + (-4 if s % 4 < 2 else 4)) % count

    return dest


def select_kernel(idx_ref, in_ref, out_ref):
    out_ref[...] = in_ref[...]


def select_blocks(picked, slab):
    _, two, rows, width = slab.shape
    return pl.pallas_call(
        select_kernel,
        grid_spec=pltpu.PrefetchScalarGridSpec(
            num_scalar_prefetch=1,
            grid=(2,),
            in_specs=[pl.BlockSpec((1, two, rows, width), lambda i, idx: (idx[i], 0, 0, 0))],
            out_specs=pl.BlockSpec((1, two, rows, width), lambda i, idx: (i, 0, 0, 0)),
        ),
        out_shape=jax.ShapeDtypeStruct((2, two, rows, width), slab.dtype),
        cost_estimate=pl.CostEstimate(flops=0, bytes_accessed=4 * two * rows * width * 2, transcendentals=0),
        name="select_blocks",
    )(picked, slab)


def attend_kernel(
    picks_ref, q_ref, k0_ref, v0_ref, k1_ref, v1_ref, y_ref, z_ref, f_ref, bias_ref, *rest
):
    o_ref = rest[-1]
    q = q_ref[...]
    rows, size = q.shape
    per = z_ref.shape[0]
    span = per * BLOCK
    i0 = picks_ref[0]
    i1 = picks_ref[1]
    near = z_ref[...]
    far_a = y_ref[i0]
    far_b = y_ref[i1]
    far = f_ref[...]
    keys = [
        k0_ref[...],
        k1_ref[...],
        near[:, 0].reshape(span, size),
        jnp.concatenate([far_a[0], far_b[0], far[0, 0], far[1, 0]], axis=0),
    ]
    values = [
        v0_ref[...],
        v1_ref[...],
        near[:, 1].reshape(span, size),
        jnp.concatenate([far_a[1], far_b[1], far[0, 1], far[1, 1]], axis=0),
    ]
    scores = []
    top = None
    for n, k in enumerate(keys):
        s = lax.dot_general(q, k, (((1,), (1,)), ((), ())), preferred_element_type=jnp.float32)
        if n:
            s = s.reshape(per, BLOCK, span) + bias_ref[:, :, (n - 1) * span : n * span]
            s = s.reshape(rows, span)
        scores.append(s)
        t = jnp.max(s, axis=1, keepdims=True)
        top = t if top is None else jnp.maximum(top, t)
    factor = math.log2(math.e) / math.sqrt(size)
    total = None
    ones = jnp.ones((span, size), jnp.bfloat16)
    for s, v in zip(scores, values):
        w = jnp.exp2((s - top) * factor).astype(jnp.bfloat16)
        part = jnp.dot(w, jnp.concatenate([v, ones], axis=1), preferred_element_type=jnp.float32)
        total = part if total is None else total + part
    o_ref[...] = (total[:, :size] / total[:, size:]).astype(o_ref.dtype)


def attend(part, parts, picks, queries, key_rows, value_rows, core_k, core_v, y, z, f, bias, into):
    rows, width = queries.shape
    size = width // HEADS
    per_part = HEADS // parts
    per = z.shape[0]
    col = lambda h, p: (0, part * per_part + h)
    chunk = lambda h, p: (0, 0, 0, h)
    flat = pl.BlockSpec((rows, size), col)
    in_specs = [
        flat, flat, flat, flat, flat,
        pl.BlockSpec((per, 2, BLOCK, size), chunk),
        pl.BlockSpec((per, 2, BLOCK, size), chunk),
        pl.BlockSpec((2, 2, BLOCK, size), chunk),
        pl.BlockSpec(bias.shape, lambda h, p: (0, 0, 0)),
    ]
    args = [queries, key_rows, value_rows, core_k, core_v, y, z, f, bias]
    aliases = {}
    if into is not None:
        in_specs.append(pl.BlockSpec(memory_space=pl.ANY))
        args.append(into)
        aliases = {len(args): 0}
    key_count = 4 * per * BLOCK
    return pl.pallas_call(
        attend_kernel,
        grid_spec=pltpu.PrefetchScalarGridSpec(
            num_scalar_prefetch=1,
            grid=(per_part,),
            in_specs=in_specs,
            out_specs=flat,
        ),
        out_shape=jax.ShapeDtypeStruct((rows, width), jnp.bfloat16),
        input_output_aliases=aliases,
        compiler_params=pltpu.CompilerParams(vmem_limit_bytes=VMEM_LIMIT),
        cost_estimate=pl.CostEstimate(
            flops=8 * per_part * rows * key_count * size,
            bytes_accessed=per_part * size * 2 * (2 * rows + 2 * key_count),
            transcendentals=per_part * rows * key_count,
        ),
        name="attend",
    )(picks, *args)


def project_kernel(place_ref, att_ref, a_ref, b_ref, c_ref, d_ref, o_ref):
    depth = a_ref.shape[2]
    total = None
    for n, w in enumerate((a_ref, b_ref, c_ref, d_ref)):
        first = pl.multiple_of(place_ref[n] * depth, depth)
        part = jnp.dot(att_ref[:, pl.ds(first, depth)], w[0, 0], preferred_element_type=jnp.float32)
        total = part if total is None else total + part
    o_ref[...] = total.astype(o_ref.dtype)


def project(places, attention, pieces):
    rows, width = attention.shape
    nz, ny, depth, cols = pieces[0].shape
    piece = pl.BlockSpec((1, 1, depth, cols), lambda g, p: (g // ny, g % ny, 0, 0))
    return pl.pallas_call(
        project_kernel,
        grid_spec=pltpu.PrefetchScalarGridSpec(
            num_scalar_prefetch=1,
            grid=(nz * ny,),
            in_specs=[pl.BlockSpec((rows, width), lambda g, p: (0, 0)), piece, piece, piece, piece],
            out_specs=pl.BlockSpec((rows, cols), lambda g, p: (0, p[4 + g])),
        ),
        out_shape=jax.ShapeDtypeStruct((rows, nz * ny * cols), jnp.bfloat16),
        compiler_params=pltpu.CompilerParams(vmem_limit_bytes=VMEM_LIMIT),
        cost_estimate=pl.CostEstimate(
            flops=2 * rows * width * nz * ny * cols,
            bytes_accessed=2 * (rows * width + width * nz * ny * cols + rows * nz * ny * cols),
            transcendentals=0,
        ),
        name="project",
    )(places, attention, *pieces)


def gathered_weight(out_weight, groups, count):
    rows = count // 4
    width, cols = out_weight.shape
    depth = width // 4
    x = lax.axis_index("groups")
    me = lax.axis_index("blk")
    core = me % 2
    mine = x * 2 + core
    theirs = x * 2 + 1 - core
    own = lax.dynamic_slice_in_dim(out_weight, mine * depth, depth, 0)
    give = lax.dynamic_slice_in_dim(out_weight, theirs * depth, depth, 0)
    got = moved(give, other_core, count)
    first = jnp.where(core == 0, own, got)
    second = jnp.where(core == 0, got, own)
    piece = jnp.concatenate([first, second], axis=1)
    across = moved(piece, other_chip, count)
    pair = jnp.stack([piece, across])
    up = moved(pair, lambda s: (s + 4) % count, count)
    down = moved(pair, lambda s: (s - 4) % count, count)
    up2 = moved(up, lambda s: (s + 4) % count, count)
    a = jnp.stack([pair, up, up2, down])
    b = moved_all(a, groups, count, lambda g, s: (1 - g, s))
    c = moved(a, other_core, count)
    d = moved(b, other_core, count)
    z, y = me // 4, me // 2 % 2
    places = [x * 2 + core, (1 - x) * 2 + core, x * 2 + 1 - core, (1 - x) * 2 + 1 - core]
    for shift in range(rows):
        for flip in range(2):
            places.append((z - shift) % rows * 2 + (y + flip) % 2)
    return jnp.stack(places).astype(jnp.int32), (a, b, c, d)


def local(groups, count, queries, key_rows, value_rows, block_mask, out_weight):
    tok_rows, feat_width = queries.shape
    per = tok_rows // BLOCK
    me = lax.axis_index("blk")
    place = me % 4
    lower = place < 2
    even = place % 2 == 0

    at = jnp.arange(per, dtype=jnp.int32)
    before = jnp.max(block_mask[:, :per], axis=0)
    after = jnp.max(block_mask[:, 2 * RADIUS * per :], axis=0)

    def picked(used):
        low = jnp.min(jnp.where(used > 0, at, per - 1))
        high = jnp.max(jnp.where(used > 0, at, 0))
        return jnp.stack([low, high])

    beyond = 2 * RADIUS * per
    first_y = jnp.where(lower, beyond, 0)
    first_f = jnp.where(lower, 0, beyond)
    first_1 = jnp.where(even, (RADIUS + 1) * per, (RADIUS - 1) * per)
    first_z = jnp.where(even, (RADIUS - 1) * per, (RADIUS + 1) * per)
    picks_y = picked(jnp.where(lower, after, before))
    picks_f = picked(jnp.where(lower, before, after))
    requested = moved(picks_f, far_request(count), count)
    columns = jnp.concatenate([first_1 + at, first_z + at, first_y + picks_y, first_f + picks_f])
    chosen = jnp.take(block_mask, columns, axis=1)
    bias = jnp.where(chosen > 0, 0.0, neg_large).astype(jnp.float32)
    bias = jnp.broadcast_to(bias[:, :, None], (per, 3 * per, BLOCK)).reshape(per, 1, 3 * per * BLOCK)

    core_k = moved(key_rows, other_core, count)
    core_v = moved(value_rows, other_core, count)
    wide = feat_width // PARTS
    packs = []
    for i in range(PARTS):
        k = key_rows[:, i * wide : (i + 1) * wide].reshape(per, 1, BLOCK, wide)
        v = value_rows[:, i * wide : (i + 1) * wide].reshape(per, 1, BLOCK, wide)
        packs.append(jnp.concatenate([k, v], axis=1))
    special = count == 16 and out_weight.shape[1] % 64 == 0
    if special:
        places, pieces = gathered_weight(out_weight, groups, count)
    into = None
    for i in range(PARTS):
        y = moved(packs[i], other_chip, count)
        z = moved(y, near_cross(count), count)
        f = moved(select_blocks(requested, y), far_cross(count), count)
        into = attend(
            i, PARTS, picks_y, queries, key_rows, value_rows, core_k, core_v, y, z, f, bias, into
        )
    if special:
        return project(places, into, pieces)
    full = lax.all_gather(out_weight, "blk", axis=1, tiled=True)
    return jnp.dot(into, full, preferred_element_type=jnp.float32).astype(jnp.bfloat16)


def solution(mesh):
    groups, count = mesh.shape["groups"], mesh.shape["blk"]
    in_specs = (
        P(("groups", "blk"), None),
        P(("groups", "blk"), None),
        P(("groups", "blk"), None),
        P("blk", None),
        P(None, "blk"),
    )
    out_specs = P(("groups", "blk"), None)

    def run(*args):
        return local(groups, count, *args)

    return jax.shard_map(run, mesh=mesh, in_specs=in_specs, out_specs=out_specs, check_vma=False)
```

time: 288 us -> 218 us (0.76)
  the two profiles are of different devices: /device:TPU:0 before, /device:TPU:1 now
where the time goes in v1:
time: 218 us; the launch traced here: 217 us
  waiting for transfers between devices  95.1 us (44%)
  Pallas kernels  59.2 us (27%)
  starting transfers between devices  41.2 us (19%)
  other arithmetic  11 us (5%)
  local copies, waits for them, and re-layouts  9.93 us (5%)
    ppermute x22, waiting for transfers between devices, moved(): return lax.ppermute(value, 'blk', [(s, dest(s)) for s in range(count)])  95.1 us
    ppermute x22, starting transfers between devices, moved(): return lax.ppermute(value, 'blk', [(s, dest(s)) for s in range(count)])  40 us
    pallas_call x4, Pallas kernels, attend(): pl.pallas_call(attend_kernel, grid_spec=pltpu.PrefetchScalarGridSpec(num_...  37.1 us
    pallas_call x1, Pallas kernels, project(): pl.pallas_call(project_kernel, grid_spec=pltpu.PrefetchScalarGridSpec(num...  12.5 us
    pallas_call x4, Pallas kernels, select_blocks(): pl.pallas_call(select_kernel, grid_spec=pltpu.PrefetchScalarGridSpec(num_...  9.63 us
  transfers between devices with their start and end apart: 23, of which 11 were waited for; matrix products, arithmetic and copies ran while one was open for 8% of the time, Pallas kernels for 22%

profile of v1, /device:TPU:1, one launch (start us, length us, event | category | flops | bytes accessed | tf_op | source)
XLA Modules:
  0.0 216.7 jit_solution(5625528848134332508)
XLA Ops:
  2.8 2.4 %collective-permute-start.16 = (bf16[384,384]{1,0:T(8,128)(2,1)S(1)}, bf16[384,384]{1,0:T(8,128)(2,1)S(1)}, u32[]{:S(2)}, u32[]{:S(2)}) collective-permute-start(bf16[384,384]{1,0:T(8,128)(2,1)S(1)} %pad_maximum_fusion.6), channel_id=1, source_target_pairs={{0,2},{1,3},{2,0},{3,1},{4,6},{5,7},{6,4},{7,5},{8,10},{9,11},{10,... | collective-permute-start | bytes 884744 | tf_op jit(solution)/shard_map/ppermute | solution.py:20
  5.4 7.0 %collective-permute-done.16 = bf16[384,384]{1,0:T(8,128)(2,1)S(1)} collective-permute-done((bf16[384,384]{1,0:T(8,128)(2,1)S(1)}, bf16[384,384]{1,0:T(8,128)(2,1)S(1)}, u32[]{:S(2)}, u32[]{:S(2)}) %collective-permute-start.16) | collective-permute-done | bytes 294944 | tf_op jit(solution)/shard_map/ppermute | solution.py:20
  13.7 2.1 collective-permute-start.19
  15.8 12.5 %collective-permute-done.17 = bf16[2,384,384]{2,1,0:T(8,128)(2,1)S(1)} collective-permute-done((bf16[2,384,384]{2,1,0:T(8,128)(2,1)S(1)}, bf16[2,384,384]{2,1,0:T(8,128)(2,1)S(1)}, u32[]{:S(2)}, u32[]{:S(2)}) %collective-permute-start.17) | collective-permute-done | bytes 589856 | tf_op jit(solution)/shard_map/ppermute | solution.py:20
  28.3 12.6 %collective-permute-done.19 = bf16[2,384,384]{2,1,0:T(8,128)(2,1)S(1)} collective-permute-done((bf16[2,384,384]{2,1,0:T(8,128)(2,1)S(1)}, bf16[2,384,384]{2,1,0:T(8,128)(2,1)S(1)}, u32[]{:S(2)}, u32[]{:S(2)}) %collective-permute-start.19) | collective-permute-done | bytes 589856 | tf_op jit(solution)/shard_map/ppermute | solution.py:20
  40.9 11.8 %collective-permute-done.18 = bf16[2,384,384]{2,1,0:T(8,128)(2,1)S(1)} collective-permute-done((bf16[2,384,384]{2,1,0:T(8,128)(2,1)S(1)}, bf16[2,384,384]{2,1,0:T(8,128)(2,1)S(1)}, u32[]{:S(2)}, u32[]{:S(2)}) %collective-permute-start.18) | collective-permute-done | bytes 589856 | tf_op jit(solution)/shard_map/ppermute | solution.py:20
  52.7 1.8 pad_maximum_fusion.a_ref
  55.6 1.5 fusion.9
  57.1 1.5 fusion.8
  61.7 1.3 broadcast_add_fusion
  65.3 1.5 collective-permute-start.9
  67.8 8.2 %collective-permute-done.2.in_ref.y_ref = bf16[4,2,128,384]{3,2,1,0:T(8,128)(2,1)S(1)} collective-permute-done((bf16[4,2,128,384]{3,2,1,0:T(8,128)(2,1)}, bf16[4,2,128,384]{3,2,1,0:T(8,128)(2,1)S(1)}, u32[]{:S(2)}, u32[]{:S(2)}) %collective-permute-start.2) | collective-permute-done | bytes 786464 | tf_op jit(solution)/shard_map/ppermute | solution.py:20
  75.9 7.4 %collective-permute-start = (bf16[512,1536]{1,0:T(8,128)(2,1)}, bf16[512,1536]{1,0:T(8,128)(2,1)}, u32[]{:S(2)}, u32[]{:S(2)}) collective-permute-start(bf16[512,1536]{1,0:T(8,128)(2,1)} %k0_ref.7), channel_id=1, source_target_pairs={{0,1},{1,0},{2,3},{3,2},{4,5},{5,4},{6,7},{7,6},{8,9},{9,8},{10,11... | collective-permute-start | bytes 4718600 | tf_op jit(solution)/shard_map/ppermute | solution.py:20
  83.4 9.4 %collective-permute-done.6.in_ref.y_ref = bf16[4,2,128,384]{3,2,1,0:T(8,128)(2,1)S(1)} collective-permute-done((bf16[4,2,128,384]{3,2,1,0:T(8,128)(2,1)S(1)}, bf16[4,2,128,384]{3,2,1,0:T(8,128)(2,1)S(1)}, u32[]{:S(2)}, u32[]{:S(2)}) %collective-permute-start.6) | collective-permute-done | bytes 786464 | tf_op jit(solution)/shard_map/ppermute | solution.py:20
  92.8 7.4 %collective-permute-start.1 = (bf16[512,1536]{1,0:T(8,128)(2,1)}, bf16[512,1536]{1,0:T(8,128)(2,1)}, u32[]{:S(2)}, u32[]{:S(2)}) collective-permute-start(bf16[512,1536]{1,0:T(8,128)(2,1)} %v0_ref.7), channel_id=1, source_target_pairs={{0,1},{1,0},{2,3},{3,2},{4,5},{5,4},{6,7},{7,6},{8,9},{9,8},{10,11... | collective-permute-start | bytes 4718600 | tf_op jit(solution)/shard_map/ppermute | solution.py:20
  100.2 2.4 %select_blocks.5 = bf16[2,2,128,384]{3,2,1,0:T(8,128)(2,1)} custom-call(s32[2]{0:T(128)} %copy-done.9, bf16[4,2,128,384]{3,2,1,0:T(8,128)(2,1)} %copy-done.3), custom_call_target="tpu_custom_call" | custom-call | bytes 786432 | tf_op jit(solution)/shard_map/select_blocks/pallas_call | solution.py:68
  102.6 7.0 %collective-permute-done.9.in_ref.y_ref = bf16[4,2,128,384]{3,2,1,0:T(8,128)(2,1)} collective-permute-done((bf16[4,2,128,384]{3,2,1,0:T(8,128)(2,1)}, bf16[4,2,128,384]{3,2,1,0:T(8,128)(2,1)}, u32[]{:S(2)}, u32[]{:S(2)}) %collective-permute-start.9) | collective-permute-done | bytes 786464 | tf_op jit(solution)/shard_map/ppermute | solution.py:20
  110.4 2.4 %select_blocks.6 = bf16[2,2,128,384]{3,2,1,0:T(8,128)(2,1)} custom-call(s32[2]{0:T(128)} %copy-done.9, bf16[4,2,128,384]{3,2,1,0:T(8,128)(2,1)} %collective-permute-done.9.in_ref.y_ref), custom_call_target="tpu_custom_call" | custom-call | bytes 786432 | tf_op jit(solution)/shard_map/select_blocks/pallas_call | solution.py:68
  112.8 13.7 %collective-permute-done.12.in_ref.y_ref = bf16[4,2,128,384]{3,2,1,0:T(8,128)(2,1)} collective-permute-done((bf16[4,2,128,384]{3,2,1,0:T(8,128)(2,1)}, bf16[4,2,128,384]{3,2,1,0:T(8,128)(2,1)}, u32[]{:S(2)}, u32[]{:S(2)}) %collective-permute-start.12) | collective-permute-done | bytes 786464 | tf_op jit(solution)/shard_map/ppermute | solution.py:20
  127.2 2.4 %select_blocks.7 = bf16[2,2,128,384]{3,2,1,0:T(8,128)(2,1)} custom-call(s32[2]{0:T(128)} %copy-done.9, bf16[4,2,128,384]{3,2,1,0:T(8,128)(2,1)} %collective-permute-done.12.in_ref.y_ref), custom_call_target="tpu_custom_call" | custom-call | bytes 786432 | tf_op jit(solution)/shard_map/select_blocks/pallas_call | solution.py:68
  129.6 5.6 %collective-permute-done.11.f_ref = bf16[2,2,128,384]{3,2,1,0:T(8,128)(2,1)} collective-permute-done((bf16[2,2,128,384]{3,2,1,0:T(8,128)(2,1)}, bf16[2,2,128,384]{3,2,1,0:T(8,128)(2,1)}, u32[]{:S(2)}, u32[]{:S(2)}) %collective-permute-start.11) | collective-permute-done | bytes 393248 | tf_op jit(solution)/shard_map/ppermute | solution.py:20
  135.2 9.1 %collective-permute-start.21 = (bf16[4,2,384,384]{3,2,1,0:T(8,128)(2,1)}, bf16[4,2,384,384]{3,2,1,0:T(8,128)(2,1)}, u32[]{:S(2)}, u32[]{:S(2)}) collective-permute-start(bf16[4,2,384,384]{3,2,1,0:T(8,128)(2,1)} %pad_maximum_fusion.a_ref), channel_id=1, source_target_pairs={{0,1},{1,0},{2,3},{3,2},{4,5},{5,4},{6,7},{7,6},{8,9},{9,8},{10,11... | collective-permute-start | bytes 7077896 | tf_op jit(solution)/shard_map/ppermute | solution.py:20
  144.4 3.0 %collective-permute-start.13 = (bf16[4,2,128,384]{3,2,1,0:T(8,128)(2,1)}, bf16[4,2,128,384]{3,2,1,0:T(8,128)(2,1)}, u32[]{:S(2)}, u32[]{:S(2)}) collective-permute-start(bf16[4,2,128,384]{3,2,1,0:T(8,128)(2,1)} %collective-permute-done.12.in_ref.y_ref), channel_id=1, source_target_pairs={{0,1},{1,4},{2,15},{3,2},{4,5},{5,8},{6,3},{7,6},{8,9},{9,12},{10,... | collective-permute-start | bytes 2359304 | tf_op jit(solution)/shard_map/ppermute | solution.py:20
  147.4 1.4 broadcast_add_fusion.1
  154.9 1.4 reshape.261.bias_ref
  156.3 2.4 %select_blocks.4 = bf16[2,2,128,384]{3,2,1,0:T(8,128)(2,1)} custom-call(s32[2]{0:T(128)} %copy-done.9, bf16[4,2,128,384]{3,2,1,0:T(8,128)(2,1)} %copy-done.1), custom_call_target="tpu_custom_call" | custom-call | bytes 786432 | tf_op jit(solution)/shard_map/select_blocks/pallas_call | solution.py:68
  159.8 9.3 %attend.4.rest_0_ = bf16[512,1536]{1,0:T(8,128)(2,1)S(1)} custom-call(s32[2]{0:T(128)S(1)} %get-tuple-element.12.picks_ref, bf16[512,1536]{1,0:T(8,128)(2,1)S(1)} %copy-done, bf16[512,1536]{1,0:T(8,128)(2,1)} %k0_ref.7, bf16[512,1536]{1,0:T(8,128)(2,1)} %v0_ref.7, bf16[512,1536]{1,0:T(8,128)(2,1)} %collective-permute-done.k1_ref, ...), custom_call_target="tpu_custom_call" | custom-call | flops 3221225472 | bytes 3932160 | tf_op jit(solution)/shard_map/attend/pallas_call | solution.py:150
  170.2 9.3 %attend.5.rest_0_ = bf16[512,1536]{1,0:T(8,128)(2,1)S(1)} custom-call(s32[2]{0:T(128)S(1)} %get-tuple-element.12.picks_ref, bf16[512,1536]{1,0:T(8,128)(2,1)S(1)} %copy-done, bf16[512,1536]{1,0:T(8,128)(2,1)} %k0_ref.7, bf16[512,1536]{1,0:T(8,128)(2,1)} %v0_ref.7, bf16[512,1536]{1,0:T(8,128)(2,1)} %collective-permute-done.k1_ref, ...), custom_call_target="tpu_custom_call", output_to_operand_aliasing={{}: (10, {})} | custom-call | flops 3221225472 | bytes 3932160 | tf_op jit(solution)/shard_map/attend/pallas_call | solution.py:150
  179.5 9.3 %attend.6.rest_0_ = bf16[512,1536]{1,0:T(8,128)(2,1)S(1)} custom-call(s32[2]{0:T(128)S(1)} %get-tuple-element.12.picks_ref, bf16[512,1536]{1,0:T(8,128)(2,1)S(1)} %copy-done, bf16[512,1536]{1,0:T(8,128)(2,1)} %k0_ref.7, bf16[512,1536]{1,0:T(8,128)(2,1)} %v0_ref.7, bf16[512,1536]{1,0:T(8,128)(2,1)} %collective-permute-done.k1_ref, ...), custom_call_target="tpu_custom_call", output_to_operand_aliasing={{}: (10, {})} | custom-call | flops 3221225472 | bytes 3932160 | tf_op jit(solution)/shard_map/attend/pallas_call | solution.py:150
  188.9 6.1 %collective-permute-done.5.f_ref = bf16[2,2,128,384]{3,2,1,0:T(8,128)(2,1)S(1)} collective-permute-done((bf16[2,2,128,384]{3,2,1,0:T(8,128)(2,1)S(1)}, bf16[2,2,128,384]{3,2,1,0:T(8,128)(2,1)S(1)}, u32[]{:S(2)}, u32[]{:S(2)}) %collective-permute-start.5) | collective-permute-done | bytes 393248 | tf_op jit(solution)/shard_map/ppermute | solution.py:20
  195.0 9.2 %attend.7.att_ref = bf16[512,1536]{1,0:T(8,128)(2,1)S(1)} custom-call(s32[2]{0:T(128)S(1)} %get-tuple-element.12.picks_ref, bf16[512,1536]{1,0:T(8,128)(2,1)S(1)} %copy-done, bf16[512,1536]{1,0:T(8,128)(2,1)} %k0_ref.7, bf16[512,1536]{1,0:T(8,128)(2,1)} %v0_ref.7, bf16[512,1536]{1,0:T(8,128)(2,1)} %collective-permute-done.k1_ref, ...), custom_call_target="tpu_custom_call", output_to_operand_aliasing={{}: (10, {})} | custom-call | flops 3221225472 | bytes 3932160 | tf_op jit(solution)/shard_map/attend/pallas_call | solution.py:150
  204.3 12.5 %project.1 = bf16[512,3072]{1,0:T(8,128)(2,1)} custom-call(s32[12]{0:T(128)S(1)} %stack.93.place_ref, bf16[512,1536]{1,0:T(8,128)(2,1)S(1)} %attend.7.att_ref, bf16[4,2,384,384]{3,2,1,0:T(8,128)(2,1)} %pad_maximum_fusion.a_ref, bf16[4,2,384,384]{3,2,1,0:T(8,128)(2,1)} %collective-permute-done.20.b_ref, ...), custom_call_target="tpu_custom_call" | custom-call | flops 4831838208 | bytes 14155776 | tf_op jit(solution)/shard_map/project/pallas_call | solution.py:184
  (77 shorter events, 21.5 us)
Async XLA Ops:
  1.2 1.5 collective-permute-start.15
  2.8 9.5 %collective-permute-start.16 = (bf16[384,384]{1,0:T(8,128)(2,1)S(1)}, bf16[384,384]{1,0:T(8,128)(2,1)S(1)}, u32[]{:S(2)}, u32[]{:S(2)}) collective-permute-start(bf16[384,384]{1,0:T(8,128)(2,1)S(1)} %pad_maximum_fusion.6), channel_id=1, source_target_pairs={{0,2},{1,3},{2,0},{3,1},{4,6},{5,7},{6,4},{7,5},{8,10},{9,11},{10,... | collective-permute-start | bytes 884744 | tf_op jit(solution)/shard_map/ppermute | solution.py:20
  12.5 15.8 %collective-permute-start.17 = (bf16[2,384,384]{2,1,0:T(8,128)(2,1)S(1)}, bf16[2,384,384]{2,1,0:T(8,128)(2,1)S(1)}, u32[]{:S(2)}, u32[]{:S(2)}) collective-permute-start(bf16[2,384,384]{2,1,0:T(8,128)(2,1)S(1)} %get-tuple-element.24), channel_id=1, source_target_pairs={{0,4},{1,5},{2,6},{3,7},{4,8},{5,9},{6,10},{7,11},{8,12},{9,13},{1... | collective-permute-start | bytes 1769480 | tf_op jit(solution)/shard_map/ppermute | solution.py:20
  13.7 27.2 %collective-permute-start.19 = (bf16[2,384,384]{2,1,0:T(8,128)(2,1)S(1)}, bf16[2,384,384]{2,1,0:T(8,128)(2,1)S(1)}, u32[]{:S(2)}, u32[]{:S(2)}) collective-permute-start(bf16[2,384,384]{2,1,0:T(8,128)(2,1)S(1)} %get-tuple-element.24), channel_id=1, source_target_pairs={{0,12},{1,13},{2,14},{3,15},{4,0},{5,1},{6,2},{7,3},{8,4},{9,5},{1... | collective-permute-start | bytes 1769480 | tf_op jit(solution)/shard_map/ppermute | solution.py:20
  28.3 24.3 %collective-permute-start.18 = (bf16[2,384,384]{2,1,0:T(8,128)(2,1)S(1)}, bf16[2,384,384]{2,1,0:T(8,128)(2,1)S(1)}, u32[]{:S(2)}, u32[]{:S(2)}) collective-permute-start(bf16[2,384,384]{2,1,0:T(8,128)(2,1)S(1)} %collective-permute-done.17), channel_id=1, source_target_pairs={{0,4},{1,5},{2,6},{3,7},{4,8},{5,9},{6,10},{7,11},{8,12},{9,13},{1... | collective-permute-start | bytes 1769480 | tf_op jit(solution)/shard_map/ppermute | solution.py:20
  54.5 89.9 %collective-permute-start.20 = (bf16[4,2,384,384]{3,2,1,0:T(8,128)(2,1)}, bf16[4,2,384,384]{3,2,1,0:T(8,128)(2,1)}, u32[]{:S(2)}, u32[]{:S(2)}) collective-permute-start(bf16[4,2,384,384]{3,2,1,0:T(8,128)(2,1)} %pad_maximum_fusion.a_ref), channel_id=1, source_target_pairs={{0,16},{1,17},{2,18},{3,19},{4,20},{5,21},{6,22},{7,23},{8,24},{9,... | collective-permute-start | bytes 7077896 | tf_op jit(solution)/shard_map/ppermute | solution.py:29
  59.6 16.3 %collective-permute-start.2 = (bf16[4,2,128,384]{3,2,1,0:T(8,128)(2,1)}, bf16[4,2,128,384]{3,2,1,0:T(8,128)(2,1)S(1)}, u32[]{:S(2)}, u32[]{:S(2)}) collective-permute-start(bf16[4,2,128,384]{3,2,1,0:T(8,128)(2,1)} %pad_maximum_fusion.1), channel_id=1, source_target_pairs={{0,2},{1,3},{2,0},{3,1},{4,6},{5,7},{6,4},{7,5},{8,10},{9,11},{10,... | collective-permute-start | bytes 2359304 | tf_op jit(solution)/shard_map/ppermute | solution.py:20
  63.0 85.8 %copy-start.10 = (s32[2]{0:T(128)}, s32[2]{0:T(128)S(1)}, u32[]{:S(2)}) copy-start(s32[2]{0:T(128)S(1)} %get-tuple-element.13) | copy-start | bytes 28
  63.1 4.7 %collective-permute-start.4 = (s32[2]{0:T(128)S(1)}, s32[2]{0:T(128)S(1)}, u32[]{:S(2)}, u32[]{:S(2)}) collective-permute-start(s32[2]{0:T(128)S(1)} %get-tuple-element.14), channel_id=1, source_target_pairs={{0,12},{1,13},{2,6},{3,7},{4,0},{5,1},{6,10},{7,11},{8,4},{9,5},{1... | collective-permute-start | bytes 32 | tf_op jit(solution)/shard_map/ppermute | solution.py:20
  64.2 28.6 %collective-permute-start.6 = (bf16[4,2,128,384]{3,2,1,0:T(8,128)(2,1)S(1)}, bf16[4,2,128,384]{3,2,1,0:T(8,128)(2,1)S(1)}, u32[]{:S(2)}, u32[]{:S(2)}) collective-permute-start(bf16[4,2,128,384]{3,2,1,0:T(8,128)(2,1)S(1)} %pad_maximum_fusion.2), channel_id=1, source_target_pairs={{0,2},{1,3},{2,0},{3,1},{4,6},{5,7},{6,4},{7,5},{8,10},{9,11},{10,... | collective-permute-start | bytes 2359304 | tf_op jit(solution)/shard_map/ppermute | solution.py:20
  65.3 44.4 %collective-permute-start.9 = (bf16[4,2,128,384]{3,2,1,0:T(8,128)(2,1)}, bf16[4,2,128,384]{3,2,1,0:T(8,128)(2,1)}, u32[]{:S(2)}, u32[]{:S(2)}) collective-permute-start(bf16[4,2,128,384]{3,2,1,0:T(8,128)(2,1)} %pad_maximum_fusion.3), channel_id=1, source_target_pairs={{0,2},{1,3},{2,0},{3,1},{4,6},{5,7},{6,4},{7,5},{8,10},{9,11},{10,... | collective-permute-start | bytes 2359304 | tf_op jit(solution)/shard_map/ppermute | solution.py:20
  67.7 91.4 %copy-start = (bf16[512,1536]{1,0:T(8,128)(2,1)S(1)}, bf16[512,1536]{1,0:T(8,128)(2,1)}, u32[]{:S(2)}) copy-start(bf16[512,1536]{1,0:T(8,128)(2,1)} %q_ref.7) | copy-start | bytes 4718596
  67.7 32.5 %copy-start.9 = (s32[2]{0:T(128)}, s32[2]{0:T(128)S(1)}, u32[]{:S(2)}) copy-start(s32[2]{0:T(128)S(1)} %collective-permute-done.4.idx_ref) | copy-start | bytes 28
  67.7 58.8 %collective-permute-start.12 = (bf16[4,2,128,384]{3,2,1,0:T(8,128)(2,1)}, bf16[4,2,128,384]{3,2,1,0:T(8,128)(2,1)}, u32[]{:S(2)}, u32[]{:S(2)}) collective-permute-start(bf16[4,2,128,384]{3,2,1,0:T(8,128)(2,1)} %pad_maximum_fusion.4), channel_id=1, source_target_pairs={{0,2},{1,3},{2,0},{3,1},{4,6},{5,7},{6,4},{7,5},{8,10},{9,11},{10,... | collective-permute-start | bytes 2359304 | tf_op jit(solution)/shard_map/ppermute | solution.py:20
  75.9 80.4 %copy-start.1 = (bf16[4,2,128,384]{3,2,1,0:T(8,128)(2,1)}, bf16[4,2,128,384]{3,2,1,0:T(8,128)(2,1)S(1)}, u32[]{:S(2)}) copy-start(bf16[4,2,128,384]{3,2,1,0:T(8,128)(2,1)S(1)} %collective-permute-done.2.in_ref.y_ref) | copy-start | bytes 2359300
  75.9 73.5 %collective-permute-start = (bf16[512,1536]{1,0:T(8,128)(2,1)}, bf16[512,1536]{1,0:T(8,128)(2,1)}, u32[]{:S(2)}, u32[]{:S(2)}) collective-permute-start(bf16[512,1536]{1,0:T(8,128)(2,1)} %k0_ref.7), channel_id=1, source_target_pairs={{0,1},{1,0},{2,3},{3,2},{4,5},{5,4},{6,7},{7,6},{8,9},{9,8},{10,11... | collective-permute-start | bytes 4718600 | tf_op jit(solution)/shard_map/ppermute | solution.py:20
  92.8 7.4 %copy-start.3 = (bf16[4,2,128,384]{3,2,1,0:T(8,128)(2,1)}, bf16[4,2,128,384]{3,2,1,0:T(8,128)(2,1)S(1)}, u32[]{:S(2)}) copy-start(bf16[4,2,128,384]{3,2,1,0:T(8,128)(2,1)S(1)} %collective-permute-done.6.in_ref.y_ref) | copy-start | bytes 2359300
  92.8 60.0 %collective-permute-start.1 = (bf16[512,1536]{1,0:T(8,128)(2,1)}, bf16[512,1536]{1,0:T(8,128)(2,1)}, u32[]{:S(2)}, u32[]{:S(2)}) collective-permute-start(bf16[512,1536]{1,0:T(8,128)(2,1)} %v0_ref.7), channel_id=1, source_target_pairs={{0,1},{1,0},{2,3},{3,2},{4,5},{5,4},{6,7},{7,6},{8,9},{9,8},{10,11... | collective-permute-start | bytes 4718600 | tf_op jit(solution)/shard_map/ppermute | solution.py:20
  102.6 50.2 %copy-start.4 = (bf16[4,2,128,384]{3,2,1,0:T(8,128)(2,1)S(1)}, bf16[4,2,128,384]{3,2,1,0:T(8,128)(2,1)}, u32[]{:S(2)}) copy-start(bf16[4,2,128,384]{3,2,1,0:T(8,128)(2,1)} %copy-done.3) | copy-start | bytes 2359300
  109.6 20.0 %collective-permute-start.8 = (bf16[2,2,128,384]{3,2,1,0:T(8,128)(2,1)}, bf16[2,2,128,384]{3,2,1,0:T(8,128)(2,1)S(1)}, u32[]{:S(2)}, u32[]{:S(2)}) collective-permute-start(bf16[2,2,128,384]{3,2,1,0:T(8,128)(2,1)} %select_blocks.5), channel_id=1, source_target_pairs={{0,4},{1,5},{2,14},{3,15},{4,8},{5,9},{6,2},{7,3},{8,12},{9,13},{1... | collective-permute-start | bytes 1179656 | tf_op jit(solution)/shard_map/ppermute | solution.py:20
  126.5 8.7 %collective-permute-start.11 = (bf16[2,2,128,384]{3,2,1,0:T(8,128)(2,1)}, bf16[2,2,128,384]{3,2,1,0:T(8,128)(2,1)}, u32[]{:S(2)}, u32[]{:S(2)}) collective-permute-start(bf16[2,2,128,384]{3,2,1,0:T(8,128)(2,1)} %select_blocks.6), channel_id=1, source_target_pairs={{0,4},{1,5},{2,14},{3,15},{4,8},{5,9},{6,2},{7,3},{8,12},{9,13},{1... | collective-permute-start | bytes 1179656 | tf_op jit(solution)/shard_map/ppermute | solution.py:20
  129.6 14.7 %collective-permute-start.14 = (bf16[2,2,128,384]{3,2,1,0:T(8,128)(2,1)}, bf16[2,2,128,384]{3,2,1,0:T(8,128)(2,1)}, u32[]{:S(2)}, u32[]{:S(2)}) collective-permute-start(bf16[2,2,128,384]{3,2,1,0:T(8,128)(2,1)} %select_blocks.7), channel_id=1, source_target_pairs={{0,4},{1,5},{2,14},{3,15},{4,8},{5,9},{6,2},{7,3},{8,12},{9,13},{1... | collective-permute-start | bytes 1179656 | tf_op jit(solution)/shard_map/ppermute | solution.py:20
  135.2 69.0 %collective-permute-start.21 = (bf16[4,2,384,384]{3,2,1,0:T(8,128)(2,1)}, bf16[4,2,384,384]{3,2,1,0:T(8,128)(2,1)}, u32[]{:S(2)}, u32[]{:S(2)}) collective-permute-start(bf16[4,2,384,384]{3,2,1,0:T(8,128)(2,1)} %pad_maximum_fusion.a_ref), channel_id=1, source_target_pairs={{0,1},{1,0},{2,3},{3,2},{4,5},{5,4},{6,7},{7,6},{8,9},{9,8},{10,11... | collective-permute-start | bytes 7077896 | tf_op jit(solution)/shard_map/ppermute | solution.py:20
  144.4 59.9 %collective-permute-start.22 = (bf16[4,2,384,384]{3,2,1,0:T(8,128)(2,1)}, bf16[4,2,384,384]{3,2,1,0:T(8,128)(2,1)}, u32[]{:S(2)}, u32[]{:S(2)}) collective-permute-start(bf16[4,2,384,384]{3,2,1,0:T(8,128)(2,1)} %collective-permute-done.20.b_ref), channel_id=1, source_target_pairs={{0,1},{1,0},{2,3},{3,2},{4,5},{5,4},{6,7},{7,6},{8,9},{9,8},{10,11... | collective-permute-start | bytes 7077896 | tf_op jit(solution)/shard_map/ppermute | solution.py:20
  144.4 14.4 %collective-permute-start.13 = (bf16[4,2,128,384]{3,2,1,0:T(8,128)(2,1)}, bf16[4,2,128,384]{3,2,1,0:T(8,128)(2,1)}, u32[]{:S(2)}, u32[]{:S(2)}) collective-permute-start(bf16[4,2,128,384]{3,2,1,0:T(8,128)(2,1)} %collective-permute-done.12.in_ref.y_ref), channel_id=1, source_target_pairs={{0,1},{1,4},{2,15},{3,2},{4,5},{5,8},{6,3},{7,6},{8,9},{9,12},{10,... | collective-permute-start | bytes 2359304 | tf_op jit(solution)/shard_map/ppermute | solution.py:20
  149.4 19.7 %collective-permute-start.10 = (bf16[4,2,128,384]{3,2,1,0:T(8,128)(2,1)}, bf16[4,2,128,384]{3,2,1,0:T(8,128)(2,1)}, u32[]{:S(2)}, u32[]{:S(2)}) collective-permute-start(bf16[4,2,128,384]{3,2,1,0:T(8,128)(2,1)} %collective-permute-done.9.in_ref.y_ref), channel_id=1, source_target_pairs={{0,1},{1,4},{2,15},{3,2},{4,5},{5,8},{6,3},{7,6},{8,9},{9,12},{10,... | collective-permute-start | bytes 2359304 | tf_op jit(solution)/shard_map/ppermute | solution.py:20
  152.8 26.7 %collective-permute-start.7 = (bf16[4,2,128,384]{3,2,1,0:T(8,128)(2,1)S(1)}, bf16[4,2,128,384]{3,2,1,0:T(8,128)(2,1)}, u32[]{:S(2)}, u32[]{:S(2)}) collective-permute-start(bf16[4,2,128,384]{3,2,1,0:T(8,128)(2,1)S(1)} %copy-done.4), channel_id=1, source_target_pairs={{0,1},{1,4},{2,15},{3,2},{4,5},{5,8},{6,3},{7,6},{8,9},{9,12},{10,... | collective-permute-start | bytes 2359304 | tf_op jit(solution)/shard_map/ppermute | solution.py:20
  158.7 36.3 %collective-permute-start.3 = (bf16[4,2,128,384]{3,2,1,0:T(8,128)(2,1)}, bf16[4,2,128,384]{3,2,1,0:T(8,128)(2,1)S(1)}, u32[]{:S(2)}, u32[]{:S(2)}) collective-permute-start(bf16[4,2,128,384]{3,2,1,0:T(8,128)(2,1)} %copy-done.1), channel_id=1, source_target_pairs={{0,1},{1,4},{2,15},{3,2},{4,5},{5,8},{6,3},{7,6},{8,9},{9,12},{10,... | collective-permute-start | bytes 2359304 | tf_op jit(solution)/shard_map/ppermute | solution.py:20
  159.8 9.3 %copy-start.7 = (bf16[2,2,128,384]{3,2,1,0:T(8,128)(2,1)S(1)}, bf16[2,2,128,384]{3,2,1,0:T(8,128)(2,1)}, u32[]{:S(2)}) copy-start(bf16[2,2,128,384]{3,2,1,0:T(8,128)(2,1)} %select_blocks.4) | copy-start | bytes 1179652
  169.1 10.4 %copy-start.6 = (f32[4,1,1536]{2,1,0:T(1,128)S(1)}, f32[4,1,1536]{2,1,0:T(1,128)}, u32[]{:S(2)}) copy-start(f32[4,1,1536]{2,1,0:T(1,128)} %reshape.261.bias_ref) | copy-start | bytes 73732
  169.2 25.8 %collective-permute-start.5 = (bf16[2,2,128,384]{3,2,1,0:T(8,128)(2,1)S(1)}, bf16[2,2,128,384]{3,2,1,0:T(8,128)(2,1)S(1)}, u32[]{:S(2)}, u32[]{:S(2)}) collective-permute-start(bf16[2,2,128,384]{3,2,1,0:T(8,128)(2,1)S(1)} %copy-done.7), channel_id=1, source_target_pairs={{0,4},{1,5},{2,14},{3,15},{4,8},{5,9},{6,2},{7,3},{8,12},{9,13},{1... | collective-permute-start | bytes 1179656 | tf_op jit(solution)/shard_map/ppermute | solution.py:20
  179.5 15.5 %copy-start.2 = (bf16[4,2,128,384]{3,2,1,0:T(8,128)(2,1)S(1)}, bf16[4,2,128,384]{3,2,1,0:T(8,128)(2,1)}, u32[]{:S(2)}) copy-start(bf16[4,2,128,384]{3,2,1,0:T(8,128)(2,1)} %copy-done.1) | copy-start | bytes 2359300
  (3 other events, 5.1 us)

commit v2 on v0

v2 whole, which is shorter than its diff:
```python
import math

import jax
import jax.numpy as jnp
from jax import lax
from jax.experimental import pallas as pl
from jax.experimental.pallas import tpu as pltpu
from jax.sharding import PartitionSpec as P

HEADS = 12
BLOCK = 128
RADIUS = 2
PARTS = (2,4,4,2)
W_A, W_B, W_C = 1, 2, 3
SPECIAL = True

neg_large = -1e30
VMEM_LIMIT = 60 * 1024 * 1024
STEP_FLOPS = 6_000_000_000
EARLY = False
ATTEND_FLOPS = 1_000_000_000
CHEAP = pl.CostEstimate(flops=1000, bytes_accessed=1000, transcendentals=0)


def moved(name, value, dest, count):
    with jax.named_scope(name):
        return lax.ppermute(value, "blk", [(s, dest(s)) for s in range(count)])


def moved_all(name, value, groups, count, dest):
    pairs = []
    for g in range(groups):
        for s in range(count):
            tg, ts = dest(g, s)
            pairs.append((g * count + s, tg * count + ts))
    with jax.named_scope(name):
        return lax.ppermute(value, ("groups", "blk"), pairs)


def after(value, *earlier):
    return lax.optimization_barrier((value, *earlier))[0]


def other_core(s):
    return s ^ 1


def other_chip(s):
    return s ^ 2


def next_row(count):
    return lambda s: (s + (4 if s % 4 < 2 else -4)) % count


def step_kernel(last_ref, *refs):
    refs[-1][0] = last_ref[0] + 1


def stepped(last, *arrived, weight=STEP_FLOPS):
    smem = pl.BlockSpec(memory_space=pltpu.SMEM)
    return pl.pallas_call(
        step_kernel,
        in_specs=[smem] + [pl.BlockSpec(memory_space=pl.ANY)] * len(arrived),
        out_specs=smem,
        out_shape=jax.ShapeDtypeStruct((1,), jnp.int32),
        cost_estimate=pl.CostEstimate(flops=weight, bytes_accessed=1000, transcendentals=0),
        name="step",
    )(last, *arrived)


def plan_kernel(place_ref, mask_ref, picks_ref, bias_ref):
    place = place_ref[0]
    per = mask_ref.shape[0]
    lower, even = place < 2, lax.rem(place, 2) == 0

    def two(first):
        used = []
        for j in range(per):
            u = mask_ref[0, first + j]
            for r in range(1, per):
                u = jnp.maximum(u, mask_ref[r, first + j])
            used.append(u)
        low, high = per - 1, 0
        for j in range(per):
            high = jnp.where(used[j] > 0, j, high)
            low = jnp.where(used[per - 1 - j] > 0, per - 1 - j, low)
        return low, high

    beyond = 2 * RADIUS * per
    first_y = jnp.where(lower, beyond, 0)
    first_f = jnp.where(lower, 0, beyond)
    first_1 = jnp.where(even, (RADIUS + 1) * per, (RADIUS - 1) * per)
    first_z = jnp.where(even, (RADIUS - 1) * per, (RADIUS + 1) * per)
    y_low, y_high = two(first_y)
    f_low, f_high = two(first_f)
    picks_ref[0] = y_low
    picks_ref[1] = y_high
    picks_ref[2] = f_low
    picks_ref[3] = f_high
    columns = [first_1 + j for j in range(per)] + [first_z + j for j in range(per)]
    columns += [first_y + y_low, first_y + y_high, first_f + f_low, first_f + f_high]
    for r in range(per):
        for n, c in enumerate(columns):
            value = jnp.where(mask_ref[r, c] > 0, 0.0, neg_large).astype(jnp.float32)
            bias_ref[r, :, n * BLOCK : (n + 1) * BLOCK] = jnp.full((1, BLOCK), value, jnp.float32)


def plan(place, block_mask):
    per = block_mask.shape[0]
    smem = pl.BlockSpec(memory_space=pltpu.SMEM)
    return pl.pallas_call(
        plan_kernel,
        in_specs=[smem, smem],
        out_specs=[smem, pl.BlockSpec(memory_space=pltpu.VMEM)],
        out_shape=[
            jax.ShapeDtypeStruct((4,), jnp.int32),
            jax.ShapeDtypeStruct((per, 1, 3 * per * BLOCK), jnp.float32),
        ],
        cost_estimate=CHEAP,
        name="plan",
    )(place, block_mask)


def attend_kernel(
    picks_ref, q_ref, k0_ref, v0_ref, k1_ref, v1_ref, near_ref, a_ref, b_ref, c_ref, d_ref, bias_ref, *rest
):
    o_ref = rest[-1]
    rows, size = q_ref.shape
    per = near_ref.shape[0]
    span = per * BLOCK
    near = near_ref[...]
    far = (a_ref, b_ref, c_ref, d_ref)
    keys = [
        k0_ref[...],
        k1_ref[...],
        near[:, 0].reshape(span, size),
        jnp.concatenate([r[0, 0] for r in far], axis=0),
    ]
    values = [
        v0_ref[...],
        v1_ref[...],
        near[:, 1].reshape(span, size),
        jnp.concatenate([r[0, 1] for r in far], axis=0),
    ]
    factor = math.log2(math.e) / math.sqrt(size)
    ones = jnp.ones((span, size), jnp.bfloat16)
    values = [jnp.concatenate([v, ones], axis=1) for v in values]
    for m in range(rows // BLOCK):
        mine = slice(m * BLOCK, (m + 1) * BLOCK)
        q = q_ref[mine, :]
        scores, top = [], None
        for n, k in enumerate(keys):
            s = lax.dot_general(q, k, (((1,), (1,)), ((), ())), preferred_element_type=jnp.float32)
            if n:
                s = s + bias_ref[m, :, (n - 1) * span : n * span]
            scores.append(s)
            t = jnp.max(s, axis=1, keepdims=True)
            top = t if top is None else jnp.maximum(top, t)
        total = None
        for s, v in zip(scores, values):
            w = jnp.exp2((s - top) * factor).astype(jnp.bfloat16)
            part = jnp.dot(w, v, preferred_element_type=jnp.float32)
            total = part if total is None else total + part
        o_ref[mine, :] = (total[:, :size] / total[:, size:]).astype(o_ref.dtype)


def attend(first_head, per_part, picks, queries, key_rows, value_rows, core_k, core_v, near, y, z, bias, into):
    rows, width = queries.shape
    size = width // HEADS
    per = near.shape[0]
    flat = pl.BlockSpec((rows, size), lambda h, p: (0, first_head + h))
    far = [
        pl.BlockSpec((1, 2, BLOCK, size), lambda h, p, n=n: (p[n], 0, 0, h)) for n in range(4)
    ]
    in_specs = [
        flat,
        flat,
        flat,
        flat,
        flat,
        pl.BlockSpec((per, 2, BLOCK, size), lambda h, p: (0, 0, 0, h)),
        *far,
        pl.BlockSpec(bias.shape, lambda h, p: (0, 0, 0)),
    ]
    args = [queries, key_rows, value_rows, core_k, core_v, near, y, y, z, z, bias]
    aliases = {}
    if into is not None:
        in_specs.append(pl.BlockSpec(memory_space=pl.ANY))
        args.append(into)
        aliases = {len(args): 0}
    return pl.pallas_call(
        attend_kernel,
        grid_spec=pltpu.PrefetchScalarGridSpec(
            num_scalar_prefetch=1,
            grid=(per_part,),
            in_specs=in_specs,
            out_specs=flat,
        ),
        out_shape=jax.ShapeDtypeStruct((rows, width), jnp.bfloat16),
        input_output_aliases=aliases,
        compiler_params=pltpu.CompilerParams(vmem_limit_bytes=VMEM_LIMIT),
        cost_estimate=pl.CostEstimate(
            flops=ATTEND_FLOPS * per_part // 3, bytes_accessed=1000, transcendentals=0
        ),
        name="attend",
    )(picks, *args)


def project_kernel(place_ref, att_ref, *refs):
    *pieces, o_ref, held_ref = refs
    _, depth, cols = pieces[0].shape
    step = pl.program_id(0)

    @pl.when(step == 0)
    def _():
        for n in range(4):
            first = pl.multiple_of(place_ref[n] * depth, depth)
            held_ref[:, n * depth : (n + 1) * depth] = att_ref[:, pl.ds(first, depth)]

    def fill(half):
        own = jnp.concatenate([pieces[n][0] for n in range(4)], axis=0)
        other = jnp.concatenate([pieces[4 + 4 * half + n][0] for n in range(4)], axis=0)
        total = jnp.dot(
            held_ref[...], jnp.concatenate([own, other], axis=1), preferred_element_type=jnp.float32
        ).astype(o_ref.dtype)
        for f in range(2):
            to = pl.multiple_of(place_ref[4 + f] * cols, cols)
            o_ref[:, pl.ds(to, cols)] = total[:, f * cols : (f + 1) * cols]

    pl.when(step < 2)(lambda: fill(0))
    pl.when(step >= 2)(lambda: fill(1))


def project(places, attention, whole, halves):
    rows, width = attention.shape
    shifts, depth, cols = whole[0].shape
    size = (1, depth, cols)
    in_specs = [pl.BlockSpec((rows, width), lambda g, p: (0, 0))]
    in_specs += [pl.BlockSpec(size, lambda g, p: (g, 0, 0))] * 4
    in_specs += [pl.BlockSpec(size, lambda g, p: (jnp.minimum(g, 1), 0, 0))] * 4
    in_specs += [pl.BlockSpec(size, lambda g, p: (jnp.maximum(g - 2, 0), 0, 0))] * 4
    return pl.pallas_call(
        project_kernel,
        grid_spec=pltpu.PrefetchScalarGridSpec(
            num_scalar_prefetch=1,
            grid=(shifts,),
            in_specs=in_specs,
            out_specs=pl.BlockSpec((rows, 2 * cols), lambda g, p: (0, p[6 + g])),
            scratch_shapes=[pltpu.VMEM((rows, width), jnp.bfloat16)],
        ),
        out_shape=jax.ShapeDtypeStruct((rows, shifts * 2 * cols), jnp.bfloat16),
        compiler_params=pltpu.CompilerParams(vmem_limit_bytes=VMEM_LIMIT),
        cost_estimate=CHEAP,
        name="project",
    )(places, attention, *whole, *halves)


def local(groups, count, queries, key_rows, value_rows, block_mask, out_weight):
    tok_rows, feat_width = queries.shape
    per = tok_rows // BLOCK
    me = lax.axis_index("blk")
    place = me % 4
    up = lambda s: (s + 4) % count
    down = lambda s: (s - 4) % count
    over = lambda g, s: (1 - g, s)

    packs, first = [], 0
    for heads in PARTS:
        wide = heads * (feat_width // HEADS)
        k = key_rows[:, first : first + wide].reshape(per, 1, BLOCK, wide)
        v = value_rows[:, first : first + wide].reshape(per, 1, BLOCK, wide)
        packs.append(jnp.concatenate([k, v], axis=1))
        first += wide
    picks, bias = plan(place[None].astype(jnp.int32), block_mask)
    core_k = moved("core_keys", key_rows, other_core, count)
    core_v = moved("core_values", value_rows, other_core, count)

    special = SPECIAL and count == 16 and out_weight.shape[1] % 64 == 0
    if special:
        depth = out_weight.shape[0] // 4
        x = lax.axis_index("groups")
        core = me % 2
        own = lax.dynamic_slice_in_dim(out_weight, (x * 2 + core) * depth, depth, 0)
        give = lax.dynamic_slice_in_dim(out_weight, (x * 2 + 1 - core) * depth, depth, 0)
        got = moved("w_core", give, other_core, count)
        sides = [jnp.where(core == 0, own, got), jnp.where(core == 0, got, own)]
        piece = jnp.concatenate(sides, axis=1)
        own_up = moved("w_up", piece, up, count)
        own_down = moved("w_down", piece, down, count)
    outer = (place == 0) | (place == 3)

    def across_chips(n, *earlier):
        pack = after(packs[n], *earlier) if earlier else packs[n]
        return moved("kv_y%d" % n, pack, other_chip, count)

    def along_rows(n, y):
        return moved("kv_z%d" % n, y, next_row(count), count)

    def within_chip(n, y, z):
        return moved("kv_g%d" % n, jnp.where(outer, y, z), other_core, count)

    def attended(n, near, y, z, att):
        return attend(
            sum(PARTS[:n]), PARTS[n], picks, queries, key_rows, value_rows, core_k, core_v, near, y, z, bias, att
        )

    if special:
        t = place[None].astype(jnp.int32)
        y0 = across_chips(0)
        y1 = across_chips(1, piece)
        y2 = across_chips(2, piece)
        t = stepped(t, piece)
        t = stepped(t, after(core_k, t), after(core_v, t))
        core_k, core_v = after(core_k, t), after(core_v, t)
        t = stepped(t, after(own_up, t))
        own_up2 = moved("w_up2", after(own_up, t), up, count)
        t = stepped(t, after(own_down, t))
        t = stepped(t, after(y0, t))
        y0 = after(y0, t)
        z0 = along_rows(0, y0)
        t = stepped(t, after(own_up2, t))
        own_up, own_up2, own_down = after(own_up, t), after(own_up2, t), after(own_down, t)
        a1 = jnp.stack([piece, own_up, own_up2, own_down])
        a1x = jnp.stack([piece, own_up])
        a1y = jnp.stack([own_up2, own_down])
        b1 = moved_all("w_x1", a1, groups, count, over)
        a2x = moved("w_yx", a1x, other_chip, count)
        t = stepped(t, after(y1, t), a1, a1x)
        y1 = after(y1, t)
        z1 = along_rows(1, y1)
        y3 = across_chips(3, a1x)
        a2y = moved("w_yy", after(a1y, y1), other_chip, count)
        t = stepped(t, after(z0, t))
        z0 = after(z0, t)
        if EARLY:
            g0 = within_chip(0, y0, z0)
        t = stepped(t, after(y2, t))
        y2 = after(y2, t)
        if not EARLY:
            g0 = within_chip(0, y0, z0)
        z2 = along_rows(2, y2)
        if EARLY:
            att = attended(0, after(g0, t), y0, z0, None)
            t = stepped(t, after(z1, t), att)
        else:
            t = stepped(t, after(z1, t))
            att = attended(0, after(g0, t), y0, z0, None)
        z1 = after(z1, t)
        g1 = within_chip(1, y1, z1)
        t = stepped(t, after(y3, t), att)
        y3 = after(y3, t)
        z3 = along_rows(3, y3)
        t = stepped(t, after(a2x, t))
        a2x = after(a2x, t)
        b2x = moved_all("w_x2x", a2x, groups, count, over)
        t = stepped(t, after(b1, t))
        b1 = after(b1, t)
        c1 = moved("w_c1", after(a1, b1), other_core, count)
        d1 = moved("w_d1", b1, other_core, count)
        att = attended(1, after(g1, t), y1, z1, att)
        t = stepped(t, after(z2, t), att)
        z2 = after(z2, t)
        g2 = within_chip(2, y2, z2)
        t = stepped(t, after(a2y, t))
        a2y = after(a2y, t)
        b2y = moved_all("w_x2y", a2y, groups, count, over)
        t = stepped(t, after(b2x, t))
        d2x = moved("w_d2x", after(b2x, t), other_core, count)
        c2x = moved("w_c2x", after(a2x, t), other_core, count)
        att = attended(2, after(g2, t), y2, z2, att)
        t = stepped(t, after(z3, t, att))
        z3 = after(z3, t)
        g3 = within_chip(3, y3, z3)
        c2y = moved("w_c2y", after(a2y, t), other_core, count)
        t = stepped(t, after(b2y, t))
        d2y = moved("w_d2y", after(b2y, t), other_core, count)
        att = attended(3, g3, y3, z3, att)
    else:
        att = None
        for n in range(len(PARTS)):
            y = across_chips(n)
            z = along_rows(n, y)
            att = attended(n, within_chip(n, y, z), y, z, att)
    if special:
        z, y = me // 4, me // 2 % 2
        places = [x * 2 + core, (1 - x) * 2 + core, x * 2 + 1 - core, (1 - x) * 2 + 1 - core, y, 1 - y]
        places += [(z - shift) % (count // 4) for shift in range(count // 4)]
        whole = (a1, b1, c1, d1)
        halves = (a2x, b2x, c2x, d2x, a2y, b2y, c2y, d2y)
        return project(jnp.stack(places).astype(jnp.int32), att, whole, halves)
    full = lax.all_gather(out_weight, "blk", axis=1, tiled=True)
    return jnp.dot(att, full, preferred_element_type=jnp.float32).astype(jnp.bfloat16)


def solution(mesh):
    groups, count = mesh.shape["groups"], mesh.shape["blk"]
    in_specs = (
        P(("groups", "blk"), None),
        P(("groups", "blk"), None),
        P(("groups", "blk"), None),
        P("blk", None),
        P(None, "blk"),
    )
    out_specs = P(("groups", "blk"), None)

    def run(*args):
        return local(groups, count, *args)

    return jax.shard_map(run, mesh=mesh, in_specs=in_specs, out_specs=out_specs, check_vma=False)
```

time: 288 us -> 151 us (0.52)
  waiting for transfers between devices: 130 us -> 61.1 us
  matrix products: 61.9 us -> 0 us
  Pallas kernels: 0 us -> 44.8 us
  local copies, waits for them, and re-layouts: 39.5 us -> 7.82 us
  other arithmetic: 28.1 us -> 6.76 us
  starting transfers between devices: 12.5 us -> 29.7 us
  between operations: 13.9 us -> 0.45 us
    ppermute x6 -> x29, waiting for transfers between devices: 130 us -> 61.1 us  [the longest x26 60.3 us: moved(): return lax.ppermute(value, 'blk', [(s, dest(s)) for s in range(count)])]
    dot_general x11 -> x0, matrix products: 61.9 us -> none  [the longest x5 32.2 us: absorb(): jnp.einsum('hqk,khe->qhe', rounded_probs, value_heads, preferred_element_...]
    pallas_call x0 -> x6, Pallas kernels: none -> 44.8 us  [the longest x4 32.5 us: attend(): pl.pallas_call(attend_kernel, grid_spec=pltpu.PrefetchScalarGridSpec(num_...]
    slice x8 -> x4, local copies, waits for them, and re-layouts: 19.9 us -> 2.03 us  [the longest x2 1.93 us: local(): v = value_rows[:, first:first + wide].reshape(per, 1, BLOCK, wide)]
    ppermute x6 -> x29, starting transfers between devices: 12.5 us -> 29.7 us  [the longest x26 24.8 us: moved(): return lax.ppermute(value, 'blk', [(s, dest(s)) for s in range(count)])]
    reduce_sum x5 -> x0, other arithmetic: 16.9 us -> none  [absorb(): jnp.sum(weights, axis=(3, 4)).reshape(head_count, tok_rows)]
    gather x4 -> x0, local copies, waits for them, and re-layouts: 8.55 us -> none  [the longest x2 7.43 us: local(): jnp.take(blocked, requests, axis=1)]
    unnamed x52 -> x30, local copies, waits for them, and re-layouts: 7.35 us -> 4.08 us
  transfers between devices with their start and end apart: 7 -> 29, of which waited for: 2 -> 13; matrix products, arithmetic and copies ran while one was open for 40% -> 8% of each run, Pallas kernels for 0% -> 23%
where the time goes in v2:
time: 151 us
  waiting for transfers between devices  61.1 us (40%)
  Pallas kernels  44.8 us (30%)
  starting transfers between devices  29.7 us (20%)
  local copies, waits for them, and re-layouts  7.82 us (5%)
  other arithmetic  6.76 us (4%)
    ppermute x26, waiting for transfers between devices, moved(): return lax.ppermute(value, 'blk', [(s, dest(s)) for s in range(count)])  60.3 us
    pallas_call x4, Pallas kernels, attend(): pl.pallas_call(attend_kernel, grid_spec=pltpu.PrefetchScalarGridSpec(num_...  32.5 us
    ppermute x26, starting transfers between devices, moved(): return lax.ppermute(value, 'blk', [(s, dest(s)) for s in range(count)])  24.8 us
    pallas_call x1, Pallas kernels, project(): pl.pallas_call(project_kernel, grid_spec=pltpu.PrefetchScalarGridSpec(num...  10.8 us
    ppermute x3, starting transfers between devices, moved_all(): return lax.ppermute(value, ('groups', 'blk'), pairs)  4.94 us
    unnamed x30, local copies, waits for them, and re-layouts  4.08 us
  transfers between devices with their start and end apart: 29, of which 13 were waited for; matrix products, arithmetic and copies ran while one was open for 8% of the time, Pallas kernels for 23%

profile of v2, /device:TPU:0, one launch (start us, length us, event | category | flops | bytes accessed | tf_op | source)
XLA Modules:
  0.0 150.6 jit_solution(14091515348621253361)
XLA Ops:
  2.8 1.1 fusion.3
  4.8 2.6 %collective-permute-start.5 = (bf16[4,2,128,256]{3,2,1,0:T(8,128)(2,1)}, bf16[4,2,128,256]{3,2,1,0:T(8,128)(2,1)}, u32[]{:S(2)}, u32[]{:S(2)}) collective-permute-start(bf16[4,2,128,256]{3,2,1,0:T(8,128)(2,1)} %pad_maximum_fusion.6), channel_id=1, source_target_pairs={{0,2},{1,3},{2,0},{3,1},{4,6},{5,7},{6,4},{7,5},{8,10},{9,11},{10,... | collective-permute-start | bytes 1572872 | tf_op jit(solution)/shard_map/kv_y0/ppermute | solution.py:27
  9.4 1.4 plan.1
  11.3 1.6 %collective-permute-start.3 = (bf16[384,384]{1,0:T(8,128)(2,1)S(1)}, bf16[384,384]{1,0:T(8,128)(2,1)S(1)}, u32[]{:S(2)}, u32[]{:S(2)}) collective-permute-start(bf16[384,384]{1,0:T(8,128)(2,1)S(1)} %pad_maximum_fusion.7), channel_id=1, source_target_pairs={{0,4},{1,5},{2,6},{3,7},{4,8},{5,9},{6,10},{7,11},{8,12},{9,13},{1... | collective-permute-start | bytes 884744 | tf_op jit(solution)/shard_map/w_up/ppermute | solution.py:27
  12.9 2.2 %collective-permute-start.4 = (bf16[384,384]{1,0:T(8,128)(2,1)S(1)}, bf16[384,384]{1,0:T(8,128)(2,1)S(1)}, u32[]{:S(2)}, u32[]{:S(2)}) collective-permute-start(bf16[384,384]{1,0:T(8,128)(2,1)S(1)} %pad_maximum_fusion.7), channel_id=1, source_target_pairs={{0,12},{1,13},{2,14},{3,15},{4,0},{5,1},{6,2},{7,3},{8,4},{9,5},{1... | collective-permute-start | bytes 884744 | tf_op jit(solution)/shard_map/w_down/ppermute | solution.py:27
  15.7 1.7 %collective-permute-start.10 = (bf16[4,2,128,512]{3,2,1,0:T(8,128)(2,1)S(1)}, bf16[4,2,128,512]{3,2,1,0:T(8,128)(2,1)S(1)}, u32[]{:S(2)}, u32[]{:S(2)}) collective-permute-start(bf16[4,2,128,512]{3,2,1,0:T(8,128)(2,1)S(1)} %pad_maximum_fusion.2), channel_id=1, source_target_pairs={{0,2},{1,3},{2,0},{3,1},{4,6},{5,7},{6,4},{7,5},{8,10},{9,11},{10,... | collective-permute-start | bytes 3145736 | tf_op jit(solution)/shard_map/kv_y2/ppermute | solution.py:27
  17.4 5.6 %collective-permute-done.3 = bf16[384,384]{1,0:T(8,128)(2,1)S(1)} collective-permute-done((bf16[384,384]{1,0:T(8,128)(2,1)S(1)}, bf16[384,384]{1,0:T(8,128)(2,1)S(1)}, u32[]{:S(2)}, u32[]{:S(2)}) %collective-permute-start.3) | collective-permute-done | bytes 294944 | tf_op jit(solution)/shard_map/w_up/ppermute | solution.py:27
  23.0 4.9 %collective-permute-done.4 = bf16[384,384]{1,0:T(8,128)(2,1)S(1)} collective-permute-done((bf16[384,384]{1,0:T(8,128)(2,1)S(1)}, bf16[384,384]{1,0:T(8,128)(2,1)S(1)}, u32[]{:S(2)}, u32[]{:S(2)}) %collective-permute-start.4) | collective-permute-done | bytes 294944 | tf_op jit(solution)/shard_map/w_down/ppermute | solution.py:27
  28.0 1.1 collective-permute-start.6
  29.8 9.9 %collective-permute-done.6 = bf16[384,384]{1,0:T(8,128)(2,1)S(1)} collective-permute-done((bf16[384,384]{1,0:T(8,128)(2,1)S(1)}, bf16[384,384]{1,0:T(8,128)(2,1)S(1)}, u32[]{:S(2)}, u32[]{:S(2)}) %collective-permute-start.6) | collective-permute-done | bytes 294944 | tf_op jit(solution)/shard_map/w_up2/ppermute | solution.py:27
  41.1 1.8 %collective-permute-done.8.a_ref.b_ref = bf16[4,2,128,512]{3,2,1,0:T(8,128)(2,1)S(1)} collective-permute-done((bf16[4,2,128,512]{3,2,1,0:T(8,128)(2,1)S(1)}, bf16[4,2,128,512]{3,2,1,0:T(8,128)(2,1)S(1)}, u32[]{:S(2)}, u32[]{:S(2)}) %collective-permute-start.8) | collective-permute-done | bytes 1048608 | tf_op jit(solution)/shard_map/kv_y1/ppermute | solution.py:27
  42.9 1.4 pad_maximum_fusion.refs_0_
  44.3 2.0 %collective-permute-start.15 = (bf16[4,384,384]{2,1,0:T(8,128)(2,1)}, bf16[4,384,384]{2,1,0:T(8,128)(2,1)}, u32[]{:S(2)}, u32[]{:S(2)}) collective-permute-start(bf16[4,384,384]{2,1,0:T(8,128)(2,1)} %pad_maximum_fusion.refs_0_), channel_id=1, source_target_pairs={{0,16},{1,17},{2,18},{3,19},{4,20},{5,21},{6,22},{7,23},{8,24},{9,... | collective-permute-start | bytes 3538952 | tf_op jit(solution)/shard_map/w_x1/ppermute | solution.py:37
  46.2 1.6 %collective-permute-start.11 = (bf16[4,2,128,512]{3,2,1,0:T(8,128)(2,1)S(1)}, bf16[4,2,128,512]{3,2,1,0:T(8,128)(2,1)S(1)}, u32[]{:S(2)}, u32[]{:S(2)}) collective-permute-start(bf16[4,2,128,512]{3,2,1,0:T(8,128)(2,1)S(1)} %collective-permute-done.8.a_ref.b_ref), channel_id=1, source_target_pairs={{0,4},{1,5},{2,14},{3,15},{4,8},{5,9},{6,2},{7,3},{8,12},{9,13},{1... | collective-permute-start | bytes 3145736 | tf_op jit(solution)/shard_map/kv_z1/ppermute | solution.py:27
  49.3 2.9 %collective-permute-start.7 = (bf16[4,2,128,256]{3,2,1,0:T(8,128)(2,1)}, bf16[4,2,128,256]{3,2,1,0:T(8,128)(2,1)S(1)}, u32[]{:S(2)}, u32[]{:S(2)}) collective-permute-start(bf16[4,2,128,256]{3,2,1,0:T(8,128)(2,1)} %pad_maximum_fusion.5), channel_id=1, source_target_pairs={{0,2},{1,3},{2,0},{3,1},{4,6},{5,7},{6,4},{7,5},{8,10},{9,11},{10,... | collective-permute-start | bytes 1572872 | tf_op jit(solution)/shard_map/kv_y3/ppermute | solution.py:27
  52.2 13.1 %collective-permute-done.10.a_ref.b_ref = bf16[4,2,128,512]{3,2,1,0:T(8,128)(2,1)S(1)} collective-permute-done((bf16[4,2,128,512]{3,2,1,0:T(8,128)(2,1)S(1)}, bf16[4,2,128,512]{3,2,1,0:T(8,128)(2,1)S(1)}, u32[]{:S(2)}, u32[]{:S(2)}) %collective-permute-start.10) | collective-permute-done | bytes 1048608 | tf_op jit(solution)/shard_map/kv_y2/ppermute | solution.py:27
  65.3 2.0 %collective-permute-start.18 = (bf16[2,384,384]{2,1,0:T(8,128)(2,1)}, bf16[2,384,384]{2,1,0:T(8,128)(2,1)}, u32[]{:S(2)}, u32[]{:S(2)}) collective-permute-start(bf16[2,384,384]{2,1,0:T(8,128)(2,1)} %pad_maximum_fusion.4), channel_id=1, source_target_pairs={{0,2},{1,3},{2,0},{3,1},{4,6},{5,7},{6,4},{7,5},{8,10},{9,11},{10,... | collective-permute-start | bytes 1769480 | tf_op jit(solution)/shard_map/w_yy/ppermute | solution.py:27
  67.3 1.1 broadcast_select_fusion.3
  68.4 3.4 %collective-permute-done.11.c_ref.d_ref = bf16[4,2,128,512]{3,2,1,0:T(8,128)(2,1)S(1)} collective-permute-done((bf16[4,2,128,512]{3,2,1,0:T(8,128)(2,1)S(1)}, bf16[4,2,128,512]{3,2,1,0:T(8,128)(2,1)S(1)}, u32[]{:S(2)}, u32[]{:S(2)}) %collective-permute-start.11) | collective-permute-done | bytes 1048608 | tf_op jit(solution)/shard_map/kv_z1/ppermute | solution.py:27
  71.9 1.9 %collective-permute-done.12.near_ref = bf16[4,2,128,256]{3,2,1,0:T(8,128)(2,1)S(1)} collective-permute-done((bf16[4,2,128,256]{3,2,1,0:T(8,128)(2,1)S(1)}, bf16[4,2,128,256]{3,2,1,0:T(8,128)(2,1)S(1)}, u32[]{:S(2)}, u32[]{:S(2)}) %collective-permute-start.12) | collective-permute-done | bytes 524320 | tf_op jit(solution)/shard_map/kv_g0/ppermute | solution.py:27
  74.6 6.3 %attend.4.rest_0_ = bf16[512,1536]{1,0:T(8,128)(2,1)} custom-call(s32[4]{0:T(128)} %get-tuple-element.52.picks_ref, bf16[512,1536]{1,0:T(8,128)(2,1)} %q_ref.7, bf16[512,1536]{1,0:T(8,128)(2,1)} %k0_ref.7, bf16[512,1536]{1,0:T(8,128)(2,1)} %v0_ref.7, bf16[512,1536]{1,0:T(8,128)(2,1)} %collective-permute-done.k1_ref, ...), custom_call_target="tpu_custom_call" | custom-call | flops 666666688 | bytes 1000 | tf_op jit(solution)/shard_map/attend/pallas_call | solution.py:192
  80.9 8.3 %collective-permute-done.7.a_ref.b_ref = bf16[4,2,128,256]{3,2,1,0:T(8,128)(2,1)S(1)} collective-permute-done((bf16[4,2,128,256]{3,2,1,0:T(8,128)(2,1)}, bf16[4,2,128,256]{3,2,1,0:T(8,128)(2,1)S(1)}, u32[]{:S(2)}, u32[]{:S(2)}) %collective-permute-start.7) | collective-permute-done | bytes 524320 | tf_op jit(solution)/shard_map/kv_y3/ppermute | solution.py:27
  89.2 2.0 %collective-permute-start.13 = (bf16[4,2,128,256]{3,2,1,0:T(8,128)(2,1)S(1)}, bf16[4,2,128,256]{3,2,1,0:T(8,128)(2,1)}, u32[]{:S(2)}, u32[]{:S(2)}) collective-permute-start(bf16[4,2,128,256]{3,2,1,0:T(8,128)(2,1)S(1)} %collective-permute-done.7.a_ref.b_ref), channel_id=1, source_target_pairs={{0,4},{1,5},{2,14},{3,15},{4,8},{5,9},{6,2},{7,3},{8,12},{9,13},{1... | collective-permute-start | bytes 1572872 | tf_op jit(solution)/shard_map/kv_z3/ppermute | solution.py:27
  91.5 1.6 %collective-permute-start.19 = (bf16[2,384,384]{2,1,0:T(8,128)(2,1)}, bf16[2,384,384]{2,1,0:T(8,128)(2,1)S(1)}, u32[]{:S(2)}, u32[]{:S(2)}) collective-permute-start(bf16[2,384,384]{2,1,0:T(8,128)(2,1)} %collective-permute-done.14.refs_4_), channel_id=1, source_target_pairs={{0,16},{1,17},{2,18},{3,19},{4,20},{5,21},{6,22},{7,23},{8,24},{9,... | collective-permute-start | bytes 1769480 | tf_op jit(solution)/shard_map/w_x2x/ppermute | solution.py:37
  93.0 9.4 %collective-permute-done.16.c_ref.d_ref = bf16[4,2,128,512]{3,2,1,0:T(8,128)(2,1)} collective-permute-done((bf16[4,2,128,512]{3,2,1,0:T(8,128)(2,1)S(1)}, bf16[4,2,128,512]{3,2,1,0:T(8,128)(2,1)}, u32[]{:S(2)}, u32[]{:S(2)}) %collective-permute-start.16) | collective-permute-done | bytes 1048608 | tf_op jit(solution)/shard_map/kv_z2/ppermute | solution.py:27
  103.0 10.0 %attend.5.rest_0_ = bf16[512,1536]{1,0:T(8,128)(2,1)} custom-call(s32[4]{0:T(128)} %get-tuple-element.52.picks_ref, bf16[512,1536]{1,0:T(8,128)(2,1)} %q_ref.7, bf16[512,1536]{1,0:T(8,128)(2,1)} %k0_ref.7, bf16[512,1536]{1,0:T(8,128)(2,1)} %v0_ref.7, bf16[512,1536]{1,0:T(8,128)(2,1)} %collective-permute-done.k1_ref, ...), custom_call_target="tpu_custom_call", output_to_operand_aliasing={{}: (12, {})} | custom-call | flops 1333333376 | bytes 1000 | tf_op jit(solution)/shard_map/attend/pallas_call | solution.py:192
  113.1 1.3 collective-permute-start.20
  114.4 1.4 collective-permute-start.26
  117.7 10.0 %attend.6.rest_0_ = bf16[512,1536]{1,0:T(8,128)(2,1)} custom-call(s32[4]{0:T(128)} %get-tuple-element.52.picks_ref, bf16[512,1536]{1,0:T(8,128)(2,1)} %q_ref.7, bf16[512,1536]{1,0:T(8,128)(2,1)} %k0_ref.7, bf16[512,1536]{1,0:T(8,128)(2,1)} %v0_ref.7, bf16[512,1536]{1,0:T(8,128)(2,1)} %collective-permute-done.k1_ref, ...), custom_call_target="tpu_custom_call", output_to_operand_aliasing={{}: (12, {})} | custom-call | flops 1333333376 | bytes 1000 | tf_op jit(solution)/shard_map/attend/pallas_call | solution.py:192
  127.7 1.5 collective-permute-start.21
  131.9 6.3 %attend.7.att_ref = bf16[512,1536]{1,0:T(8,128)(2,1)} custom-call(s32[4]{0:T(128)} %get-tuple-element.52.picks_ref, bf16[512,1536]{1,0:T(8,128)(2,1)} %q_ref.7, bf16[512,1536]{1,0:T(8,128)(2,1)} %k0_ref.7, bf16[512,1536]{1,0:T(8,128)(2,1)} %v0_ref.7, bf16[512,1536]{1,0:T(8,128)(2,1)} %collective-permute-done.k1_ref, ...), custom_call_target="tpu_custom_call", output_to_operand_aliasing={{}: (12, {})} | custom-call | flops 666666688 | bytes 1000 | tf_op jit(solution)/shard_map/attend/pallas_call | solution.py:192
  139.6 10.8 %project.1 = bf16[512,3072]{1,0:T(8,128)(2,1)} custom-call(s32[10]{0:T(128)} %stack.68.place_ref, bf16[512,1536]{1,0:T(8,128)(2,1)} %attend.7.att_ref, bf16[4,384,384]{2,1,0:T(8,128)(2,1)} %pad_maximum_fusion.refs_0_, bf16[4,384,384]{2,1,0:T(8,128)(2,1)} %collective-permute-done.15.refs_1_, bf16[4,384,384]{2,1,0:T(8,128)(2,1)} %collective-permute-done.22.refs_2_, ...), custom_call_target="tpu_custom_call" | custom-call | flops 1000 | bytes 1000 | tf_op jit(solution)/shard_map/project/pallas_call | solution.py:243
  (82 shorter events, 17.8 us)
Async XLA Ops:
  0.0 15.3 %collective-permute-start = (bf16[512,1536]{1,0:T(8,128)(2,1)}, bf16[512,1536]{1,0:T(8,128)(2,1)}, u32[]{:S(2)}, u32[]{:S(2)}) collective-permute-start(bf16[512,1536]{1,0:T(8,128)(2,1)} %k0_ref.7), channel_id=1, source_target_pairs={{0,1},{1,0},{2,3},{3,2},{4,5},{5,4},{6,7},{7,6},{8,9},{9,8},{10,11... | collective-permute-start | bytes 4718600 | tf_op jit(solution)/shard_map/core_keys/ppermute | solution.py:27
  2.3 8.8 %collective-permute-start.1 = (bf16[384,192]{1,0:T(8,128)(2,1)}, bf16[384,192]{1,0:T(8,128)(2,1)S(1)}, u32[]{:S(2)}, u32[]{:S(2)}) collective-permute-start(bf16[384,192]{1,0:T(8,128)(2,1)} %copy.12), channel_id=1, source_target_pairs={{0,1},{1,0},{2,3},{3,2},{4,5},{5,4},{6,7},{7,6},{8,9},{9,8},{10,11... | collective-permute-start | bytes 442376 | tf_op jit(solution)/shard_map/w_core/ppermute | solution.py:27
  2.5 13.3 %collective-permute-start.2 = (bf16[512,1536]{1,0:T(8,128)(2,1)}, bf16[512,1536]{1,0:T(8,128)(2,1)}, u32[]{:S(2)}, u32[]{:S(2)}) collective-permute-start(bf16[512,1536]{1,0:T(8,128)(2,1)} %v0_ref.7), channel_id=1, source_target_pairs={{0,1},{1,0},{2,3},{3,2},{4,5},{5,4},{6,7},{7,6},{8,9},{9,8},{10,11... | collective-permute-start | bytes 4718600 | tf_op jit(solution)/shard_map/core_values/ppermute | solution.py:27
  4.8 23.1 %collective-permute-start.5 = (bf16[4,2,128,256]{3,2,1,0:T(8,128)(2,1)}, bf16[4,2,128,256]{3,2,1,0:T(8,128)(2,1)}, u32[]{:S(2)}, u32[]{:S(2)}) collective-permute-start(bf16[4,2,128,256]{3,2,1,0:T(8,128)(2,1)} %pad_maximum_fusion.6), channel_id=1, source_target_pairs={{0,2},{1,3},{2,0},{3,1},{4,6},{5,7},{6,4},{7,5},{8,10},{9,11},{10,... | collective-permute-start | bytes 1572872 | tf_op jit(solution)/shard_map/kv_y0/ppermute | solution.py:27
  11.3 11.7 %collective-permute-start.3 = (bf16[384,384]{1,0:T(8,128)(2,1)S(1)}, bf16[384,384]{1,0:T(8,128)(2,1)S(1)}, u32[]{:S(2)}, u32[]{:S(2)}) collective-permute-start(bf16[384,384]{1,0:T(8,128)(2,1)S(1)} %pad_maximum_fusion.7), channel_id=1, source_target_pairs={{0,4},{1,5},{2,6},{3,7},{4,8},{5,9},{6,10},{7,11},{8,12},{9,13},{1... | collective-permute-start | bytes 884744 | tf_op jit(solution)/shard_map/w_up/ppermute | solution.py:27
  12.9 15.0 %collective-permute-start.4 = (bf16[384,384]{1,0:T(8,128)(2,1)S(1)}, bf16[384,384]{1,0:T(8,128)(2,1)S(1)}, u32[]{:S(2)}, u32[]{:S(2)}) collective-permute-start(bf16[384,384]{1,0:T(8,128)(2,1)S(1)} %pad_maximum_fusion.7), channel_id=1, source_target_pairs={{0,12},{1,13},{2,14},{3,15},{4,0},{5,1},{6,2},{7,3},{8,4},{9,5},{1... | collective-permute-start | bytes 884744 | tf_op jit(solution)/shard_map/w_down/ppermute | solution.py:27
  15.3 27.6 %collective-permute-start.8 = (bf16[4,2,128,512]{3,2,1,0:T(8,128)(2,1)S(1)}, bf16[4,2,128,512]{3,2,1,0:T(8,128)(2,1)S(1)}, u32[]{:S(2)}, u32[]{:S(2)}) collective-permute-start(bf16[4,2,128,512]{3,2,1,0:T(8,128)(2,1)S(1)} %pad_maximum_fusion.1), channel_id=1, source_target_pairs={{0,2},{1,3},{2,0},{3,1},{4,6},{5,7},{6,4},{7,5},{8,10},{9,11},{10,... | collective-permute-start | bytes 3145736 | tf_op jit(solution)/shard_map/kv_y1/ppermute | solution.py:27
  15.7 49.6 %collective-permute-start.10 = (bf16[4,2,128,512]{3,2,1,0:T(8,128)(2,1)S(1)}, bf16[4,2,128,512]{3,2,1,0:T(8,128)(2,1)S(1)}, u32[]{:S(2)}, u32[]{:S(2)}) collective-permute-start(bf16[4,2,128,512]{3,2,1,0:T(8,128)(2,1)S(1)} %pad_maximum_fusion.2), channel_id=1, source_target_pairs={{0,2},{1,3},{2,0},{3,1},{4,6},{5,7},{6,4},{7,5},{8,10},{9,11},{10,... | collective-permute-start | bytes 3145736 | tf_op jit(solution)/shard_map/kv_y2/ppermute | solution.py:27
  28.0 11.7 %collective-permute-start.6 = (bf16[384,384]{1,0:T(8,128)(2,1)S(1)}, bf16[384,384]{1,0:T(8,128)(2,1)S(1)}, u32[]{:S(2)}, u32[]{:S(2)}) collective-permute-start(bf16[384,384]{1,0:T(8,128)(2,1)S(1)} %collective-permute-done.3), channel_id=1, source_target_pairs={{0,4},{1,5},{2,6},{3,7},{4,8},{5,9},{6,10},{7,11},{8,12},{9,13},{1... | collective-permute-start | bytes 884744 | tf_op jit(solution)/shard_map/w_up2/ppermute | solution.py:27
  29.1 20.2 %collective-permute-start.9 = (bf16[4,2,128,256]{3,2,1,0:T(8,128)(2,1)}, bf16[4,2,128,256]{3,2,1,0:T(8,128)(2,1)S(1)}, u32[]{:S(2)}, u32[]{:S(2)}) collective-permute-start(bf16[4,2,128,256]{3,2,1,0:T(8,128)(2,1)} %collective-permute-done.5.a_ref.b_ref), channel_id=1, source_target_pairs={{0,4},{1,5},{2,14},{3,15},{4,8},{5,9},{6,2},{7,3},{8,12},{9,13},{1... | collective-permute-start | bytes 1572872 | tf_op jit(solution)/shard_map/kv_z0/ppermute | solution.py:27
  40.6 50.7 %collective-permute-start.14 = (bf16[2,384,384]{2,1,0:T(8,128)(2,1)}, bf16[2,384,384]{2,1,0:T(8,128)(2,1)}, u32[]{:S(2)}, u32[]{:S(2)}) collective-permute-start(bf16[2,384,384]{2,1,0:T(8,128)(2,1)} %pad_maximum_fusion.3), channel_id=1, source_target_pairs={{0,2},{1,3},{2,0},{3,1},{4,6},{5,7},{6,4},{7,5},{8,10},{9,11},{10,... | collective-permute-start | bytes 1769480 | tf_op jit(solution)/shard_map/w_yx/ppermute | solution.py:27
  42.9 48.4 %copy-start.3 = (bf16[4,2,128,512]{3,2,1,0:T(8,128)(2,1)}, bf16[4,2,128,512]{3,2,1,0:T(8,128)(2,1)S(1)}, u32[]{:S(2)}) copy-start(bf16[4,2,128,512]{3,2,1,0:T(8,128)(2,1)S(1)} %collective-permute-done.8.a_ref.b_ref) | copy-start | bytes 3145732
  44.3 47.2 %collective-permute-start.15 = (bf16[4,384,384]{2,1,0:T(8,128)(2,1)}, bf16[4,384,384]{2,1,0:T(8,128)(2,1)}, u32[]{:S(2)}, u32[]{:S(2)}) collective-permute-start(bf16[4,384,384]{2,1,0:T(8,128)(2,1)} %pad_maximum_fusion.refs_0_), channel_id=1, source_target_pairs={{0,16},{1,17},{2,18},{3,19},{4,20},{5,21},{6,22},{7,23},{8,24},{9,... | collective-permute-start | bytes 3538952 | tf_op jit(solution)/shard_map/w_x1/ppermute | solution.py:37
  46.2 25.7 %collective-permute-start.11 = (bf16[4,2,128,512]{3,2,1,0:T(8,128)(2,1)S(1)}, bf16[4,2,128,512]{3,2,1,0:T(8,128)(2,1)S(1)}, u32[]{:S(2)}, u32[]{:S(2)}) collective-permute-start(bf16[4,2,128,512]{3,2,1,0:T(8,128)(2,1)S(1)} %collective-permute-done.8.a_ref.b_ref), channel_id=1, source_target_pairs={{0,4},{1,5},{2,14},{3,15},{4,8},{5,9},{6,2},{7,3},{8,12},{9,13},{1... | collective-permute-start | bytes 3145736 | tf_op jit(solution)/shard_map/kv_z1/ppermute | solution.py:27
  49.3 39.9 %collective-permute-start.7 = (bf16[4,2,128,256]{3,2,1,0:T(8,128)(2,1)}, bf16[4,2,128,256]{3,2,1,0:T(8,128)(2,1)S(1)}, u32[]{:S(2)}, u32[]{:S(2)}) collective-permute-start(bf16[4,2,128,256]{3,2,1,0:T(8,128)(2,1)} %pad_maximum_fusion.5), channel_id=1, source_target_pairs={{0,2},{1,3},{2,0},{3,1},{4,6},{5,7},{6,4},{7,5},{8,10},{9,11},{10,... | collective-permute-start | bytes 1572872 | tf_op jit(solution)/shard_map/kv_y3/ppermute | solution.py:27
  65.3 47.6 %copy-start.2 = (bf16[4,2,128,512]{3,2,1,0:T(8,128)(2,1)}, bf16[4,2,128,512]{3,2,1,0:T(8,128)(2,1)S(1)}, u32[]{:S(2)}) copy-start(bf16[4,2,128,512]{3,2,1,0:T(8,128)(2,1)S(1)} %collective-permute-done.10.a_ref.b_ref) | copy-start | bytes 3145732
  65.3 47.8 %collective-permute-start.18 = (bf16[2,384,384]{2,1,0:T(8,128)(2,1)}, bf16[2,384,384]{2,1,0:T(8,128)(2,1)}, u32[]{:S(2)}, u32[]{:S(2)}) collective-permute-start(bf16[2,384,384]{2,1,0:T(8,128)(2,1)} %pad_maximum_fusion.4), channel_id=1, source_target_pairs={{0,2},{1,3},{2,0},{3,1},{4,6},{5,7},{6,4},{7,5},{8,10},{9,11},{10,... | collective-permute-start | bytes 1769480 | tf_op jit(solution)/shard_map/w_yy/ppermute | solution.py:27
  71.9 1.9 %collective-permute-start.12 = (bf16[4,2,128,256]{3,2,1,0:T(8,128)(2,1)S(1)}, bf16[4,2,128,256]{3,2,1,0:T(8,128)(2,1)S(1)}, u32[]{:S(2)}, u32[]{:S(2)}) collective-permute-start(bf16[4,2,128,256]{3,2,1,0:T(8,128)(2,1)S(1)} %broadcast_select_fusion.3), channel_id=1, source_target_pairs={{0,1},{1,0},{2,3},{3,2},{4,5},{5,4},{6,7},{7,6},{8,9},{9,8},{10,11... | collective-permute-start | bytes 1572872 | tf_op jit(solution)/shard_map/kv_g0/ppermute | solution.py:27
  74.6 27.9 %collective-permute-start.16 = (bf16[4,2,128,512]{3,2,1,0:T(8,128)(2,1)S(1)}, bf16[4,2,128,512]{3,2,1,0:T(8,128)(2,1)}, u32[]{:S(2)}, u32[]{:S(2)}) collective-permute-start(bf16[4,2,128,512]{3,2,1,0:T(8,128)(2,1)S(1)} %collective-permute-done.10.a_ref.b_ref), channel_id=1, source_target_pairs={{0,4},{1,5},{2,14},{3,15},{4,8},{5,9},{6,2},{7,3},{8,12},{9,13},{1... | collective-permute-start | bytes 3145736 | tf_op jit(solution)/shard_map/kv_z2/ppermute | solution.py:27
  89.2 38.4 %copy-start.5 = (bf16[4,2,128,256]{3,2,1,0:T(8,128)(2,1)}, bf16[4,2,128,256]{3,2,1,0:T(8,128)(2,1)S(1)}, u32[]{:S(2)}) copy-start(bf16[4,2,128,256]{3,2,1,0:T(8,128)(2,1)S(1)} %collective-permute-done.7.a_ref.b_ref) | copy-start | bytes 1572868
  89.2 38.4 %collective-permute-start.13 = (bf16[4,2,128,256]{3,2,1,0:T(8,128)(2,1)S(1)}, bf16[4,2,128,256]{3,2,1,0:T(8,128)(2,1)}, u32[]{:S(2)}, u32[]{:S(2)}) collective-permute-start(bf16[4,2,128,256]{3,2,1,0:T(8,128)(2,1)S(1)} %collective-permute-done.7.a_ref.b_ref), channel_id=1, source_target_pairs={{0,4},{1,5},{2,14},{3,15},{4,8},{5,9},{6,2},{7,3},{8,12},{9,13},{1... | collective-permute-start | bytes 1572872 | tf_op jit(solution)/shard_map/kv_z3/ppermute | solution.py:27
  91.4 11.1 %collective-permute-start.17 = (bf16[4,2,128,512]{3,2,1,0:T(8,128)(2,1)S(1)}, bf16[4,2,128,512]{3,2,1,0:T(8,128)(2,1)}, u32[]{:S(2)}, u32[]{:S(2)}) collective-permute-start(bf16[4,2,128,512]{3,2,1,0:T(8,128)(2,1)S(1)} %broadcast_select_fusion.1), channel_id=1, source_target_pairs={{0,1},{1,0},{2,3},{3,2},{4,5},{5,4},{6,7},{7,6},{8,9},{9,8},{10,11... | collective-permute-start | bytes 3145736 | tf_op jit(solution)/shard_map/kv_g1/ppermute | solution.py:27
  91.5 22.9 %collective-permute-start.19 = (bf16[2,384,384]{2,1,0:T(8,128)(2,1)}, bf16[2,384,384]{2,1,0:T(8,128)(2,1)S(1)}, u32[]{:S(2)}, u32[]{:S(2)}) collective-permute-start(bf16[2,384,384]{2,1,0:T(8,128)(2,1)} %collective-permute-done.14.refs_4_), channel_id=1, source_target_pairs={{0,16},{1,17},{2,18},{3,19},{4,20},{5,21},{6,22},{7,23},{8,24},{9,... | collective-permute-start | bytes 1769480 | tf_op jit(solution)/shard_map/w_x2x/ppermute | solution.py:37
  102.5 35.7 %collective-permute-start.23 = (bf16[4,384,384]{2,1,0:T(8,128)(2,1)}, bf16[4,384,384]{2,1,0:T(8,128)(2,1)S(1)}, u32[]{:S(2)}, u32[]{:S(2)}) collective-permute-start(bf16[4,384,384]{2,1,0:T(8,128)(2,1)} %collective-permute-done.15.refs_1_), channel_id=1, source_target_pairs={{0,1},{1,0},{2,3},{3,2},{4,5},{5,4},{6,7},{7,6},{8,9},{9,8},{10,11... | collective-permute-start | bytes 3538952 | tf_op jit(solution)/shard_map/w_d1/ppermute | solution.py:27
  102.5 27.6 %collective-permute-start.22 = (bf16[4,384,384]{2,1,0:T(8,128)(2,1)}, bf16[4,384,384]{2,1,0:T(8,128)(2,1)}, u32[]{:S(2)}, u32[]{:S(2)}) collective-permute-start(bf16[4,384,384]{2,1,0:T(8,128)(2,1)} %pad_maximum_fusion.refs_0_), channel_id=1, source_target_pairs={{0,1},{1,0},{2,3},{3,2},{4,5},{5,4},{6,7},{7,6},{8,9},{9,8},{10,11... | collective-permute-start | bytes 3538952 | tf_op jit(solution)/shard_map/w_c1/ppermute | solution.py:27
  113.1 3.6 %collective-permute-start.20 = (bf16[4,2,128,512]{3,2,1,0:T(8,128)(2,1)S(1)}, bf16[4,2,128,512]{3,2,1,0:T(8,128)(2,1)S(1)}, u32[]{:S(2)}, u32[]{:S(2)}) collective-permute-start(bf16[4,2,128,512]{3,2,1,0:T(8,128)(2,1)S(1)} %broadcast_select_fusion), channel_id=1, source_target_pairs={{0,1},{1,0},{2,3},{3,2},{4,5},{5,4},{6,7},{7,6},{8,9},{9,8},{10,11... | collective-permute-start | bytes 3145736 | tf_op jit(solution)/shard_map/kv_g2/ppermute | solution.py:27
  114.4 15.6 %collective-permute-start.26 = (bf16[2,384,384]{2,1,0:T(8,128)(2,1)}, bf16[2,384,384]{2,1,0:T(8,128)(2,1)}, u32[]{:S(2)}, u32[]{:S(2)}) collective-permute-start(bf16[2,384,384]{2,1,0:T(8,128)(2,1)} %collective-permute-done.18.refs_8_), channel_id=1, source_target_pairs={{0,16},{1,17},{2,18},{3,19},{4,20},{5,21},{6,22},{7,23},{8,24},{9,... | collective-permute-start | bytes 1769480 | tf_op jit(solution)/shard_map/w_x2y/ppermute | solution.py:37
  127.7 3.1 %collective-permute-start.21 = (bf16[4,2,128,256]{3,2,1,0:T(8,128)(2,1)S(1)}, bf16[4,2,128,256]{3,2,1,0:T(8,128)(2,1)}, u32[]{:S(2)}, u32[]{:S(2)}) collective-permute-start(bf16[4,2,128,256]{3,2,1,0:T(8,128)(2,1)S(1)} %broadcast_select_fusion.2), channel_id=1, source_target_pairs={{0,1},{1,0},{2,3},{3,2},{4,5},{5,4},{6,7},{7,6},{8,9},{9,8},{10,11... | collective-permute-start | bytes 1572872 | tf_op jit(solution)/shard_map/kv_g3/ppermute | solution.py:27
  129.2 9.0 %collective-permute-start.24 = (bf16[2,384,384]{2,1,0:T(8,128)(2,1)}, bf16[2,384,384]{2,1,0:T(8,128)(2,1)S(1)}, u32[]{:S(2)}, u32[]{:S(2)}) collective-permute-start(bf16[2,384,384]{2,1,0:T(8,128)(2,1)} %collective-permute-done.14.refs_4_), channel_id=1, source_target_pairs={{0,1},{1,0},{2,3},{3,2},{4,5},{5,4},{6,7},{7,6},{8,9},{9,8},{10,11... | collective-permute-start | bytes 1769480 | tf_op jit(solution)/shard_map/w_c2x/ppermute | solution.py:27
  130.1 8.2 %collective-permute-start.25 = (bf16[2,384,384]{2,1,0:T(8,128)(2,1)S(1)}, bf16[2,384,384]{2,1,0:T(8,128)(2,1)S(1)}, u32[]{:S(2)}, u32[]{:S(2)}) collective-permute-start(bf16[2,384,384]{2,1,0:T(8,128)(2,1)S(1)} %collective-permute-done.19.refs_5_), channel_id=1, source_target_pairs={{0,1},{1,0},{2,3},{3,2},{4,5},{5,4},{6,7},{7,6},{8,9},{9,8},{10,11... | collective-permute-start | bytes 1769480 | tf_op jit(solution)/shard_map/w_d2x/ppermute | solution.py:27
  130.1 8.2 %collective-permute-start.28 = (bf16[2,384,384]{2,1,0:T(8,128)(2,1)}, bf16[2,384,384]{2,1,0:T(8,128)(2,1)}, u32[]{:S(2)}, u32[]{:S(2)}) collective-permute-start(bf16[2,384,384]{2,1,0:T(8,128)(2,1)} %collective-permute-done.26.refs_9_), channel_id=1, source_target_pairs={{0,1},{1,0},{2,3},{3,2},{4,5},{5,4},{6,7},{7,6},{8,9},{9,8},{10,11... | collective-permute-start | bytes 1769480 | tf_op jit(solution)/shard_map/w_d2y/ppermute | solution.py:27
  130.9 7.4 %collective-permute-start.27 = (bf16[2,384,384]{2,1,0:T(8,128)(2,1)}, bf16[2,384,384]{2,1,0:T(8,128)(2,1)}, u32[]{:S(2)}, u32[]{:S(2)}) collective-permute-start(bf16[2,384,384]{2,1,0:T(8,128)(2,1)} %collective-permute-done.18.refs_8_), channel_id=1, source_target_pairs={{0,1},{1,0},{2,3},{3,2},{4,5},{5,4},{6,7},{7,6},{8,9},{9,8},{10,11... | collective-permute-start | bytes 1769480 | tf_op jit(solution)/shard_map/w_c2y/ppermute | solution.py:27
  (11 other events, 74.6 us)

commit v3 on v2

--- a/solution.py
+++ b/solution.py
@@ -146,9 +146,9 @@
     factor = math.log2(math.e) / math.sqrt(size)
     ones = jnp.ones((span, size), jnp.bfloat16)
     values = [jnp.concatenate([v, ones], axis=1) for v in values]
-    for m in range(rows // BLOCK):
-        mine = slice(m * BLOCK, (m + 1) * BLOCK)
-        q = q_ref[mine, :]
+
+    def scores_of(m):
+        q = q_ref[m * BLOCK : (m + 1) * BLOCK, :]
         scores, top = [], None
         for n, k in enumerate(keys):
             s = lax.dot_general(q, k, (((1,), (1,)), ((), ())), preferred_element_type=jnp.float32)
@@ -157,12 +157,22 @@
             scores.append(s)
             t = jnp.max(s, axis=1, keepdims=True)
             top = t if top is None else jnp.maximum(top, t)
+        return scores, top
+
+    def finish(m, scores, top):
         total = None
         for s, v in zip(scores, values):
             w = jnp.exp2((s - top) * factor).astype(jnp.bfloat16)
             part = jnp.dot(w, v, preferred_element_type=jnp.float32)
             total = part if total is None else total + part
-        o_ref[mine, :] = (total[:, :size] / total[:, size:]).astype(o_ref.dtype)
+        o_ref[m * BLOCK : (m + 1) * BLOCK, :] = (total[:, :size] / total[:, size:]).astype(o_ref.dtype)
+
+    held = scores_of(0)
+    for m in range(1, rows // BLOCK):
+        ahead = scores_of(m)
+        finish(m - 1, *held)
+        held = ahead
+    finish(rows // BLOCK - 1, *held)
 
 
 def attend(first_head, per_part, picks, queries, key_rows, value_rows, core_k, core_v, near, y, z, bias, into):

time: 151 us -> 149 us (0.987)
  Pallas kernels: 44.8 us -> 41.9 us
    pallas_call x4, Pallas kernels: 32.5 us -> 29.7 us  [attend(): pl.pallas_call(attend_kernel, grid_spec=pltpu.PrefetchScalarGridSpec(num_...]
  transfers between devices with their start and end apart: 29 -> 29, of which waited for: 13 -> 12; matrix products, arithmetic and copies ran while one was open for 8% -> 8% of each run, Pallas kernels for 23% -> 21%
where the time goes in v3:
time: 149 us
  waiting for transfers between devices  62.2 us (42%)
  Pallas kernels  41.9 us (28%)
  starting transfers between devices  29.4 us (20%)
  local copies, waits for them, and re-layouts  7.82 us (5%)
  other arithmetic  6.76 us (5%)
    ppermute x26, waiting for transfers between devices, moved(): return lax.ppermute(value, 'blk', [(s, dest(s)) for s in range(count)])  60.5 us
    pallas_call x4, Pallas kernels, attend(): pl.pallas_call(attend_kernel, grid_spec=pltpu.PrefetchScalarGridSpec(num_...  29.7 us
    ppermute x26, starting transfers between devices, moved(): return lax.ppermute(value, 'blk', [(s, dest(s)) for s in range(count)])  24.5 us
    pallas_call x1, Pallas kernels, project(): pl.pallas_call(project_kernel, grid_spec=pltpu.PrefetchScalarGridSpec(num...  10.8 us
    ppermute x3, starting transfers between devices, moved_all(): return lax.ppermute(value, ('groups', 'blk'), pairs)  4.94 us
    unnamed x30, local copies, waits for them, and re-layouts  4.08 us
  transfers between devices with their start and end apart: 29, of which 12 were waited for; matrix products, arithmetic and copies ran while one was open for 8% of the time, Pallas kernels for 21%

profile of v3, /device:TPU:0, one launch (start us, length us, event | category | flops | bytes accessed | tf_op | source)
XLA Modules:
  0.0 148.6 jit_solution(8103940312734705166)
XLA Ops:
  4.8 2.6 %collective-permute-start.5 = (bf16[4,2,128,256]{3,2,1,0:T(8,128)(2,1)}, bf16[4,2,128,256]{3,2,1,0:T(8,128)(2,1)}, u32[]{:S(2)}, u32[]{:S(2)}) collective-permute-start(bf16[4,2,128,256]{3,2,1,0:T(8,128)(2,1)} %pad_maximum_fusion.6), channel_id=1, source_target_pairs={{0,2},{1,3},{2,0},{3,1},{4,6},{5,7},{6,4},{7,5},{8,10},{9,11},{10,... | collective-permute-start | bytes 1572872 | tf_op jit(solution)/shard_map/kv_y0/ppermute | solution.py:27
  9.4 1.4 plan.1
  11.3 1.6 %collective-permute-start.3 = (bf16[384,384]{1,0:T(8,128)(2,1)S(1)}, bf16[384,384]{1,0:T(8,128)(2,1)S(1)}, u32[]{:S(2)}, u32[]{:S(2)}) collective-permute-start(bf16[384,384]{1,0:T(8,128)(2,1)S(1)} %pad_maximum_fusion.7), channel_id=1, source_target_pairs={{0,4},{1,5},{2,6},{3,7},{4,8},{5,9},{6,10},{7,11},{8,12},{9,13},{1... | collective-permute-start | bytes 884744 | tf_op jit(solution)/shard_map/w_up/ppermute | solution.py:27
  12.9 2.2 %collective-permute-start.4 = (bf16[384,384]{1,0:T(8,128)(2,1)S(1)}, bf16[384,384]{1,0:T(8,128)(2,1)S(1)}, u32[]{:S(2)}, u32[]{:S(2)}) collective-permute-start(bf16[384,384]{1,0:T(8,128)(2,1)S(1)} %pad_maximum_fusion.7), channel_id=1, source_target_pairs={{0,12},{1,13},{2,14},{3,15},{4,0},{5,1},{6,2},{7,3},{8,4},{9,5},{1... | collective-permute-start | bytes 884744 | tf_op jit(solution)/shard_map/w_down/ppermute | solution.py:27
  15.7 1.7 %collective-permute-start.10 = (bf16[4,2,128,512]{3,2,1,0:T(8,128)(2,1)S(1)}, bf16[4,2,128,512]{3,2,1,0:T(8,128)(2,1)S(1)}, u32[]{:S(2)}, u32[]{:S(2)}) collective-permute-start(bf16[4,2,128,512]{3,2,1,0:T(8,128)(2,1)S(1)} %pad_maximum_fusion.2), channel_id=1, source_target_pairs={{0,2},{1,3},{2,0},{3,1},{4,6},{5,7},{6,4},{7,5},{8,10},{9,11},{10,... | collective-permute-start | bytes 3145736 | tf_op jit(solution)/shard_map/kv_y2/ppermute | solution.py:27
  17.4 5.6 %collective-permute-done.3 = bf16[384,384]{1,0:T(8,128)(2,1)S(1)} collective-permute-done((bf16[384,384]{1,0:T(8,128)(2,1)S(1)}, bf16[384,384]{1,0:T(8,128)(2,1)S(1)}, u32[]{:S(2)}, u32[]{:S(2)}) %collective-permute-start.3) | collective-permute-done | bytes 294944 | tf_op jit(solution)/shard_map/w_up/ppermute | solution.py:27
  23.0 4.9 %collective-permute-done.4 = bf16[384,384]{1,0:T(8,128)(2,1)S(1)} collective-permute-done((bf16[384,384]{1,0:T(8,128)(2,1)S(1)}, bf16[384,384]{1,0:T(8,128)(2,1)S(1)}, u32[]{:S(2)}, u32[]{:S(2)}) %collective-permute-start.4) | collective-permute-done | bytes 294944 | tf_op jit(solution)/shard_map/w_down/ppermute | solution.py:27
  28.0 1.1 collective-permute-start.6
  29.8 9.9 %collective-permute-done.6 = bf16[384,384]{1,0:T(8,128)(2,1)S(1)} collective-permute-done((bf16[384,384]{1,0:T(8,128)(2,1)S(1)}, bf16[384,384]{1,0:T(8,128)(2,1)S(1)}, u32[]{:S(2)}, u32[]{:S(2)}) %collective-permute-start.6) | collective-permute-done | bytes 294944 | tf_op jit(solution)/shard_map/w_up2/ppermute | solution.py:27
  41.1 1.8 %collective-permute-done.8.a_ref.b_ref = bf16[4,2,128,512]{3,2,1,0:T(8,128)(2,1)S(1)} collective-permute-done((bf16[4,2,128,512]{3,2,1,0:T(8,128)(2,1)S(1)}, bf16[4,2,128,512]{3,2,1,0:T(8,128)(2,1)S(1)}, u32[]{:S(2)}, u32[]{:S(2)}) %collective-permute-start.8) | collective-permute-done | bytes 1048608 | tf_op jit(solution)/shard_map/kv_y1/ppermute | solution.py:27
  42.9 1.4 pad_maximum_fusion.refs_0_
  44.3 2.0 %collective-permute-start.15 = (bf16[4,384,384]{2,1,0:T(8,128)(2,1)}, bf16[4,384,384]{2,1,0:T(8,128)(2,1)}, u32[]{:S(2)}, u32[]{:S(2)}) collective-permute-start(bf16[4,384,384]{2,1,0:T(8,128)(2,1)} %pad_maximum_fusion.refs_0_), channel_id=1, source_target_pairs={{0,16},{1,17},{2,18},{3,19},{4,20},{5,21},{6,22},{7,23},{8,24},{9,... | collective-permute-start | bytes 3538952 | tf_op jit(solution)/shard_map/w_x1/ppermute | solution.py:37
  46.2 1.6 %collective-permute-start.11 = (bf16[4,2,128,512]{3,2,1,0:T(8,128)(2,1)S(1)}, bf16[4,2,128,512]{3,2,1,0:T(8,128)(2,1)S(1)}, u32[]{:S(2)}, u32[]{:S(2)}) collective-permute-start(bf16[4,2,128,512]{3,2,1,0:T(8,128)(2,1)S(1)} %collective-permute-done.8.a_ref.b_ref), channel_id=1, source_target_pairs={{0,4},{1,5},{2,14},{3,15},{4,8},{5,9},{6,2},{7,3},{8,12},{9,13},{1... | collective-permute-start | bytes 3145736 | tf_op jit(solution)/shard_map/kv_z1/ppermute | solution.py:27
  49.3 2.9 %collective-permute-start.7 = (bf16[4,2,128,256]{3,2,1,0:T(8,128)(2,1)}, bf16[4,2,128,256]{3,2,1,0:T(8,128)(2,1)S(1)}, u32[]{:S(2)}, u32[]{:S(2)}) collective-permute-start(bf16[4,2,128,256]{3,2,1,0:T(8,128)(2,1)} %pad_maximum_fusion.5), channel_id=1, source_target_pairs={{0,2},{1,3},{2,0},{3,1},{4,6},{5,7},{6,4},{7,5},{8,10},{9,11},{10,... | collective-permute-start | bytes 1572872 | tf_op jit(solution)/shard_map/kv_y3/ppermute | solution.py:27
  52.2 13.1 %collective-permute-done.10.a_ref.b_ref = bf16[4,2,128,512]{3,2,1,0:T(8,128)(2,1)S(1)} collective-permute-done((bf16[4,2,128,512]{3,2,1,0:T(8,128)(2,1)S(1)}, bf16[4,2,128,512]{3,2,1,0:T(8,128)(2,1)S(1)}, u32[]{:S(2)}, u32[]{:S(2)}) %collective-permute-start.10) | collective-permute-done | bytes 1048608 | tf_op jit(solution)/shard_map/kv_y2/ppermute | solution.py:27
  65.3 2.0 %collective-permute-start.18 = (bf16[2,384,384]{2,1,0:T(8,128)(2,1)}, bf16[2,384,384]{2,1,0:T(8,128)(2,1)}, u32[]{:S(2)}, u32[]{:S(2)}) collective-permute-start(bf16[2,384,384]{2,1,0:T(8,128)(2,1)} %pad_maximum_fusion.4), channel_id=1, source_target_pairs={{0,2},{1,3},{2,0},{3,1},{4,6},{5,7},{6,4},{7,5},{8,10},{9,11},{10,... | collective-permute-start | bytes 1769480 | tf_op jit(solution)/shard_map/w_yy/ppermute | solution.py:27
  67.3 1.1 broadcast_select_fusion.3
  68.4 3.4 %collective-permute-done.11.c_ref.d_ref = bf16[4,2,128,512]{3,2,1,0:T(8,128)(2,1)S(1)} collective-permute-done((bf16[4,2,128,512]{3,2,1,0:T(8,128)(2,1)S(1)}, bf16[4,2,128,512]{3,2,1,0:T(8,128)(2,1)S(1)}, u32[]{:S(2)}, u32[]{:S(2)}) %collective-permute-start.11) | collective-permute-done | bytes 1048608 | tf_op jit(solution)/shard_map/kv_z1/ppermute | solution.py:27
  71.9 1.9 %collective-permute-done.12.near_ref = bf16[4,2,128,256]{3,2,1,0:T(8,128)(2,1)S(1)} collective-permute-done((bf16[4,2,128,256]{3,2,1,0:T(8,128)(2,1)S(1)}, bf16[4,2,128,256]{3,2,1,0:T(8,128)(2,1)S(1)}, u32[]{:S(2)}, u32[]{:S(2)}) %collective-permute-start.12) | collective-permute-done | bytes 524320 | tf_op jit(solution)/shard_map/kv_g0/ppermute | solution.py:27
  74.6 5.8 %attend.4.rest_0_ = bf16[512,1536]{1,0:T(8,128)(2,1)} custom-call(s32[4]{0:T(128)} %get-tuple-element.52.picks_ref, bf16[512,1536]{1,0:T(8,128)(2,1)} %q_ref.7, bf16[512,1536]{1,0:T(8,128)(2,1)} %k0_ref.7, bf16[512,1536]{1,0:T(8,128)(2,1)} %v0_ref.7, bf16[512,1536]{1,0:T(8,128)(2,1)} %collective-permute-done.k1_ref, ...), custom_call_target="tpu_custom_call" | custom-call | flops 666666688 | bytes 1000 | tf_op jit(solution)/shard_map/attend/pallas_call | solution.py:202
  80.4 8.8 %collective-permute-done.7.a_ref.b_ref = bf16[4,2,128,256]{3,2,1,0:T(8,128)(2,1)S(1)} collective-permute-done((bf16[4,2,128,256]{3,2,1,0:T(8,128)(2,1)}, bf16[4,2,128,256]{3,2,1,0:T(8,128)(2,1)S(1)}, u32[]{:S(2)}, u32[]{:S(2)}) %collective-permute-start.7) | collective-permute-done | bytes 524320 | tf_op jit(solution)/shard_map/kv_y3/ppermute | solution.py:27
  89.2 2.0 %collective-permute-start.13 = (bf16[4,2,128,256]{3,2,1,0:T(8,128)(2,1)S(1)}, bf16[4,2,128,256]{3,2,1,0:T(8,128)(2,1)}, u32[]{:S(2)}, u32[]{:S(2)}) collective-permute-start(bf16[4,2,128,256]{3,2,1,0:T(8,128)(2,1)S(1)} %collective-permute-done.7.a_ref.b_ref), channel_id=1, source_target_pairs={{0,4},{1,5},{2,14},{3,15},{4,8},{5,9},{6,2},{7,3},{8,12},{9,13},{1... | collective-permute-start | bytes 1572872 | tf_op jit(solution)/shard_map/kv_z3/ppermute | solution.py:27
  91.5 1.6 %collective-permute-start.19 = (bf16[2,384,384]{2,1,0:T(8,128)(2,1)}, bf16[2,384,384]{2,1,0:T(8,128)(2,1)S(1)}, u32[]{:S(2)}, u32[]{:S(2)}) collective-permute-start(bf16[2,384,384]{2,1,0:T(8,128)(2,1)} %collective-permute-done.14.refs_4_), channel_id=1, source_target_pairs={{0,16},{1,17},{2,18},{3,19},{4,20},{5,21},{6,22},{7,23},{8,24},{9,... | collective-permute-start | bytes 1769480 | tf_op jit(solution)/shard_map/w_x2x/ppermute | solution.py:37
  93.0 9.4 %collective-permute-done.16.c_ref.d_ref = bf16[4,2,128,512]{3,2,1,0:T(8,128)(2,1)} collective-permute-done((bf16[4,2,128,512]{3,2,1,0:T(8,128)(2,1)S(1)}, bf16[4,2,128,512]{3,2,1,0:T(8,128)(2,1)}, u32[]{:S(2)}, u32[]{:S(2)}) %collective-permute-start.16) | collective-permute-done | bytes 1048608 | tf_op jit(solution)/shard_map/kv_z2/ppermute | solution.py:27
  103.0 9.0 %attend.5.rest_0_ = bf16[512,1536]{1,0:T(8,128)(2,1)} custom-call(s32[4]{0:T(128)} %get-tuple-element.52.picks_ref, bf16[512,1536]{1,0:T(8,128)(2,1)} %q_ref.7, bf16[512,1536]{1,0:T(8,128)(2,1)} %k0_ref.7, bf16[512,1536]{1,0:T(8,128)(2,1)} %v0_ref.7, bf16[512,1536]{1,0:T(8,128)(2,1)} %collective-permute-done.k1_ref, ...), custom_call_target="tpu_custom_call", output_to_operand_aliasing={{}: (12, {})} | custom-call | flops 1333333376 | bytes 1000 | tf_op jit(solution)/shard_map/attend/pallas_call | solution.py:202
  112.2 1.3 collective-permute-start.20
  113.5 1.4 collective-permute-start.26
  116.7 9.0 %attend.6.rest_0_ = bf16[512,1536]{1,0:T(8,128)(2,1)} custom-call(s32[4]{0:T(128)} %get-tuple-element.52.picks_ref, bf16[512,1536]{1,0:T(8,128)(2,1)} %q_ref.7, bf16[512,1536]{1,0:T(8,128)(2,1)} %k0_ref.7, bf16[512,1536]{1,0:T(8,128)(2,1)} %v0_ref.7, bf16[512,1536]{1,0:T(8,128)(2,1)} %collective-permute-done.k1_ref, ...), custom_call_target="tpu_custom_call", output_to_operand_aliasing={{}: (12, {})} | custom-call | flops 1333333376 | bytes 1000 | tf_op jit(solution)/shard_map/attend/pallas_call | solution.py:202
  125.8 1.5 collective-permute-start.21
  127.4 1.7 %collective-permute-done.26.refs_9_ = bf16[2,384,384]{2,1,0:T(8,128)(2,1)} collective-permute-done((bf16[2,384,384]{2,1,0:T(8,128)(2,1)}, bf16[2,384,384]{2,1,0:T(8,128)(2,1)}, u32[]{:S(2)}, u32[]{:S(2)}) %collective-permute-start.26) | collective-permute-done | bytes 589856 | tf_op jit(solution)/shard_map/w_x2y/ppermute | solution.py:37
  130.4 5.8 %attend.7.att_ref = bf16[512,1536]{1,0:T(8,128)(2,1)} custom-call(s32[4]{0:T(128)} %get-tuple-element.52.picks_ref, bf16[512,1536]{1,0:T(8,128)(2,1)} %q_ref.7, bf16[512,1536]{1,0:T(8,128)(2,1)} %k0_ref.7, bf16[512,1536]{1,0:T(8,128)(2,1)} %v0_ref.7, bf16[512,1536]{1,0:T(8,128)(2,1)} %collective-permute-done.k1_ref, ...), custom_call_target="tpu_custom_call", output_to_operand_aliasing={{}: (12, {})} | custom-call | flops 666666688 | bytes 1000 | tf_op jit(solution)/shard_map/attend/pallas_call | solution.py:202
  137.6 10.8 %project.1 = bf16[512,3072]{1,0:T(8,128)(2,1)} custom-call(s32[10]{0:T(128)} %stack.68.place_ref, bf16[512,1536]{1,0:T(8,128)(2,1)} %attend.7.att_ref, bf16[4,384,384]{2,1,0:T(8,128)(2,1)} %pad_maximum_fusion.refs_0_, bf16[4,384,384]{2,1,0:T(8,128)(2,1)} %collective-permute-done.15.refs_1_, bf16[4,384,384]{2,1,0:T(8,128)(2,1)} %collective-permute-done.22.refs_2_, ...), custom_call_target="tpu_custom_call" | custom-call | flops 1000 | bytes 1000 | tf_op jit(solution)/shard_map/project/pallas_call | solution.py:253
  (82 shorter events, 17.5 us)
Async XLA Ops:
  0.0 15.3 %collective-permute-start = (bf16[512,1536]{1,0:T(8,128)(2,1)}, bf16[512,1536]{1,0:T(8,128)(2,1)}, u32[]{:S(2)}, u32[]{:S(2)}) collective-permute-start(bf16[512,1536]{1,0:T(8,128)(2,1)} %k0_ref.7), channel_id=1, source_target_pairs={{0,1},{1,0},{2,3},{3,2},{4,5},{5,4},{6,7},{7,6},{8,9},{9,8},{10,11... | collective-permute-start | bytes 4718600 | tf_op jit(solution)/shard_map/core_keys/ppermute | solution.py:27
  2.3 8.8 %collective-permute-start.1 = (bf16[384,192]{1,0:T(8,128)(2,1)}, bf16[384,192]{1,0:T(8,128)(2,1)S(1)}, u32[]{:S(2)}, u32[]{:S(2)}) collective-permute-start(bf16[384,192]{1,0:T(8,128)(2,1)} %copy.12), channel_id=1, source_target_pairs={{0,1},{1,0},{2,3},{3,2},{4,5},{5,4},{6,7},{7,6},{8,9},{9,8},{10,11... | collective-permute-start | bytes 442376 | tf_op jit(solution)/shard_map/w_core/ppermute | solution.py:27
  2.5 13.3 %collective-permute-start.2 = (bf16[512,1536]{1,0:T(8,128)(2,1)}, bf16[512,1536]{1,0:T(8,128)(2,1)}, u32[]{:S(2)}, u32[]{:S(2)}) collective-permute-start(bf16[512,1536]{1,0:T(8,128)(2,1)} %v0_ref.7), channel_id=1, source_target_pairs={{0,1},{1,0},{2,3},{3,2},{4,5},{5,4},{6,7},{7,6},{8,9},{9,8},{10,11... | collective-permute-start | bytes 4718600 | tf_op jit(solution)/shard_map/core_values/ppermute | solution.py:27
  4.8 23.1 %collective-permute-start.5 = (bf16[4,2,128,256]{3,2,1,0:T(8,128)(2,1)}, bf16[4,2,128,256]{3,2,1,0:T(8,128)(2,1)}, u32[]{:S(2)}, u32[]{:S(2)}) collective-permute-start(bf16[4,2,128,256]{3,2,1,0:T(8,128)(2,1)} %pad_maximum_fusion.6), channel_id=1, source_target_pairs={{0,2},{1,3},{2,0},{3,1},{4,6},{5,7},{6,4},{7,5},{8,10},{9,11},{10,... | collective-permute-start | bytes 1572872 | tf_op jit(solution)/shard_map/kv_y0/ppermute | solution.py:27
  11.3 11.7 %collective-permute-start.3 = (bf16[384,384]{1,0:T(8,128)(2,1)S(1)}, bf16[384,384]{1,0:T(8,128)(2,1)S(1)}, u32[]{:S(2)}, u32[]{:S(2)}) collective-permute-start(bf16[384,384]{1,0:T(8,128)(2,1)S(1)} %pad_maximum_fusion.7), channel_id=1, source_target_pairs={{0,4},{1,5},{2,6},{3,7},{4,8},{5,9},{6,10},{7,11},{8,12},{9,13},{1... | collective-permute-start | bytes 884744 | tf_op jit(solution)/shard_map/w_up/ppermute | solution.py:27
  12.9 15.0 %collective-permute-start.4 = (bf16[384,384]{1,0:T(8,128)(2,1)S(1)}, bf16[384,384]{1,0:T(8,128)(2,1)S(1)}, u32[]{:S(2)}, u32[]{:S(2)}) collective-permute-start(bf16[384,384]{1,0:T(8,128)(2,1)S(1)} %pad_maximum_fusion.7), channel_id=1, source_target_pairs={{0,12},{1,13},{2,14},{3,15},{4,0},{5,1},{6,2},{7,3},{8,4},{9,5},{1... | collective-permute-start | bytes 884744 | tf_op jit(solution)/shard_map/w_down/ppermute | solution.py:27
  15.3 27.6 %collective-permute-start.8 = (bf16[4,2,128,512]{3,2,1,0:T(8,128)(2,1)S(1)}, bf16[4,2,128,512]{3,2,1,0:T(8,128)(2,1)S(1)}, u32[]{:S(2)}, u32[]{:S(2)}) collective-permute-start(bf16[4,2,128,512]{3,2,1,0:T(8,128)(2,1)S(1)} %pad_maximum_fusion.1), channel_id=1, source_target_pairs={{0,2},{1,3},{2,0},{3,1},{4,6},{5,7},{6,4},{7,5},{8,10},{9,11},{10,... | collective-permute-start | bytes 3145736 | tf_op jit(solution)/shard_map/kv_y1/ppermute | solution.py:27
  15.7 49.6 %collective-permute-start.10 = (bf16[4,2,128,512]{3,2,1,0:T(8,128)(2,1)S(1)}, bf16[4,2,128,512]{3,2,1,0:T(8,128)(2,1)S(1)}, u32[]{:S(2)}, u32[]{:S(2)}) collective-permute-start(bf16[4,2,128,512]{3,2,1,0:T(8,128)(2,1)S(1)} %pad_maximum_fusion.2), channel_id=1, source_target_pairs={{0,2},{1,3},{2,0},{3,1},{4,6},{5,7},{6,4},{7,5},{8,10},{9,11},{10,... | collective-permute-start | bytes 3145736 | tf_op jit(solution)/shard_map/kv_y2/ppermute | solution.py:27
  28.0 11.7 %collective-permute-start.6 = (bf16[384,384]{1,0:T(8,128)(2,1)S(1)}, bf16[384,384]{1,0:T(8,128)(2,1)S(1)}, u32[]{:S(2)}, u32[]{:S(2)}) collective-permute-start(bf16[384,384]{1,0:T(8,128)(2,1)S(1)} %collective-permute-done.3), channel_id=1, source_target_pairs={{0,4},{1,5},{2,6},{3,7},{4,8},{5,9},{6,10},{7,11},{8,12},{9,13},{1... | collective-permute-start | bytes 884744 | tf_op jit(solution)/shard_map/w_up2/ppermute | solution.py:27
  29.1 20.2 %collective-permute-start.9 = (bf16[4,2,128,256]{3,2,1,0:T(8,128)(2,1)}, bf16[4,2,128,256]{3,2,1,0:T(8,128)(2,1)S(1)}, u32[]{:S(2)}, u32[]{:S(2)}) collective-permute-start(bf16[4,2,128,256]{3,2,1,0:T(8,128)(2,1)} %collective-permute-done.5.a_ref.b_ref), channel_id=1, source_target_pairs={{0,4},{1,5},{2,14},{3,15},{4,8},{5,9},{6,2},{7,3},{8,12},{9,13},{1... | collective-permute-start | bytes 1572872 | tf_op jit(solution)/shard_map/kv_z0/ppermute | solution.py:27
  40.6 50.7 %collective-permute-start.14 = (bf16[2,384,384]{2,1,0:T(8,128)(2,1)}, bf16[2,384,384]{2,1,0:T(8,128)(2,1)}, u32[]{:S(2)}, u32[]{:S(2)}) collective-permute-start(bf16[2,384,384]{2,1,0:T(8,128)(2,1)} %pad_maximum_fusion.3), channel_id=1, source_target_pairs={{0,2},{1,3},{2,0},{3,1},{4,6},{5,7},{6,4},{7,5},{8,10},{9,11},{10,... | collective-permute-start | bytes 1769480 | tf_op jit(solution)/shard_map/w_yx/ppermute | solution.py:27
  42.9 48.4 %copy-start.3 = (bf16[4,2,128,512]{3,2,1,0:T(8,128)(2,1)}, bf16[4,2,128,512]{3,2,1,0:T(8,128)(2,1)S(1)}, u32[]{:S(2)}) copy-start(bf16[4,2,128,512]{3,2,1,0:T(8,128)(2,1)S(1)} %collective-permute-done.8.a_ref.b_ref) | copy-start | bytes 3145732
  44.3 47.2 %collective-permute-start.15 = (bf16[4,384,384]{2,1,0:T(8,128)(2,1)}, bf16[4,384,384]{2,1,0:T(8,128)(2,1)}, u32[]{:S(2)}, u32[]{:S(2)}) collective-permute-start(bf16[4,384,384]{2,1,0:T(8,128)(2,1)} %pad_maximum_fusion.refs_0_), channel_id=1, source_target_pairs={{0,16},{1,17},{2,18},{3,19},{4,20},{5,21},{6,22},{7,23},{8,24},{9,... | collective-permute-start | bytes 3538952 | tf_op jit(solution)/shard_map/w_x1/ppermute | solution.py:37
  46.2 25.7 %collective-permute-start.11 = (bf16[4,2,128,512]{3,2,1,0:T(8,128)(2,1)S(1)}, bf16[4,2,128,512]{3,2,1,0:T(8,128)(2,1)S(1)}, u32[]{:S(2)}, u32[]{:S(2)}) collective-permute-start(bf16[4,2,128,512]{3,2,1,0:T(8,128)(2,1)S(1)} %collective-permute-done.8.a_ref.b_ref), channel_id=1, source_target_pairs={{0,4},{1,5},{2,14},{3,15},{4,8},{5,9},{6,2},{7,3},{8,12},{9,13},{1... | collective-permute-start | bytes 3145736 | tf_op jit(solution)/shard_map/kv_z1/ppermute | solution.py:27
  49.3 39.9 %collective-permute-start.7 = (bf16[4,2,128,256]{3,2,1,0:T(8,128)(2,1)}, bf16[4,2,128,256]{3,2,1,0:T(8,128)(2,1)S(1)}, u32[]{:S(2)}, u32[]{:S(2)}) collective-permute-start(bf16[4,2,128,256]{3,2,1,0:T(8,128)(2,1)} %pad_maximum_fusion.5), channel_id=1, source_target_pairs={{0,2},{1,3},{2,0},{3,1},{4,6},{5,7},{6,4},{7,5},{8,10},{9,11},{10,... | collective-permute-start | bytes 1572872 | tf_op jit(solution)/shard_map/kv_y3/ppermute | solution.py:27
  65.3 46.7 %copy-start.2 = (bf16[4,2,128,512]{3,2,1,0:T(8,128)(2,1)}, bf16[4,2,128,512]{3,2,1,0:T(8,128)(2,1)S(1)}, u32[]{:S(2)}) copy-start(bf16[4,2,128,512]{3,2,1,0:T(8,128)(2,1)S(1)} %collective-permute-done.10.a_ref.b_ref) | copy-start | bytes 3145732
  65.3 46.8 %collective-permute-start.18 = (bf16[2,384,384]{2,1,0:T(8,128)(2,1)}, bf16[2,384,384]{2,1,0:T(8,128)(2,1)}, u32[]{:S(2)}, u32[]{:S(2)}) collective-permute-start(bf16[2,384,384]{2,1,0:T(8,128)(2,1)} %pad_maximum_fusion.4), channel_id=1, source_target_pairs={{0,2},{1,3},{2,0},{3,1},{4,6},{5,7},{6,4},{7,5},{8,10},{9,11},{10,... | collective-permute-start | bytes 1769480 | tf_op jit(solution)/shard_map/w_yy/ppermute | solution.py:27
  71.9 1.9 %collective-permute-start.12 = (bf16[4,2,128,256]{3,2,1,0:T(8,128)(2,1)S(1)}, bf16[4,2,128,256]{3,2,1,0:T(8,128)(2,1)S(1)}, u32[]{:S(2)}, u32[]{:S(2)}) collective-permute-start(bf16[4,2,128,256]{3,2,1,0:T(8,128)(2,1)S(1)} %broadcast_select_fusion.3), channel_id=1, source_target_pairs={{0,1},{1,0},{2,3},{3,2},{4,5},{5,4},{6,7},{7,6},{8,9},{9,8},{10,11... | collective-permute-start | bytes 1572872 | tf_op jit(solution)/shard_map/kv_g0/ppermute | solution.py:27
  74.6 27.9 %collective-permute-start.16 = (bf16[4,2,128,512]{3,2,1,0:T(8,128)(2,1)S(1)}, bf16[4,2,128,512]{3,2,1,0:T(8,128)(2,1)}, u32[]{:S(2)}, u32[]{:S(2)}) collective-permute-start(bf16[4,2,128,512]{3,2,1,0:T(8,128)(2,1)S(1)} %collective-permute-done.10.a_ref.b_ref), channel_id=1, source_target_pairs={{0,4},{1,5},{2,14},{3,15},{4,8},{5,9},{6,2},{7,3},{8,12},{9,13},{1... | collective-permute-start | bytes 3145736 | tf_op jit(solution)/shard_map/kv_z2/ppermute | solution.py:27
  89.2 36.5 %copy-start.5 = (bf16[4,2,128,256]{3,2,1,0:T(8,128)(2,1)}, bf16[4,2,128,256]{3,2,1,0:T(8,128)(2,1)S(1)}, u32[]{:S(2)}) copy-start(bf16[4,2,128,256]{3,2,1,0:T(8,128)(2,1)S(1)} %collective-permute-done.7.a_ref.b_ref) | copy-start | bytes 1572868
  89.2 36.5 %collective-permute-start.13 = (bf16[4,2,128,256]{3,2,1,0:T(8,128)(2,1)S(1)}, bf16[4,2,128,256]{3,2,1,0:T(8,128)(2,1)}, u32[]{:S(2)}, u32[]{:S(2)}) collective-permute-start(bf16[4,2,128,256]{3,2,1,0:T(8,128)(2,1)S(1)} %collective-permute-done.7.a_ref.b_ref), channel_id=1, source_target_pairs={{0,4},{1,5},{2,14},{3,15},{4,8},{5,9},{6,2},{7,3},{8,12},{9,13},{1... | collective-permute-start | bytes 1572872 | tf_op jit(solution)/shard_map/kv_z3/ppermute | solution.py:27
  91.4 11.1 %collective-permute-start.17 = (bf16[4,2,128,512]{3,2,1,0:T(8,128)(2,1)S(1)}, bf16[4,2,128,512]{3,2,1,0:T(8,128)(2,1)}, u32[]{:S(2)}, u32[]{:S(2)}) collective-permute-start(bf16[4,2,128,512]{3,2,1,0:T(8,128)(2,1)S(1)} %broadcast_select_fusion.1), channel_id=1, source_target_pairs={{0,1},{1,0},{2,3},{3,2},{4,5},{5,4},{6,7},{7,6},{8,9},{9,8},{10,11... | collective-permute-start | bytes 3145736 | tf_op jit(solution)/shard_map/kv_g1/ppermute | solution.py:27
  91.5 22.0 %collective-permute-start.19 = (bf16[2,384,384]{2,1,0:T(8,128)(2,1)}, bf16[2,384,384]{2,1,0:T(8,128)(2,1)S(1)}, u32[]{:S(2)}, u32[]{:S(2)}) collective-permute-start(bf16[2,384,384]{2,1,0:T(8,128)(2,1)} %collective-permute-done.14.refs_4_), channel_id=1, source_target_pairs={{0,16},{1,17},{2,18},{3,19},{4,20},{5,21},{6,22},{7,23},{8,24},{9,... | collective-permute-start | bytes 1769480 | tf_op jit(solution)/shard_map/w_x2x/ppermute | solution.py:37
  102.5 33.7 %collective-permute-start.23 = (bf16[4,384,384]{2,1,0:T(8,128)(2,1)}, bf16[4,384,384]{2,1,0:T(8,128)(2,1)S(1)}, u32[]{:S(2)}, u32[]{:S(2)}) collective-permute-start(bf16[4,384,384]{2,1,0:T(8,128)(2,1)} %collective-permute-done.15.refs_1_), channel_id=1, source_target_pairs={{0,1},{1,0},{2,3},{3,2},{4,5},{5,4},{6,7},{7,6},{8,9},{9,8},{10,11... | collective-permute-start | bytes 3538952 | tf_op jit(solution)/shard_map/w_d1/ppermute | solution.py:27
  102.5 26.6 %collective-permute-start.22 = (bf16[4,384,384]{2,1,0:T(8,128)(2,1)}, bf16[4,384,384]{2,1,0:T(8,128)(2,1)}, u32[]{:S(2)}, u32[]{:S(2)}) collective-permute-start(bf16[4,384,384]{2,1,0:T(8,128)(2,1)} %pad_maximum_fusion.refs_0_), channel_id=1, source_target_pairs={{0,1},{1,0},{2,3},{3,2},{4,5},{5,4},{6,7},{7,6},{8,9},{9,8},{10,11... | collective-permute-start | bytes 3538952 | tf_op jit(solution)/shard_map/w_c1/ppermute | solution.py:27
  112.2 3.6 %collective-permute-start.20 = (bf16[4,2,128,512]{3,2,1,0:T(8,128)(2,1)S(1)}, bf16[4,2,128,512]{3,2,1,0:T(8,128)(2,1)S(1)}, u32[]{:S(2)}, u32[]{:S(2)}) collective-permute-start(bf16[4,2,128,512]{3,2,1,0:T(8,128)(2,1)S(1)} %broadcast_select_fusion), channel_id=1, source_target_pairs={{0,1},{1,0},{2,3},{3,2},{4,5},{5,4},{6,7},{7,6},{8,9},{9,8},{10,11... | collective-permute-start | bytes 3145736 | tf_op jit(solution)/shard_map/kv_g2/ppermute | solution.py:27
  113.5 15.6 %collective-permute-start.26 = (bf16[2,384,384]{2,1,0:T(8,128)(2,1)}, bf16[2,384,384]{2,1,0:T(8,128)(2,1)}, u32[]{:S(2)}, u32[]{:S(2)}) collective-permute-start(bf16[2,384,384]{2,1,0:T(8,128)(2,1)} %collective-permute-done.18.refs_8_), channel_id=1, source_target_pairs={{0,16},{1,17},{2,18},{3,19},{4,20},{5,21},{6,22},{7,23},{8,24},{9,... | collective-permute-start | bytes 1769480 | tf_op jit(solution)/shard_map/w_x2y/ppermute | solution.py:37
  125.8 3.8 %collective-permute-start.21 = (bf16[4,2,128,256]{3,2,1,0:T(8,128)(2,1)S(1)}, bf16[4,2,128,256]{3,2,1,0:T(8,128)(2,1)}, u32[]{:S(2)}, u32[]{:S(2)}) collective-permute-start(bf16[4,2,128,256]{3,2,1,0:T(8,128)(2,1)S(1)} %broadcast_select_fusion.2), channel_id=1, source_target_pairs={{0,1},{1,0},{2,3},{3,2},{4,5},{5,4},{6,7},{7,6},{8,9},{9,8},{10,11... | collective-permute-start | bytes 1572872 | tf_op jit(solution)/shard_map/kv_g3/ppermute | solution.py:27
  127.3 8.9 %collective-permute-start.24 = (bf16[2,384,384]{2,1,0:T(8,128)(2,1)}, bf16[2,384,384]{2,1,0:T(8,128)(2,1)S(1)}, u32[]{:S(2)}, u32[]{:S(2)}) collective-permute-start(bf16[2,384,384]{2,1,0:T(8,128)(2,1)} %collective-permute-done.14.refs_4_), channel_id=1, source_target_pairs={{0,1},{1,0},{2,3},{3,2},{4,5},{5,4},{6,7},{7,6},{8,9},{9,8},{10,11... | collective-permute-start | bytes 1769480 | tf_op jit(solution)/shard_map/w_c2x/ppermute | solution.py:27
  129.1 7.1 %collective-permute-start.25 = (bf16[2,384,384]{2,1,0:T(8,128)(2,1)S(1)}, bf16[2,384,384]{2,1,0:T(8,128)(2,1)S(1)}, u32[]{:S(2)}, u32[]{:S(2)}) collective-permute-start(bf16[2,384,384]{2,1,0:T(8,128)(2,1)S(1)} %collective-permute-done.19.refs_5_), channel_id=1, source_target_pairs={{0,1},{1,0},{2,3},{3,2},{4,5},{5,4},{6,7},{7,6},{8,9},{9,8},{10,11... | collective-permute-start | bytes 1769480 | tf_op jit(solution)/shard_map/w_d2x/ppermute | solution.py:27
  129.1 7.1 %collective-permute-start.28 = (bf16[2,384,384]{2,1,0:T(8,128)(2,1)}, bf16[2,384,384]{2,1,0:T(8,128)(2,1)}, u32[]{:S(2)}, u32[]{:S(2)}) collective-permute-start(bf16[2,384,384]{2,1,0:T(8,128)(2,1)} %collective-permute-done.26.refs_9_), channel_id=1, source_target_pairs={{0,1},{1,0},{2,3},{3,2},{4,5},{5,4},{6,7},{7,6},{8,9},{9,8},{10,11... | collective-permute-start | bytes 1769480 | tf_op jit(solution)/shard_map/w_d2y/ppermute | solution.py:27
  129.6 6.6 %collective-permute-start.27 = (bf16[2,384,384]{2,1,0:T(8,128)(2,1)}, bf16[2,384,384]{2,1,0:T(8,128)(2,1)}, u32[]{:S(2)}, u32[]{:S(2)}) collective-permute-start(bf16[2,384,384]{2,1,0:T(8,128)(2,1)} %collective-permute-done.18.refs_8_), channel_id=1, source_target_pairs={{0,1},{1,0},{2,3},{3,2},{4,5},{5,4},{6,7},{7,6},{8,9},{9,8},{10,11... | collective-permute-start | bytes 1769480 | tf_op jit(solution)/shard_map/w_c2y/ppermute | solution.py:27
  (11 other events, 74.6 us)

commit v4 on v2

--- a/solution.py
+++ b/solution.py
@@ -122,56 +122,75 @@
     )(place, block_mask)
 
 
+PAIR = 2
+
+
 def attend_kernel(
     picks_ref, q_ref, k0_ref, v0_ref, k1_ref, v1_ref, near_ref, a_ref, b_ref, c_ref, d_ref, bias_ref, *rest
 ):
     o_ref = rest[-1]
-    rows, size = q_ref.shape
+    rows, size = q_ref.shape[0], q_ref.shape[1] // PAIR
     per = near_ref.shape[0]
     span = per * BLOCK
-    near = near_ref[...]
     far = (a_ref, b_ref, c_ref, d_ref)
-    keys = [
-        k0_ref[...],
-        k1_ref[...],
-        near[:, 0].reshape(span, size),
-        jnp.concatenate([r[0, 0] for r in far], axis=0),
-    ]
-    values = [
-        v0_ref[...],
-        v1_ref[...],
-        near[:, 1].reshape(span, size),
-        jnp.concatenate([r[0, 1] for r in far], axis=0),
-    ]
     factor = math.log2(math.e) / math.sqrt(size)
     ones = jnp.ones((span, size), jnp.bfloat16)
-    values = [jnp.concatenate([v, ones], axis=1) for v in values]
-    for m in range(rows // BLOCK):
-        mine = slice(m * BLOCK, (m + 1) * BLOCK)
-        q = q_ref[mine, :]
+    keys, values = [], []
+    for head in range(PAIR):
+        cols = slice(head * size, (head + 1) * size)
+        near = near_ref[:, :, :, cols]
+        keys.append([
+            k0_ref[:, cols],
+            k1_ref[:, cols],
+            near[:, 0].reshape(span, size),
+            jnp.concatenate([r[0, 0, :, cols] for r in far], axis=0),
+        ])
+        own = [
+            v0_ref[:, cols],
+            v1_ref[:, cols],
+            near[:, 1].reshape(span, size),
+            jnp.concatenate([r[0, 1, :, cols] for r in far], axis=0),
+        ]
+        values.append([jnp.concatenate([v, ones], axis=1) for v in own])
+
+    def scores_of(head, m):
+        q = q_ref[m * BLOCK : (m + 1) * BLOCK, head * size : (head + 1) * size]
         scores, top = [], None
-        for n, k in enumerate(keys):
+        for n, k in enumerate(keys[head]):
             s = lax.dot_general(q, k, (((1,), (1,)), ((), ())), preferred_element_type=jnp.float32)
             if n:
                 s = s + bias_ref[m, :, (n - 1) * span : n * span]
             scores.append(s)
             t = jnp.max(s, axis=1, keepdims=True)
             top = t if top is None else jnp.maximum(top, t)
+        return scores, top
+
+    def finish(head, m, scores, top):
         total = None
-        for s, v in zip(scores, values):
+        for s, v in zip(scores, values[head]):
             w = jnp.exp2((s - top) * factor).astype(jnp.bfloat16)
             part = jnp.dot(w, v, preferred_element_type=jnp.float32)
             total = part if total is None else total + part
-        o_ref[mine, :] = (total[:, :size] / total[:, size:]).astype(o_ref.dtype)
+        o_ref[m * BLOCK : (m + 1) * BLOCK, head * size : (head + 1) * size] = (
+            total[:, :size] / total[:, size:]
+        ).astype(o_ref.dtype)
+
+    blocks = [(head, m) for head in range(PAIR) for m in range(rows // BLOCK)]
+    held = scores_of(*blocks[0])
+    for block, following in zip(blocks, blocks[1:]):
+        ahead = scores_of(*following)
+        finish(*block, *held)
+        held = ahead
+    finish(*blocks[-1], *held)
 
 
 def attend(first_head, per_part, picks, queries, key_rows, value_rows, core_k, core_v, near, y, z, bias, into):
     rows, width = queries.shape
-    size = width // HEADS
+    wide = width // HEADS * PAIR
     per = near.shape[0]
-    flat = pl.BlockSpec((rows, size), lambda h, p: (0, first_head + h))
+    flat = pl.BlockSpec((rows, wide), lambda h, p: (0, first_head // PAIR + h))
     far = [
-        pl.BlockSpec((1, 2, BLOCK, size), lambda h, p, n=n: (p[n], 0, 0, h)) for n in range(4)
+        pl.BlockSpec((1, 2, BLOCK, wide), lambda h, p, n=n: (p[n], 0, 0, h)) for n in range(4)
     ]
     in_specs = [
         flat,
@@ -179,7 +198,7 @@
         flat,
         flat,
         flat,
-        pl.BlockSpec((per, 2, BLOCK, size), lambda h, p: (0, 0, 0, h)),
+        pl.BlockSpec((per, 2, BLOCK, wide), lambda h, p: (0, 0, 0, h)),
         *far,
         pl.BlockSpec(bias.shape, lambda h, p: (0, 0, 0)),
     ]
@@ -193,7 +212,7 @@
         attend_kernel,
         grid_spec=pltpu.PrefetchScalarGridSpec(
             num_scalar_prefetch=1,
-            grid=(per_part,),
+            grid=(per_part // PAIR,),
             in_specs=in_specs,
             out_specs=flat,
         ),
@@ -208,48 +227,86 @@
 
 
 def project_kernel(place_ref, att_ref, *refs):
-    *pieces, o_ref, held_ref = refs
-    _, depth, cols = pieces[0].shape
-    step = pl.program_id(0)
-
-    @pl.when(step == 0)
-    def _():
-        for n in range(4):
-            first = pl.multiple_of(place_ref[n] * depth, depth)
-            held_ref[:, n * depth : (n + 1) * depth] = att_ref[:, pl.ds(first, depth)]
-
-    def fill(half):
-        own = jnp.concatenate([pieces[n][0] for n in range(4)], axis=0)
-        other = jnp.concatenate([pieces[4 + 4 * half + n][0] for n in range(4)], axis=0)
-        total = jnp.dot(
-            held_ref[...], jnp.concatenate([own, other], axis=1), preferred_element_type=jnp.float32
-        ).astype(o_ref.dtype)
-        for f in range(2):
-            to = pl.multiple_of(place_ref[4 + f] * cols, cols)
-            o_ref[:, pl.ds(to, cols)] = total[:, f * cols : (f + 1) * cols]
-
-    pl.when(step < 2)(lambda: fill(0))
-    pl.when(step >= 2)(lambda: fill(1))
+    *pieces, o_ref, held_ref, w_ref, out_ref, att_sems, w_sems, out_sems = refs
+    shifts, _, wide = w_ref.shape
+    depth, cols = held_ref.shape[1] // 4, wide // 2
+    ahead = 1
+
+    def source(shift, flip, quarter):
+        if flip == 0:
+            return pieces[quarter].at[shift]
+        return pieces[4 + 4 * (shift // 2) + quarter].at[shift % 2]
+
+    att_copies = [
+        pltpu.make_async_copy(
+            att_ref.at[:, pl.ds(pl.multiple_of(place_ref[n] * depth, depth), depth)],
+            held_ref.at[:, pl.ds(n * depth, depth)],
+            att_sems.at[n],
+        )
+        for n in range(4)
+    ]
+    w_copies = [
+        [
+            pltpu.make_async_copy(
+                source(shift, flip, n),
+                w_ref.at[shift, pl.ds(n * depth, depth), pl.ds(flip * cols, cols)],
+                w_sems.at[shift, flip * 4 + n],
+            )
+            for flip in range(2)
+            for n in range(4)
+        ]
+        for shift in range(shifts)
+    ]
+    for copy in att_copies:
+        copy.start()
+    for copies in w_copies[:ahead]:
+        for copy in copies:
+            copy.start()
+    for copy in att_copies:
+        copy.wait()
+    out_copies = []
+    for shift in range(shifts):
+        for copy in w_copies[shift]:
+            copy.wait()
+        if shift + ahead < shifts:
+            for copy in w_copies[shift + ahead]:
+                copy.start()
+        half = held_ref.shape[0] // 2
+        for m in range(2):
+            mine = slice(m * half, (m + 1) * half)
+            out_ref[shift, mine, :] = jnp.dot(
+                held_ref[mine, :], w_ref[shift], preferred_element_type=jnp.float32
+            ).astype(o_ref.dtype)
+        for flip in range(2):
+            to = pl.multiple_of((place_ref[6 + shift] * 2 + place_ref[4 + flip]) * cols, cols)
+            copy = pltpu.make_async_copy(
+                out_ref.at[shift, :, pl.ds(flip * cols, cols)],
+                o_ref.at[:, pl.ds(to, cols)],
+                out_sems.at[shift, flip],
+            )
+            copy.start()
+            out_copies.append(copy)
+    for copy in out_copies:
+        copy.wait()
 
 
 def project(places, attention, whole, halves):
     rows, width = attention.shape
     shifts, depth, cols = whole[0].shape
-    size = (1, depth, cols)
-    in_specs = [pl.BlockSpec((rows, width), lambda g, p: (0, 0))]
-    in_specs += [pl.BlockSpec(size, lambda g, p: (g, 0, 0))] * 4
-    in_specs += [pl.BlockSpec(size, lambda g, p: (jnp.minimum(g, 1), 0, 0))] * 4
-    in_specs += [pl.BlockSpec(size, lambda g, p: (jnp.maximum(g - 2, 0), 0, 0))] * 4
+    anywhere = pl.BlockSpec(memory_space=pl.ANY)
     return pl.pallas_call(
         project_kernel,
-        grid_spec=pltpu.PrefetchScalarGridSpec(
-            num_scalar_prefetch=1,
-            grid=(shifts,),
-            in_specs=in_specs,
-            out_specs=pl.BlockSpec((rows, 2 * cols), lambda g, p: (0, p[6 + g])),
-            scratch_shapes=[pltpu.VMEM((rows, width), jnp.bfloat16)],
-        ),
+        in_specs=[pl.BlockSpec(memory_space=pltpu.SMEM)] + [anywhere] * 13,
+        out_specs=anywhere,
         out_shape=jax.ShapeDtypeStruct((rows, shifts * 2 * cols), jnp.bfloat16),
+        scratch_shapes=[
+            pltpu.VMEM((rows, width), jnp.bfloat16),
+            pltpu.VMEM((shifts, width, 2 * cols), jnp.bfloat16),
+            pltpu.VMEM((shifts, rows, 2 * cols), jnp.bfloat16),
+            pltpu.SemaphoreType.DMA((4,)),
+            pltpu.SemaphoreType.DMA((shifts, 8)),
+            pltpu.SemaphoreType.DMA((shifts, 2)),
+        ],
         compiler_params=pltpu.CompilerParams(vmem_limit_bytes=VMEM_LIMIT),
         cost_estimate=CHEAP,
         name="project",

time: 151 us -> 148 us (0.980)
  Pallas kernels: 44.8 us -> 40.4 us
  waiting for transfers between devices: 61.1 us -> 62.7 us
    pallas_call x4, Pallas kernels: 32.5 us -> 28.7 us  [attend(): pl.pallas_call(attend_kernel, grid_spec=pltpu.PrefetchScalarGridSpec(num_...]
  transfers between devices with their start and end apart: 29 -> 29, of which waited for: 13 -> 12; matrix products, arithmetic and copies ran while one was open for 8% -> 8% of each run, Pallas kernels for 23% -> 20%
where the time goes in v4:
time: 148 us
  waiting for transfers between devices  62.7 us (42%)
  Pallas kernels  40.4 us (27%)
  starting transfers between devices  29.4 us (20%)
  local copies, waits for them, and re-layouts  7.82 us (5%)
  other arithmetic  6.76 us (5%)
    ppermute x26, waiting for transfers between devices, moved(): return lax.ppermute(value, 'blk', [(s, dest(s)) for s in range(count)])  60.7 us
    pallas_call x4, Pallas kernels, attend(): pl.pallas_call(attend_kernel, grid_spec=pltpu.PrefetchScalarGridSpec(num_...  28.7 us
    ppermute x26, starting transfers between devices, moved(): return lax.ppermute(value, 'blk', [(s, dest(s)) for s in range(count)])  24.5 us
    pallas_call x1, Pallas kernels, project(): pl.pallas_call(project_kernel, in_specs=[pl.BlockSpec(memory_space=pltpu....  10.2 us
    ppermute x3, starting transfers between devices, moved_all(): return lax.ppermute(value, ('groups', 'blk'), pairs)  4.94 us
    unnamed x30, local copies, waits for them, and re-layouts  4.09 us
  transfers between devices with their start and end apart: 29, of which 12 were waited for; matrix products, arithmetic and copies ran while one was open for 8% of the time, Pallas kernels for 20%

profile of v4, /device:TPU:0, one launch (start us, length us, event | category | flops | bytes accessed | tf_op | source)
XLA Modules:
  0.0 147.5 jit_solution(2760479052905742230)
XLA Ops:
  4.8 2.6 %collective-permute-start.5 = (bf16[4,2,128,256]{3,2,1,0:T(8,128)(2,1)}, bf16[4,2,128,256]{3,2,1,0:T(8,128)(2,1)}, u32[]{:S(2)}, u32[]{:S(2)}) collective-permute-start(bf16[4,2,128,256]{3,2,1,0:T(8,128)(2,1)} %pad_maximum_fusion.6), channel_id=1, source_target_pairs={{0,2},{1,3},{2,0},{3,1},{4,6},{5,7},{6,4},{7,5},{8,10},{9,11},{10,... | collective-permute-start | bytes 1572872 | tf_op jit(solution)/shard_map/kv_y0/ppermute | solution.py:27
  9.4 1.4 plan.1
  11.3 1.6 %collective-permute-start.3 = (bf16[384,384]{1,0:T(8,128)(2,1)S(1)}, bf16[384,384]{1,0:T(8,128)(2,1)S(1)}, u32[]{:S(2)}, u32[]{:S(2)}) collective-permute-start(bf16[384,384]{1,0:T(8,128)(2,1)S(1)} %pad_maximum_fusion.7), channel_id=1, source_target_pairs={{0,4},{1,5},{2,6},{3,7},{4,8},{5,9},{6,10},{7,11},{8,12},{9,13},{1... | collective-permute-start | bytes 884744 | tf_op jit(solution)/shard_map/w_up/ppermute | solution.py:27
  12.9 2.2 %collective-permute-start.4 = (bf16[384,384]{1,0:T(8,128)(2,1)S(1)}, bf16[384,384]{1,0:T(8,128)(2,1)S(1)}, u32[]{:S(2)}, u32[]{:S(2)}) collective-permute-start(bf16[384,384]{1,0:T(8,128)(2,1)S(1)} %pad_maximum_fusion.7), channel_id=1, source_target_pairs={{0,12},{1,13},{2,14},{3,15},{4,0},{5,1},{6,2},{7,3},{8,4},{9,5},{1... | collective-permute-start | bytes 884744 | tf_op jit(solution)/shard_map/w_down/ppermute | solution.py:27
  15.7 1.7 %collective-permute-start.10 = (bf16[4,2,128,512]{3,2,1,0:T(8,128)(2,1)S(1)}, bf16[4,2,128,512]{3,2,1,0:T(8,128)(2,1)S(1)}, u32[]{:S(2)}, u32[]{:S(2)}) collective-permute-start(bf16[4,2,128,512]{3,2,1,0:T(8,128)(2,1)S(1)} %pad_maximum_fusion.2), channel_id=1, source_target_pairs={{0,2},{1,3},{2,0},{3,1},{4,6},{5,7},{6,4},{7,5},{8,10},{9,11},{10,... | collective-permute-start | bytes 3145736 | tf_op jit(solution)/shard_map/kv_y2/ppermute | solution.py:27
  17.4 5.6 %collective-permute-done.3 = bf16[384,384]{1,0:T(8,128)(2,1)S(1)} collective-permute-done((bf16[384,384]{1,0:T(8,128)(2,1)S(1)}, bf16[384,384]{1,0:T(8,128)(2,1)S(1)}, u32[]{:S(2)}, u32[]{:S(2)}) %collective-permute-start.3) | collective-permute-done | bytes 294944 | tf_op jit(solution)/shard_map/w_up/ppermute | solution.py:27
  23.0 4.9 %collective-permute-done.4 = bf16[384,384]{1,0:T(8,128)(2,1)S(1)} collective-permute-done((bf16[384,384]{1,0:T(8,128)(2,1)S(1)}, bf16[384,384]{1,0:T(8,128)(2,1)S(1)}, u32[]{:S(2)}, u32[]{:S(2)}) %collective-permute-start.4) | collective-permute-done | bytes 294944 | tf_op jit(solution)/shard_map/w_down/ppermute | solution.py:27
  28.0 1.1 collective-permute-start.6
  29.8 9.9 %collective-permute-done.6 = bf16[384,384]{1,0:T(8,128)(2,1)S(1)} collective-permute-done((bf16[384,384]{1,0:T(8,128)(2,1)S(1)}, bf16[384,384]{1,0:T(8,128)(2,1)S(1)}, u32[]{:S(2)}, u32[]{:S(2)}) %collective-permute-start.6) | collective-permute-done | bytes 294944 | tf_op jit(solution)/shard_map/w_up2/ppermute | solution.py:27
  41.1 1.8 %collective-permute-done.8.a_ref.b_ref = bf16[4,2,128,512]{3,2,1,0:T(8,128)(2,1)S(1)} collective-permute-done((bf16[4,2,128,512]{3,2,1,0:T(8,128)(2,1)S(1)}, bf16[4,2,128,512]{3,2,1,0:T(8,128)(2,1)S(1)}, u32[]{:S(2)}, u32[]{:S(2)}) %collective-permute-start.8) | collective-permute-done | bytes 1048608 | tf_op jit(solution)/shard_map/kv_y1/ppermute | solution.py:27
  42.9 1.4 pad_maximum_fusion.refs_0_
  44.3 2.0 %collective-permute-start.15 = (bf16[4,384,384]{2,1,0:T(8,128)(2,1)}, bf16[4,384,384]{2,1,0:T(8,128)(2,1)}, u32[]{:S(2)}, u32[]{:S(2)}) collective-permute-start(bf16[4,384,384]{2,1,0:T(8,128)(2,1)} %pad_maximum_fusion.refs_0_), channel_id=1, source_target_pairs={{0,16},{1,17},{2,18},{3,19},{4,20},{5,21},{6,22},{7,23},{8,24},{9,... | collective-permute-start | bytes 3538952 | tf_op jit(solution)/shard_map/w_x1/ppermute | solution.py:37
  46.2 1.6 %collective-permute-start.11 = (bf16[4,2,128,512]{3,2,1,0:T(8,128)(2,1)S(1)}, bf16[4,2,128,512]{3,2,1,0:T(8,128)(2,1)S(1)}, u32[]{:S(2)}, u32[]{:S(2)}) collective-permute-start(bf16[4,2,128,512]{3,2,1,0:T(8,128)(2,1)S(1)} %collective-permute-done.8.a_ref.b_ref), channel_id=1, source_target_pairs={{0,4},{1,5},{2,14},{3,15},{4,8},{5,9},{6,2},{7,3},{8,12},{9,13},{1... | collective-permute-start | bytes 3145736 | tf_op jit(solution)/shard_map/kv_z1/ppermute | solution.py:27
  49.3 2.9 %collective-permute-start.7 = (bf16[4,2,128,256]{3,2,1,0:T(8,128)(2,1)}, bf16[4,2,128,256]{3,2,1,0:T(8,128)(2,1)S(1)}, u32[]{:S(2)}, u32[]{:S(2)}) collective-permute-start(bf16[4,2,128,256]{3,2,1,0:T(8,128)(2,1)} %pad_maximum_fusion.5), channel_id=1, source_target_pairs={{0,2},{1,3},{2,0},{3,1},{4,6},{5,7},{6,4},{7,5},{8,10},{9,11},{10,... | collective-permute-start | bytes 1572872 | tf_op jit(solution)/shard_map/kv_y3/ppermute | solution.py:27
  52.2 13.1 %collective-permute-done.10.a_ref.b_ref = bf16[4,2,128,512]{3,2,1,0:T(8,128)(2,1)S(1)} collective-permute-done((bf16[4,2,128,512]{3,2,1,0:T(8,128)(2,1)S(1)}, bf16[4,2,128,512]{3,2,1,0:T(8,128)(2,1)S(1)}, u32[]{:S(2)}, u32[]{:S(2)}) %collective-permute-start.10) | collective-permute-done | bytes 1048608 | tf_op jit(solution)/shard_map/kv_y2/ppermute | solution.py:27
  65.3 2.0 %collective-permute-start.18 = (bf16[2,384,384]{2,1,0:T(8,128)(2,1)}, bf16[2,384,384]{2,1,0:T(8,128)(2,1)}, u32[]{:S(2)}, u32[]{:S(2)}) collective-permute-start(bf16[2,384,384]{2,1,0:T(8,128)(2,1)} %pad_maximum_fusion.4), channel_id=1, source_target_pairs={{0,2},{1,3},{2,0},{3,1},{4,6},{5,7},{6,4},{7,5},{8,10},{9,11},{10,... | collective-permute-start | bytes 1769480 | tf_op jit(solution)/shard_map/w_yy/ppermute | solution.py:27
  67.3 1.1 broadcast_select_fusion.3
  68.4 3.4 %collective-permute-done.11.c_ref.d_ref = bf16[4,2,128,512]{3,2,1,0:T(8,128)(2,1)S(1)} collective-permute-done((bf16[4,2,128,512]{3,2,1,0:T(8,128)(2,1)S(1)}, bf16[4,2,128,512]{3,2,1,0:T(8,128)(2,1)S(1)}, u32[]{:S(2)}, u32[]{:S(2)}) %collective-permute-start.11) | collective-permute-done | bytes 1048608 | tf_op jit(solution)/shard_map/kv_z1/ppermute | solution.py:27
  71.9 1.9 %collective-permute-done.12.near_ref = bf16[4,2,128,256]{3,2,1,0:T(8,128)(2,1)S(1)} collective-permute-done((bf16[4,2,128,256]{3,2,1,0:T(8,128)(2,1)S(1)}, bf16[4,2,128,256]{3,2,1,0:T(8,128)(2,1)S(1)}, u32[]{:S(2)}, u32[]{:S(2)}) %collective-permute-start.12) | collective-permute-done | bytes 524320 | tf_op jit(solution)/shard_map/kv_g0/ppermute | solution.py:27
  74.6 5.6 %attend.4.rest_0_ = bf16[512,1536]{1,0:T(8,128)(2,1)} custom-call(s32[4]{0:T(128)} %get-tuple-element.52.picks_ref, bf16[512,1536]{1,0:T(8,128)(2,1)} %q_ref.7, bf16[512,1536]{1,0:T(8,128)(2,1)} %k0_ref.7, bf16[512,1536]{1,0:T(8,128)(2,1)} %v0_ref.7, bf16[512,1536]{1,0:T(8,128)(2,1)} %collective-permute-done.k1_ref, ...), custom_call_target="tpu_custom_call" | custom-call | flops 666666688 | bytes 1000 | tf_op jit(solution)/shard_map/attend/pallas_call | solution.py:211
  80.2 9.0 %collective-permute-done.7.a_ref.b_ref = bf16[4,2,128,256]{3,2,1,0:T(8,128)(2,1)S(1)} collective-permute-done((bf16[4,2,128,256]{3,2,1,0:T(8,128)(2,1)}, bf16[4,2,128,256]{3,2,1,0:T(8,128)(2,1)S(1)}, u32[]{:S(2)}, u32[]{:S(2)}) %collective-permute-start.7) | collective-permute-done | bytes 524320 | tf_op jit(solution)/shard_map/kv_y3/ppermute | solution.py:27
  89.2 2.0 %collective-permute-start.13 = (bf16[4,2,128,256]{3,2,1,0:T(8,128)(2,1)S(1)}, bf16[4,2,128,256]{3,2,1,0:T(8,128)(2,1)}, u32[]{:S(2)}, u32[]{:S(2)}) collective-permute-start(bf16[4,2,128,256]{3,2,1,0:T(8,128)(2,1)S(1)} %collective-permute-done.7.a_ref.b_ref), channel_id=1, source_target_pairs={{0,4},{1,5},{2,14},{3,15},{4,8},{5,9},{6,2},{7,3},{8,12},{9,13},{1... | collective-permute-start | bytes 1572872 | tf_op jit(solution)/shard_map/kv_z3/ppermute | solution.py:27
  91.5 1.6 %collective-permute-start.19 = (bf16[2,384,384]{2,1,0:T(8,128)(2,1)}, bf16[2,384,384]{2,1,0:T(8,128)(2,1)S(1)}, u32[]{:S(2)}, u32[]{:S(2)}) collective-permute-start(bf16[2,384,384]{2,1,0:T(8,128)(2,1)} %collective-permute-done.14.refs_4_), channel_id=1, source_target_pairs={{0,16},{1,17},{2,18},{3,19},{4,20},{5,21},{6,22},{7,23},{8,24},{9,... | collective-permute-start | bytes 1769480 | tf_op jit(solution)/shard_map/w_x2x/ppermute | solution.py:37
  93.0 9.4 %collective-permute-done.16.c_ref.d_ref = bf16[4,2,128,512]{3,2,1,0:T(8,128)(2,1)} collective-permute-done((bf16[4,2,128,512]{3,2,1,0:T(8,128)(2,1)S(1)}, bf16[4,2,128,512]{3,2,1,0:T(8,128)(2,1)}, u32[]{:S(2)}, u32[]{:S(2)}) %collective-permute-start.16) | collective-permute-done | bytes 1048608 | tf_op jit(solution)/shard_map/kv_z2/ppermute | solution.py:27
  103.0 8.8 %attend.5.rest_0_ = bf16[512,1536]{1,0:T(8,128)(2,1)} custom-call(s32[4]{0:T(128)} %get-tuple-element.52.picks_ref, bf16[512,1536]{1,0:T(8,128)(2,1)} %q_ref.7, bf16[512,1536]{1,0:T(8,128)(2,1)} %k0_ref.7, bf16[512,1536]{1,0:T(8,128)(2,1)} %v0_ref.7, bf16[512,1536]{1,0:T(8,128)(2,1)} %collective-permute-done.k1_ref, ...), custom_call_target="tpu_custom_call", output_to_operand_aliasing={{}: (12, {})} | custom-call | flops 1333333376 | bytes 1000 | tf_op jit(solution)/shard_map/attend/pallas_call | solution.py:211
  111.9 1.3 collective-permute-start.20
  113.3 1.4 collective-permute-start.26
  116.5 8.7 %attend.6.rest_0_ = bf16[512,1536]{1,0:T(8,128)(2,1)} custom-call(s32[4]{0:T(128)} %get-tuple-element.52.picks_ref, bf16[512,1536]{1,0:T(8,128)(2,1)} %q_ref.7, bf16[512,1536]{1,0:T(8,128)(2,1)} %k0_ref.7, bf16[512,1536]{1,0:T(8,128)(2,1)} %v0_ref.7, bf16[512,1536]{1,0:T(8,128)(2,1)} %collective-permute-done.k1_ref, ...), custom_call_target="tpu_custom_call", output_to_operand_aliasing={{}: (12, {})} | custom-call | flops 1333333376 | bytes 1000 | tf_op jit(solution)/shard_map/attend/pallas_call | solution.py:211
  125.3 1.4 collective-permute-start.21
  126.9 2.0 %collective-permute-done.26.refs_9_ = bf16[2,384,384]{2,1,0:T(8,128)(2,1)} collective-permute-done((bf16[2,384,384]{2,1,0:T(8,128)(2,1)}, bf16[2,384,384]{2,1,0:T(8,128)(2,1)}, u32[]{:S(2)}, u32[]{:S(2)}) %collective-permute-start.26) | collective-permute-done | bytes 589856 | tf_op jit(solution)/shard_map/w_x2y/ppermute | solution.py:37
  130.1 5.6 %attend.7.att_ref = bf16[512,1536]{1,0:T(8,128)(2,1)} custom-call(s32[4]{0:T(128)} %get-tuple-element.52.picks_ref, bf16[512,1536]{1,0:T(8,128)(2,1)} %q_ref.7, bf16[512,1536]{1,0:T(8,128)(2,1)} %k0_ref.7, bf16[512,1536]{1,0:T(8,128)(2,1)} %v0_ref.7, bf16[512,1536]{1,0:T(8,128)(2,1)} %collective-permute-done.k1_ref, ...), custom_call_target="tpu_custom_call", output_to_operand_aliasing={{}: (12, {})} | custom-call | flops 666666688 | bytes 1000 | tf_op jit(solution)/shard_map/attend/pallas_call | solution.py:211
  137.1 10.2 %project.1 = bf16[512,3072]{1,0:T(8,128)(2,1)} custom-call(s32[10]{0:T(128)} %stack.68.place_ref, bf16[512,1536]{1,0:T(8,128)(2,1)} %attend.7.att_ref, bf16[4,384,384]{2,1,0:T(8,128)(2,1)} %pad_maximum_fusion.refs_0_, bf16[4,384,384]{2,1,0:T(8,128)(2,1)} %collective-permute-done.15.refs_1_, bf16[4,384,384]{2,1,0:T(8,128)(2,1)} %collective-permute-done.22.refs_2_, ...), custom_call_target="tpu_custom_call" | custom-call | flops 1000 | bytes 1000 | tf_op jit(solution)/shard_map/project/pallas_call | solution.py:297
  (82 shorter events, 17.5 us)
Async XLA Ops:
  0.0 15.3 %collective-permute-start = (bf16[512,1536]{1,0:T(8,128)(2,1)}, bf16[512,1536]{1,0:T(8,128)(2,1)}, u32[]{:S(2)}, u32[]{:S(2)}) collective-permute-start(bf16[512,1536]{1,0:T(8,128)(2,1)} %k0_ref.7), channel_id=1, source_target_pairs={{0,1},{1,0},{2,3},{3,2},{4,5},{5,4},{6,7},{7,6},{8,9},{9,8},{10,11... | collective-permute-start | bytes 4718600 | tf_op jit(solution)/shard_map/core_keys/ppermute | solution.py:27
  2.3 8.8 %collective-permute-start.1 = (bf16[384,192]{1,0:T(8,128)(2,1)}, bf16[384,192]{1,0:T(8,128)(2,1)S(1)}, u32[]{:S(2)}, u32[]{:S(2)}) collective-permute-start(bf16[384,192]{1,0:T(8,128)(2,1)} %copy.12), channel_id=1, source_target_pairs={{0,1},{1,0},{2,3},{3,2},{4,5},{5,4},{6,7},{7,6},{8,9},{9,8},{10,11... | collective-permute-start | bytes 442376 | tf_op jit(solution)/shard_map/w_core/ppermute | solution.py:27
  2.5 13.3 %collective-permute-start.2 = (bf16[512,1536]{1,0:T(8,128)(2,1)}, bf16[512,1536]{1,0:T(8,128)(2,1)}, u32[]{:S(2)}, u32[]{:S(2)}) collective-permute-start(bf16[512,1536]{1,0:T(8,128)(2,1)} %v0_ref.7), channel_id=1, source_target_pairs={{0,1},{1,0},{2,3},{3,2},{4,5},{5,4},{6,7},{7,6},{8,9},{9,8},{10,11... | collective-permute-start | bytes 4718600 | tf_op jit(solution)/shard_map/core_values/ppermute | solution.py:27
  4.8 23.1 %collective-permute-start.5 = (bf16[4,2,128,256]{3,2,1,0:T(8,128)(2,1)}, bf16[4,2,128,256]{3,2,1,0:T(8,128)(2,1)}, u32[]{:S(2)}, u32[]{:S(2)}) collective-permute-start(bf16[4,2,128,256]{3,2,1,0:T(8,128)(2,1)} %pad_maximum_fusion.6), channel_id=1, source_target_pairs={{0,2},{1,3},{2,0},{3,1},{4,6},{5,7},{6,4},{7,5},{8,10},{9,11},{10,... | collective-permute-start | bytes 1572872 | tf_op jit(solution)/shard_map/kv_y0/ppermute | solution.py:27
  11.3 11.7 %collective-permute-start.3 = (bf16[384,384]{1,0:T(8,128)(2,1)S(1)}, bf16[384,384]{1,0:T(8,128)(2,1)S(1)}, u32[]{:S(2)}, u32[]{:S(2)}) collective-permute-start(bf16[384,384]{1,0:T(8,128)(2,1)S(1)} %pad_maximum_fusion.7), channel_id=1, source_target_pairs={{0,4},{1,5},{2,6},{3,7},{4,8},{5,9},{6,10},{7,11},{8,12},{9,13},{1... | collective-permute-start | bytes 884744 | tf_op jit(solution)/shard_map/w_up/ppermute | solution.py:27
  12.9 15.0 %collective-permute-start.4 = (bf16[384,384]{1,0:T(8,128)(2,1)S(1)}, bf16[384,384]{1,0:T(8,128)(2,1)S(1)}, u32[]{:S(2)}, u32[]{:S(2)}) collective-permute-start(bf16[384,384]{1,0:T(8,128)(2,1)S(1)} %pad_maximum_fusion.7), channel_id=1, source_target_pairs={{0,12},{1,13},{2,14},{3,15},{4,0},{5,1},{6,2},{7,3},{8,4},{9,5},{1... | collective-permute-start | bytes 884744 | tf_op jit(solution)/shard_map/w_down/ppermute | solution.py:27
  15.3 27.6 %collective-permute-start.8 = (bf16[4,2,128,512]{3,2,1,0:T(8,128)(2,1)S(1)}, bf16[4,2,128,512]{3,2,1,0:T(8,128)(2,1)S(1)}, u32[]{:S(2)}, u32[]{:S(2)}) collective-permute-start(bf16[4,2,128,512]{3,2,1,0:T(8,128)(2,1)S(1)} %pad_maximum_fusion.1), channel_id=1, source_target_pairs={{0,2},{1,3},{2,0},{3,1},{4,6},{5,7},{6,4},{7,5},{8,10},{9,11},{10,... | collective-permute-start | bytes 3145736 | tf_op jit(solution)/shard_map/kv_y1/ppermute | solution.py:27
  15.7 49.6 %collective-permute-start.10 = (bf16[4,2,128,512]{3,2,1,0:T(8,128)(2,1)S(1)}, bf16[4,2,128,512]{3,2,1,0:T(8,128)(2,1)S(1)}, u32[]{:S(2)}, u32[]{:S(2)}) collective-permute-start(bf16[4,2,128,512]{3,2,1,0:T(8,128)(2,1)S(1)} %pad_maximum_fusion.2), channel_id=1, source_target_pairs={{0,2},{1,3},{2,0},{3,1},{4,6},{5,7},{6,4},{7,5},{8,10},{9,11},{10,... | collective-permute-start | bytes 3145736 | tf_op jit(solution)/shard_map/kv_y2/ppermute | solution.py:27
  28.0 11.7 %collective-permute-start.6 = (bf16[384,384]{1,0:T(8,128)(2,1)S(1)}, bf16[384,384]{1,0:T(8,128)(2,1)S(1)}, u32[]{:S(2)}, u32[]{:S(2)}) collective-permute-start(bf16[384,384]{1,0:T(8,128)(2,1)S(1)} %collective-permute-done.3), channel_id=1, source_target_pairs={{0,4},{1,5},{2,6},{3,7},{4,8},{5,9},{6,10},{7,11},{8,12},{9,13},{1... | collective-permute-start | bytes 884744 | tf_op jit(solution)/shard_map/w_up2/ppermute | solution.py:27
  29.1 20.2 %collective-permute-start.9 = (bf16[4,2,128,256]{3,2,1,0:T(8,128)(2,1)}, bf16[4,2,128,256]{3,2,1,0:T(8,128)(2,1)S(1)}, u32[]{:S(2)}, u32[]{:S(2)}) collective-permute-start(bf16[4,2,128,256]{3,2,1,0:T(8,128)(2,1)} %collective-permute-done.5.a_ref.b_ref), channel_id=1, source_target_pairs={{0,4},{1,5},{2,14},{3,15},{4,8},{5,9},{6,2},{7,3},{8,12},{9,13},{1... | collective-permute-start | bytes 1572872 | tf_op jit(solution)/shard_map/kv_z0/ppermute | solution.py:27
  40.6 50.7 %collective-permute-start.14 = (bf16[2,384,384]{2,1,0:T(8,128)(2,1)}, bf16[2,384,384]{2,1,0:T(8,128)(2,1)}, u32[]{:S(2)}, u32[]{:S(2)}) collective-permute-start(bf16[2,384,384]{2,1,0:T(8,128)(2,1)} %pad_maximum_fusion.3), channel_id=1, source_target_pairs={{0,2},{1,3},{2,0},{3,1},{4,6},{5,7},{6,4},{7,5},{8,10},{9,11},{10,... | collective-permute-start | bytes 1769480 | tf_op jit(solution)/shard_map/w_yx/ppermute | solution.py:27
  42.9 48.4 %copy-start.3 = (bf16[4,2,128,512]{3,2,1,0:T(8,128)(2,1)}, bf16[4,2,128,512]{3,2,1,0:T(8,128)(2,1)S(1)}, u32[]{:S(2)}) copy-start(bf16[4,2,128,512]{3,2,1,0:T(8,128)(2,1)S(1)} %collective-permute-done.8.a_ref.b_ref) | copy-start | bytes 3145732
  44.3 47.2 %collective-permute-start.15 = (bf16[4,384,384]{2,1,0:T(8,128)(2,1)}, bf16[4,384,384]{2,1,0:T(8,128)(2,1)}, u32[]{:S(2)}, u32[]{:S(2)}) collective-permute-start(bf16[4,384,384]{2,1,0:T(8,128)(2,1)} %pad_maximum_fusion.refs_0_), channel_id=1, source_target_pairs={{0,16},{1,17},{2,18},{3,19},{4,20},{5,21},{6,22},{7,23},{8,24},{9,... | collective-permute-start | bytes 3538952 | tf_op jit(solution)/shard_map/w_x1/ppermute | solution.py:37
  46.2 25.7 %collective-permute-start.11 = (bf16[4,2,128,512]{3,2,1,0:T(8,128)(2,1)S(1)}, bf16[4,2,128,512]{3,2,1,0:T(8,128)(2,1)S(1)}, u32[]{:S(2)}, u32[]{:S(2)}) collective-permute-start(bf16[4,2,128,512]{3,2,1,0:T(8,128)(2,1)S(1)} %collective-permute-done.8.a_ref.b_ref), channel_id=1, source_target_pairs={{0,4},{1,5},{2,14},{3,15},{4,8},{5,9},{6,2},{7,3},{8,12},{9,13},{1... | collective-permute-start | bytes 3145736 | tf_op jit(solution)/shard_map/kv_z1/ppermute | solution.py:27
  49.3 39.9 %collective-permute-start.7 = (bf16[4,2,128,256]{3,2,1,0:T(8,128)(2,1)}, bf16[4,2,128,256]{3,2,1,0:T(8,128)(2,1)S(1)}, u32[]{:S(2)}, u32[]{:S(2)}) collective-permute-start(bf16[4,2,128,256]{3,2,1,0:T(8,128)(2,1)} %pad_maximum_fusion.5), channel_id=1, source_target_pairs={{0,2},{1,3},{2,0},{3,1},{4,6},{5,7},{6,4},{7,5},{8,10},{9,11},{10,... | collective-permute-start | bytes 1572872 | tf_op jit(solution)/shard_map/kv_y3/ppermute | solution.py:27
  65.3 46.4 %copy-start.2 = (bf16[4,2,128,512]{3,2,1,0:T(8,128)(2,1)}, bf16[4,2,128,512]{3,2,1,0:T(8,128)(2,1)S(1)}, u32[]{:S(2)}) copy-start(bf16[4,2,128,512]{3,2,1,0:T(8,128)(2,1)S(1)} %collective-permute-done.10.a_ref.b_ref) | copy-start | bytes 3145732
  65.3 46.6 %collective-permute-start.18 = (bf16[2,384,384]{2,1,0:T(8,128)(2,1)}, bf16[2,384,384]{2,1,0:T(8,128)(2,1)}, u32[]{:S(2)}, u32[]{:S(2)}) collective-permute-start(bf16[2,384,384]{2,1,0:T(8,128)(2,1)} %pad_maximum_fusion.4), channel_id=1, source_target_pairs={{0,2},{1,3},{2,0},{3,1},{4,6},{5,7},{6,4},{7,5},{8,10},{9,11},{10,... | collective-permute-start | bytes 1769480 | tf_op jit(solution)/shard_map/w_yy/ppermute | solution.py:27
  71.9 1.9 %collective-permute-start.12 = (bf16[4,2,128,256]{3,2,1,0:T(8,128)(2,1)S(1)}, bf16[4,2,128,256]{3,2,1,0:T(8,128)(2,1)S(1)}, u32[]{:S(2)}, u32[]{:S(2)}) collective-permute-start(bf16[4,2,128,256]{3,2,1,0:T(8,128)(2,1)S(1)} %broadcast_select_fusion.3), channel_id=1, source_target_pairs={{0,1},{1,0},{2,3},{3,2},{4,5},{5,4},{6,7},{7,6},{8,9},{9,8},{10,11... | collective-permute-start | bytes 1572872 | tf_op jit(solution)/shard_map/kv_g0/ppermute | solution.py:27
  74.6 27.9 %collective-permute-start.16 = (bf16[4,2,128,512]{3,2,1,0:T(8,128)(2,1)S(1)}, bf16[4,2,128,512]{3,2,1,0:T(8,128)(2,1)}, u32[]{:S(2)}, u32[]{:S(2)}) collective-permute-start(bf16[4,2,128,512]{3,2,1,0:T(8,128)(2,1)S(1)} %collective-permute-done.10.a_ref.b_ref), channel_id=1, source_target_pairs={{0,4},{1,5},{2,14},{3,15},{4,8},{5,9},{6,2},{7,3},{8,12},{9,13},{1... | collective-permute-start | bytes 3145736 | tf_op jit(solution)/shard_map/kv_z2/ppermute | solution.py:27
  89.2 36.0 %copy-start.5 = (bf16[4,2,128,256]{3,2,1,0:T(8,128)(2,1)}, bf16[4,2,128,256]{3,2,1,0:T(8,128)(2,1)S(1)}, u32[]{:S(2)}) copy-start(bf16[4,2,128,256]{3,2,1,0:T(8,128)(2,1)S(1)} %collective-permute-done.7.a_ref.b_ref) | copy-start | bytes 1572868
  89.2 36.0 %collective-permute-start.13 = (bf16[4,2,128,256]{3,2,1,0:T(8,128)(2,1)S(1)}, bf16[4,2,128,256]{3,2,1,0:T(8,128)(2,1)}, u32[]{:S(2)}, u32[]{:S(2)}) collective-permute-start(bf16[4,2,128,256]{3,2,1,0:T(8,128)(2,1)S(1)} %collective-permute-done.7.a_ref.b_ref), channel_id=1, source_target_pairs={{0,4},{1,5},{2,14},{3,15},{4,8},{5,9},{6,2},{7,3},{8,12},{9,13},{1... | collective-permute-start | bytes 1572872 | tf_op jit(solution)/shard_map/kv_z3/ppermute | solution.py:27
  91.4 11.1 %collective-permute-start.17 = (bf16[4,2,128,512]{3,2,1,0:T(8,128)(2,1)S(1)}, bf16[4,2,128,512]{3,2,1,0:T(8,128)(2,1)}, u32[]{:S(2)}, u32[]{:S(2)}) collective-permute-start(bf16[4,2,128,512]{3,2,1,0:T(8,128)(2,1)S(1)} %broadcast_select_fusion.1), channel_id=1, source_target_pairs={{0,1},{1,0},{2,3},{3,2},{4,5},{5,4},{6,7},{7,6},{8,9},{9,8},{10,11... | collective-permute-start | bytes 3145736 | tf_op jit(solution)/shard_map/kv_g1/ppermute | solution.py:27
  91.5 21.8 %collective-permute-start.19 = (bf16[2,384,384]{2,1,0:T(8,128)(2,1)}, bf16[2,384,384]{2,1,0:T(8,128)(2,1)S(1)}, u32[]{:S(2)}, u32[]{:S(2)}) collective-permute-start(bf16[2,384,384]{2,1,0:T(8,128)(2,1)} %collective-permute-done.14.refs_4_), channel_id=1, source_target_pairs={{0,16},{1,17},{2,18},{3,19},{4,20},{5,21},{6,22},{7,23},{8,24},{9,... | collective-permute-start | bytes 1769480 | tf_op jit(solution)/shard_map/w_x2x/ppermute | solution.py:37
  102.5 33.2 %collective-permute-start.23 = (bf16[4,384,384]{2,1,0:T(8,128)(2,1)}, bf16[4,384,384]{2,1,0:T(8,128)(2,1)S(1)}, u32[]{:S(2)}, u32[]{:S(2)}) collective-permute-start(bf16[4,384,384]{2,1,0:T(8,128)(2,1)} %collective-permute-done.15.refs_1_), channel_id=1, source_target_pairs={{0,1},{1,0},{2,3},{3,2},{4,5},{5,4},{6,7},{7,6},{8,9},{9,8},{10,11... | collective-permute-start | bytes 3538952 | tf_op jit(solution)/shard_map/w_d1/ppermute | solution.py:27
  102.5 26.4 %collective-permute-start.22 = (bf16[4,384,384]{2,1,0:T(8,128)(2,1)}, bf16[4,384,384]{2,1,0:T(8,128)(2,1)}, u32[]{:S(2)}, u32[]{:S(2)}) collective-permute-start(bf16[4,384,384]{2,1,0:T(8,128)(2,1)} %pad_maximum_fusion.refs_0_), channel_id=1, source_target_pairs={{0,1},{1,0},{2,3},{3,2},{4,5},{5,4},{6,7},{7,6},{8,9},{9,8},{10,11... | collective-permute-start | bytes 3538952 | tf_op jit(solution)/shard_map/w_c1/ppermute | solution.py:27
  111.9 3.6 %collective-permute-start.20 = (bf16[4,2,128,512]{3,2,1,0:T(8,128)(2,1)S(1)}, bf16[4,2,128,512]{3,2,1,0:T(8,128)(2,1)S(1)}, u32[]{:S(2)}, u32[]{:S(2)}) collective-permute-start(bf16[4,2,128,512]{3,2,1,0:T(8,128)(2,1)S(1)} %broadcast_select_fusion), channel_id=1, source_target_pairs={{0,1},{1,0},{2,3},{3,2},{4,5},{5,4},{6,7},{7,6},{8,9},{9,8},{10,11... | collective-permute-start | bytes 3145736 | tf_op jit(solution)/shard_map/kv_g2/ppermute | solution.py:27
  113.3 15.6 %collective-permute-start.26 = (bf16[2,384,384]{2,1,0:T(8,128)(2,1)}, bf16[2,384,384]{2,1,0:T(8,128)(2,1)}, u32[]{:S(2)}, u32[]{:S(2)}) collective-permute-start(bf16[2,384,384]{2,1,0:T(8,128)(2,1)} %collective-permute-done.18.refs_8_), channel_id=1, source_target_pairs={{0,16},{1,17},{2,18},{3,19},{4,20},{5,21},{6,22},{7,23},{8,24},{9,... | collective-permute-start | bytes 1769480 | tf_op jit(solution)/shard_map/w_x2y/ppermute | solution.py:37
  125.3 4.1 %collective-permute-start.21 = (bf16[4,2,128,256]{3,2,1,0:T(8,128)(2,1)S(1)}, bf16[4,2,128,256]{3,2,1,0:T(8,128)(2,1)}, u32[]{:S(2)}, u32[]{:S(2)}) collective-permute-start(bf16[4,2,128,256]{3,2,1,0:T(8,128)(2,1)S(1)} %broadcast_select_fusion.2), channel_id=1, source_target_pairs={{0,1},{1,0},{2,3},{3,2},{4,5},{5,4},{6,7},{7,6},{8,9},{9,8},{10,11... | collective-permute-start | bytes 1572872 | tf_op jit(solution)/shard_map/kv_g3/ppermute | solution.py:27
  126.8 9.0 %collective-permute-start.24 = (bf16[2,384,384]{2,1,0:T(8,128)(2,1)}, bf16[2,384,384]{2,1,0:T(8,128)(2,1)S(1)}, u32[]{:S(2)}, u32[]{:S(2)}) collective-permute-start(bf16[2,384,384]{2,1,0:T(8,128)(2,1)} %collective-permute-done.14.refs_4_), channel_id=1, source_target_pairs={{0,1},{1,0},{2,3},{3,2},{4,5},{5,4},{6,7},{7,6},{8,9},{9,8},{10,11... | collective-permute-start | bytes 1769480 | tf_op jit(solution)/shard_map/w_c2x/ppermute | solution.py:27
  128.9 6.9 %collective-permute-start.25 = (bf16[2,384,384]{2,1,0:T(8,128)(2,1)S(1)}, bf16[2,384,384]{2,1,0:T(8,128)(2,1)S(1)}, u32[]{:S(2)}, u32[]{:S(2)}) collective-permute-start(bf16[2,384,384]{2,1,0:T(8,128)(2,1)S(1)} %collective-permute-done.19.refs_5_), channel_id=1, source_target_pairs={{0,1},{1,0},{2,3},{3,2},{4,5},{5,4},{6,7},{7,6},{8,9},{9,8},{10,11... | collective-permute-start | bytes 1769480 | tf_op jit(solution)/shard_map/w_d2x/ppermute | solution.py:27
  128.9 6.9 %collective-permute-start.28 = (bf16[2,384,384]{2,1,0:T(8,128)(2,1)}, bf16[2,384,384]{2,1,0:T(8,128)(2,1)}, u32[]{:S(2)}, u32[]{:S(2)}) collective-permute-start(bf16[2,384,384]{2,1,0:T(8,128)(2,1)} %collective-permute-done.26.refs_9_), channel_id=1, source_target_pairs={{0,1},{1,0},{2,3},{3,2},{4,5},{5,4},{6,7},{7,6},{8,9},{9,8},{10,11... | collective-permute-start | bytes 1769480 | tf_op jit(solution)/shard_map/w_d2y/ppermute | solution.py:27
  129.4 6.4 %collective-permute-start.27 = (bf16[2,384,384]{2,1,0:T(8,128)(2,1)}, bf16[2,384,384]{2,1,0:T(8,128)(2,1)}, u32[]{:S(2)}, u32[]{:S(2)}) collective-permute-start(bf16[2,384,384]{2,1,0:T(8,128)(2,1)} %collective-permute-done.18.refs_8_), channel_id=1, source_target_pairs={{0,1},{1,0},{2,3},{3,2},{4,5},{5,4},{6,7},{7,6},{8,9},{9,8},{10,11... | collective-permute-start | bytes 1769480 | tf_op jit(solution)/shard_map/w_c2y/ppermute | solution.py:27
  (11 other events, 74.6 us)

commit v5 on v4

--- a/solution.py
+++ b/solution.py
@@ -277,15 +277,15 @@
             out_ref[shift, mine, :] = jnp.dot(
                 held_ref[mine, :], w_ref[shift], preferred_element_type=jnp.float32
             ).astype(o_ref.dtype)
-        for flip in range(2):
-            to = pl.multiple_of((place_ref[6 + shift] * 2 + place_ref[4 + flip]) * cols, cols)
-            copy = pltpu.make_async_copy(
-                out_ref.at[shift, :, pl.ds(flip * cols, cols)],
-                o_ref.at[:, pl.ds(to, cols)],
-                out_sems.at[shift, flip],
-            )
-            copy.start()
-            out_copies.append(copy)
+            for flip in range(2):
+                to = pl.multiple_of((place_ref[6 + shift] * 2 + place_ref[4 + flip]) * cols, cols)
+                copy = pltpu.make_async_copy(
+                    out_ref.at[shift, pl.ds(m * half, half), pl.ds(flip * cols, cols)],
+                    o_ref.at[pl.ds(m * half, half), pl.ds(to, cols)],
+                    out_sems.at[shift, m * 2 + flip],
+                )
+                copy.start()
+                out_copies.append(copy)
     for copy in out_copies:
         copy.wait()
 
@@ -305,7 +305,7 @@
             pltpu.VMEM((shifts, rows, 2 * cols), jnp.bfloat16),
             pltpu.SemaphoreType.DMA((4,)),
             pltpu.SemaphoreType.DMA((shifts, 8)),
-            pltpu.SemaphoreType.DMA((shifts, 2)),
+            pltpu.SemaphoreType.DMA((shifts, 4)),
         ],
         compiler_params=pltpu.CompilerParams(vmem_limit_bytes=VMEM_LIMIT),
         cost_estimate=CHEAP,

time: 148 us -> 148 us (level)
  no operation moved by 1% of the time
where the time goes in v5:
time: 148 us; the launch traced here: 147 us
  waiting for transfers between devices  62.7 us (42%)
  Pallas kernels  40.2 us (27%)
  starting transfers between devices  29.5 us (20%)
  local copies, waits for them, and re-layouts  7.82 us (5%)
  other arithmetic  6.76 us (5%)
    ppermute x26, waiting for transfers between devices, moved(): return lax.ppermute(value, 'blk', [(s, dest(s)) for s in range(count)])  60.7 us
    pallas_call x4, Pallas kernels, attend(): pl.pallas_call(attend_kernel, grid_spec=pltpu.PrefetchScalarGridSpec(num_...  28.7 us
    ppermute x26, starting transfers between devices, moved(): return lax.ppermute(value, 'blk', [(s, dest(s)) for s in range(count)])  24.5 us
    pallas_call x1, Pallas kernels, project(): pl.pallas_call(project_kernel, in_specs=[pl.BlockSpec(memory_space=pltpu....  10.1 us
    ppermute x3, starting transfers between devices, moved_all(): return lax.ppermute(value, ('groups', 'blk'), pairs)  4.94 us
    unnamed x30, local copies, waits for them, and re-layouts  4.09 us
  transfers between devices with their start and end apart: 29, of which 12 were waited for; matrix products, arithmetic and copies ran while one was open for 8% of the time, Pallas kernels for 20%

profile of v5, /device:TPU:0, one launch (start us, length us, event | category | flops | bytes accessed | tf_op | source)
XLA Modules:
  0.0 147.4 jit_solution(12736126186420072533)
XLA Ops:
  4.8 2.6 %collective-permute-start.5 = (bf16[4,2,128,256]{3,2,1,0:T(8,128)(2,1)}, bf16[4,2,128,256]{3,2,1,0:T(8,128)(2,1)}, u32[]{:S(2)}, u32[]{:S(2)}) collective-permute-start(bf16[4,2,128,256]{3,2,1,0:T(8,128)(2,1)} %pad_maximum_fusion.6), channel_id=1, source_target_pairs={{0,2},{1,3},{2,0},{3,1},{4,6},{5,7},{6,4},{7,5},{8,10},{9,11},{10,... | collective-permute-start | bytes 1572872 | tf_op jit(solution)/shard_map/kv_y0/ppermute | solution.py:27
  9.4 1.4 plan.1
  11.3 1.6 %collective-permute-start.3 = (bf16[384,384]{1,0:T(8,128)(2,1)S(1)}, bf16[384,384]{1,0:T(8,128)(2,1)S(1)}, u32[]{:S(2)}, u32[]{:S(2)}) collective-permute-start(bf16[384,384]{1,0:T(8,128)(2,1)S(1)} %pad_maximum_fusion.7), channel_id=1, source_target_pairs={{0,4},{1,5},{2,6},{3,7},{4,8},{5,9},{6,10},{7,11},{8,12},{9,13},{1... | collective-permute-start | bytes 884744 | tf_op jit(solution)/shard_map/w_up/ppermute | solution.py:27
  12.9 2.2 %collective-permute-start.4 = (bf16[384,384]{1,0:T(8,128)(2,1)S(1)}, bf16[384,384]{1,0:T(8,128)(2,1)S(1)}, u32[]{:S(2)}, u32[]{:S(2)}) collective-permute-start(bf16[384,384]{1,0:T(8,128)(2,1)S(1)} %pad_maximum_fusion.7), channel_id=1, source_target_pairs={{0,12},{1,13},{2,14},{3,15},{4,0},{5,1},{6,2},{7,3},{8,4},{9,5},{1... | collective-permute-start | bytes 884744 | tf_op jit(solution)/shard_map/w_down/ppermute | solution.py:27
  15.7 1.7 %collective-permute-start.10 = (bf16[4,2,128,512]{3,2,1,0:T(8,128)(2,1)S(1)}, bf16[4,2,128,512]{3,2,1,0:T(8,128)(2,1)S(1)}, u32[]{:S(2)}, u32[]{:S(2)}) collective-permute-start(bf16[4,2,128,512]{3,2,1,0:T(8,128)(2,1)S(1)} %pad_maximum_fusion.2), channel_id=1, source_target_pairs={{0,2},{1,3},{2,0},{3,1},{4,6},{5,7},{6,4},{7,5},{8,10},{9,11},{10,... | collective-permute-start | bytes 3145736 | tf_op jit(solution)/shard_map/kv_y2/ppermute | solution.py:27
  17.4 5.6 %collective-permute-done.3 = bf16[384,384]{1,0:T(8,128)(2,1)S(1)} collective-permute-done((bf16[384,384]{1,0:T(8,128)(2,1)S(1)}, bf16[384,384]{1,0:T(8,128)(2,1)S(1)}, u32[]{:S(2)}, u32[]{:S(2)}) %collective-permute-start.3) | collective-permute-done | bytes 294944 | tf_op jit(solution)/shard_map/w_up/ppermute | solution.py:27
  23.0 4.9 %collective-permute-done.4 = bf16[384,384]{1,0:T(8,128)(2,1)S(1)} collective-permute-done((bf16[384,384]{1,0:T(8,128)(2,1)S(1)}, bf16[384,384]{1,0:T(8,128)(2,1)S(1)}, u32[]{:S(2)}, u32[]{:S(2)}) %collective-permute-start.4) | collective-permute-done | bytes 294944 | tf_op jit(solution)/shard_map/w_down/ppermute | solution.py:27
  28.0 1.1 collective-permute-start.6
  29.8 9.9 %collective-permute-done.6 = bf16[384,384]{1,0:T(8,128)(2,1)S(1)} collective-permute-done((bf16[384,384]{1,0:T(8,128)(2,1)S(1)}, bf16[384,384]{1,0:T(8,128)(2,1)S(1)}, u32[]{:S(2)}, u32[]{:S(2)}) %collective-permute-start.6) | collective-permute-done | bytes 294944 | tf_op jit(solution)/shard_map/w_up2/ppermute | solution.py:27
  41.1 1.8 %collective-permute-done.8.a_ref.b_ref = bf16[4,2,128,512]{3,2,1,0:T(8,128)(2,1)S(1)} collective-permute-done((bf16[4,2,128,512]{3,2,1,0:T(8,128)(2,1)S(1)}, bf16[4,2,128,512]{3,2,1,0:T(8,128)(2,1)S(1)}, u32[]{:S(2)}, u32[]{:S(2)}) %collective-permute-start.8) | collective-permute-done | bytes 1048608 | tf_op jit(solution)/shard_map/kv_y1/ppermute | solution.py:27
  42.9 1.4 pad_maximum_fusion.refs_0_
  44.3 2.0 %collective-permute-start.15 = (bf16[4,384,384]{2,1,0:T(8,128)(2,1)}, bf16[4,384,384]{2,1,0:T(8,128)(2,1)}, u32[]{:S(2)}, u32[]{:S(2)}) collective-permute-start(bf16[4,384,384]{2,1,0:T(8,128)(2,1)} %pad_maximum_fusion.refs_0_), channel_id=1, source_target_pairs={{0,16},{1,17},{2,18},{3,19},{4,20},{5,21},{6,22},{7,23},{8,24},{9,... | collective-permute-start | bytes 3538952 | tf_op jit(solution)/shard_map/w_x1/ppermute | solution.py:37
  46.2 1.6 %collective-permute-start.11 = (bf16[4,2,128,512]{3,2,1,0:T(8,128)(2,1)S(1)}, bf16[4,2,128,512]{3,2,1,0:T(8,128)(2,1)S(1)}, u32[]{:S(2)}, u32[]{:S(2)}) collective-permute-start(bf16[4,2,128,512]{3,2,1,0:T(8,128)(2,1)S(1)} %collective-permute-done.8.a_ref.b_ref), channel_id=1, source_target_pairs={{0,4},{1,5},{2,14},{3,15},{4,8},{5,9},{6,2},{7,3},{8,12},{9,13},{1... | collective-permute-start | bytes 3145736 | tf_op jit(solution)/shard_map/kv_z1/ppermute | solution.py:27
  49.3 2.9 %collective-permute-start.7 = (bf16[4,2,128,256]{3,2,1,0:T(8,128)(2,1)}, bf16[4,2,128,256]{3,2,1,0:T(8,128)(2,1)S(1)}, u32[]{:S(2)}, u32[]{:S(2)}) collective-permute-start(bf16[4,2,128,256]{3,2,1,0:T(8,128)(2,1)} %pad_maximum_fusion.5), channel_id=1, source_target_pairs={{0,2},{1,3},{2,0},{3,1},{4,6},{5,7},{6,4},{7,5},{8,10},{9,11},{10,... | collective-permute-start | bytes 1572872 | tf_op jit(solution)/shard_map/kv_y3/ppermute | solution.py:27
  52.2 13.1 %collective-permute-done.10.a_ref.b_ref = bf16[4,2,128,512]{3,2,1,0:T(8,128)(2,1)S(1)} collective-permute-done((bf16[4,2,128,512]{3,2,1,0:T(8,128)(2,1)S(1)}, bf16[4,2,128,512]{3,2,1,0:T(8,128)(2,1)S(1)}, u32[]{:S(2)}, u32[]{:S(2)}) %collective-permute-start.10) | collective-permute-done | bytes 1048608 | tf_op jit(solution)/shard_map/kv_y2/ppermute | solution.py:27
  65.3 2.0 %collective-permute-start.18 = (bf16[2,384,384]{2,1,0:T(8,128)(2,1)}, bf16[2,384,384]{2,1,0:T(8,128)(2,1)}, u32[]{:S(2)}, u32[]{:S(2)}) collective-permute-start(bf16[2,384,384]{2,1,0:T(8,128)(2,1)} %pad_maximum_fusion.4), channel_id=1, source_target_pairs={{0,2},{1,3},{2,0},{3,1},{4,6},{5,7},{6,4},{7,5},{8,10},{9,11},{10,... | collective-permute-start | bytes 1769480 | tf_op jit(solution)/shard_map/w_yy/ppermute | solution.py:27
  67.3 1.1 broadcast_select_fusion.3
  68.4 3.4 %collective-permute-done.11.c_ref.d_ref = bf16[4,2,128,512]{3,2,1,0:T(8,128)(2,1)S(1)} collective-permute-done((bf16[4,2,128,512]{3,2,1,0:T(8,128)(2,1)S(1)}, bf16[4,2,128,512]{3,2,1,0:T(8,128)(2,1)S(1)}, u32[]{:S(2)}, u32[]{:S(2)}) %collective-permute-start.11) | collective-permute-done | bytes 1048608 | tf_op jit(solution)/shard_map/kv_z1/ppermute | solution.py:27
  71.9 1.9 %collective-permute-done.12.near_ref = bf16[4,2,128,256]{3,2,1,0:T(8,128)(2,1)S(1)} collective-permute-done((bf16[4,2,128,256]{3,2,1,0:T(8,128)(2,1)S(1)}, bf16[4,2,128,256]{3,2,1,0:T(8,128)(2,1)S(1)}, u32[]{:S(2)}, u32[]{:S(2)}) %collective-permute-start.12) | collective-permute-done | bytes 524320 | tf_op jit(solution)/shard_map/kv_g0/ppermute | solution.py:27
  74.6 5.6 %attend.4.rest_0_ = bf16[512,1536]{1,0:T(8,128)(2,1)} custom-call(s32[4]{0:T(128)} %get-tuple-element.52.picks_ref, bf16[512,1536]{1,0:T(8,128)(2,1)} %q_ref.7, bf16[512,1536]{1,0:T(8,128)(2,1)} %k0_ref.7, bf16[512,1536]{1,0:T(8,128)(2,1)} %v0_ref.7, bf16[512,1536]{1,0:T(8,128)(2,1)} %collective-permute-done.k1_ref, ...), custom_call_target="tpu_custom_call" | custom-call | flops 666666688 | bytes 1000 | tf_op jit(solution)/shard_map/attend/pallas_call | solution.py:211
  80.2 9.0 %collective-permute-done.7.a_ref.b_ref = bf16[4,2,128,256]{3,2,1,0:T(8,128)(2,1)S(1)} collective-permute-done((bf16[4,2,128,256]{3,2,1,0:T(8,128)(2,1)}, bf16[4,2,128,256]{3,2,1,0:T(8,128)(2,1)S(1)}, u32[]{:S(2)}, u32[]{:S(2)}) %collective-permute-start.7) | collective-permute-done | bytes 524320 | tf_op jit(solution)/shard_map/kv_y3/ppermute | solution.py:27
  89.2 2.0 %collective-permute-start.13 = (bf16[4,2,128,256]{3,2,1,0:T(8,128)(2,1)S(1)}, bf16[4,2,128,256]{3,2,1,0:T(8,128)(2,1)}, u32[]{:S(2)}, u32[]{:S(2)}) collective-permute-start(bf16[4,2,128,256]{3,2,1,0:T(8,128)(2,1)S(1)} %collective-permute-done.7.a_ref.b_ref), channel_id=1, source_target_pairs={{0,4},{1,5},{2,14},{3,15},{4,8},{5,9},{6,2},{7,3},{8,12},{9,13},{1... | collective-permute-start | bytes 1572872 | tf_op jit(solution)/shard_map/kv_z3/ppermute | solution.py:27
  91.5 1.6 %collective-permute-start.19 = (bf16[2,384,384]{2,1,0:T(8,128)(2,1)}, bf16[2,384,384]{2,1,0:T(8,128)(2,1)S(1)}, u32[]{:S(2)}, u32[]{:S(2)}) collective-permute-start(bf16[2,384,384]{2,1,0:T(8,128)(2,1)} %collective-permute-done.14.refs_4_), channel_id=1, source_target_pairs={{0,16},{1,17},{2,18},{3,19},{4,20},{5,21},{6,22},{7,23},{8,24},{9,... | collective-permute-start | bytes 1769480 | tf_op jit(solution)/shard_map/w_x2x/ppermute | solution.py:37
  93.0 9.4 %collective-permute-done.16.c_ref.d_ref = bf16[4,2,128,512]{3,2,1,0:T(8,128)(2,1)} collective-permute-done((bf16[4,2,128,512]{3,2,1,0:T(8,128)(2,1)S(1)}, bf16[4,2,128,512]{3,2,1,0:T(8,128)(2,1)}, u32[]{:S(2)}, u32[]{:S(2)}) %collective-permute-start.16) | collective-permute-done | bytes 1048608 | tf_op jit(solution)/shard_map/kv_z2/ppermute | solution.py:27
  103.0 8.7 %attend.5.rest_0_ = bf16[512,1536]{1,0:T(8,128)(2,1)} custom-call(s32[4]{0:T(128)} %get-tuple-element.52.picks_ref, bf16[512,1536]{1,0:T(8,128)(2,1)} %q_ref.7, bf16[512,1536]{1,0:T(8,128)(2,1)} %k0_ref.7, bf16[512,1536]{1,0:T(8,128)(2,1)} %v0_ref.7, bf16[512,1536]{1,0:T(8,128)(2,1)} %collective-permute-done.k1_ref, ...), custom_call_target="tpu_custom_call", output_to_operand_aliasing={{}: (12, {})} | custom-call | flops 1333333376 | bytes 1000 | tf_op jit(solution)/shard_map/attend/pallas_call | solution.py:211
  111.9 1.4 collective-permute-start.20
  113.3 1.4 collective-permute-start.26
  116.5 8.8 %attend.6.rest_0_ = bf16[512,1536]{1,0:T(8,128)(2,1)} custom-call(s32[4]{0:T(128)} %get-tuple-element.52.picks_ref, bf16[512,1536]{1,0:T(8,128)(2,1)} %q_ref.7, bf16[512,1536]{1,0:T(8,128)(2,1)} %k0_ref.7, bf16[512,1536]{1,0:T(8,128)(2,1)} %v0_ref.7, bf16[512,1536]{1,0:T(8,128)(2,1)} %collective-permute-done.k1_ref, ...), custom_call_target="tpu_custom_call", output_to_operand_aliasing={{}: (12, {})} | custom-call | flops 1333333376 | bytes 1000 | tf_op jit(solution)/shard_map/attend/pallas_call | solution.py:211
  125.4 1.5 collective-permute-start.21
  126.9 2.0 %collective-permute-done.26.refs_9_ = bf16[2,384,384]{2,1,0:T(8,128)(2,1)} collective-permute-done((bf16[2,384,384]{2,1,0:T(8,128)(2,1)}, bf16[2,384,384]{2,1,0:T(8,128)(2,1)}, u32[]{:S(2)}, u32[]{:S(2)}) %collective-permute-start.26) | collective-permute-done | bytes 589856 | tf_op jit(solution)/shard_map/w_x2y/ppermute | solution.py:37
  130.1 5.6 %attend.7.att_ref = bf16[512,1536]{1,0:T(8,128)(2,1)} custom-call(s32[4]{0:T(128)} %get-tuple-element.52.picks_ref, bf16[512,1536]{1,0:T(8,128)(2,1)} %q_ref.7, bf16[512,1536]{1,0:T(8,128)(2,1)} %k0_ref.7, bf16[512,1536]{1,0:T(8,128)(2,1)} %v0_ref.7, bf16[512,1536]{1,0:T(8,128)(2,1)} %collective-permute-done.k1_ref, ...), custom_call_target="tpu_custom_call", output_to_operand_aliasing={{}: (12, {})} | custom-call | flops 666666688 | bytes 1000 | tf_op jit(solution)/shard_map/attend/pallas_call | solution.py:211
  137.1 10.1 %project.1 = bf16[512,3072]{1,0:T(8,128)(2,1)} custom-call(s32[10]{0:T(128)} %stack.68.place_ref, bf16[512,1536]{1,0:T(8,128)(2,1)} %attend.7.att_ref, bf16[4,384,384]{2,1,0:T(8,128)(2,1)} %pad_maximum_fusion.refs_0_, bf16[4,384,384]{2,1,0:T(8,128)(2,1)} %collective-permute-done.15.refs_1_, bf16[4,384,384]{2,1,0:T(8,128)(2,1)} %collective-permute-done.22.refs_2_, ...), custom_call_target="tpu_custom_call" | custom-call | flops 1000 | bytes 1000 | tf_op jit(solution)/shard_map/project/pallas_call | solution.py:297
  (82 shorter events, 17.5 us)
Async XLA Ops:
  0.0 15.3 %collective-permute-start = (bf16[512,1536]{1,0:T(8,128)(2,1)}, bf16[512,1536]{1,0:T(8,128)(2,1)}, u32[]{:S(2)}, u32[]{:S(2)}) collective-permute-start(bf16[512,1536]{1,0:T(8,128)(2,1)} %k0_ref.7), channel_id=1, source_target_pairs={{0,1},{1,0},{2,3},{3,2},{4,5},{5,4},{6,7},{7,6},{8,9},{9,8},{10,11... | collective-permute-start | bytes 4718600 | tf_op jit(solution)/shard_map/core_keys/ppermute | solution.py:27
  2.3 8.8 %collective-permute-start.1 = (bf16[384,192]{1,0:T(8,128)(2,1)}, bf16[384,192]{1,0:T(8,128)(2,1)S(1)}, u32[]{:S(2)}, u32[]{:S(2)}) collective-permute-start(bf16[384,192]{1,0:T(8,128)(2,1)} %copy.12), channel_id=1, source_target_pairs={{0,1},{1,0},{2,3},{3,2},{4,5},{5,4},{6,7},{7,6},{8,9},{9,8},{10,11... | collective-permute-start | bytes 442376 | tf_op jit(solution)/shard_map/w_core/ppermute | solution.py:27
  2.5 13.3 %collective-permute-start.2 = (bf16[512,1536]{1,0:T(8,128)(2,1)}, bf16[512,1536]{1,0:T(8,128)(2,1)}, u32[]{:S(2)}, u32[]{:S(2)}) collective-permute-start(bf16[512,1536]{1,0:T(8,128)(2,1)} %v0_ref.7), channel_id=1, source_target_pairs={{0,1},{1,0},{2,3},{3,2},{4,5},{5,4},{6,7},{7,6},{8,9},{9,8},{10,11... | collective-permute-start | bytes 4718600 | tf_op jit(solution)/shard_map/core_values/ppermute | solution.py:27
  4.8 23.1 %collective-permute-start.5 = (bf16[4,2,128,256]{3,2,1,0:T(8,128)(2,1)}, bf16[4,2,128,256]{3,2,1,0:T(8,128)(2,1)}, u32[]{:S(2)}, u32[]{:S(2)}) collective-permute-start(bf16[4,2,128,256]{3,2,1,0:T(8,128)(2,1)} %pad_maximum_fusion.6), channel_id=1, source_target_pairs={{0,2},{1,3},{2,0},{3,1},{4,6},{5,7},{6,4},{7,5},{8,10},{9,11},{10,... | collective-permute-start | bytes 1572872 | tf_op jit(solution)/shard_map/kv_y0/ppermute | solution.py:27
  11.3 11.7 %collective-permute-start.3 = (bf16[384,384]{1,0:T(8,128)(2,1)S(1)}, bf16[384,384]{1,0:T(8,128)(2,1)S(1)}, u32[]{:S(2)}, u32[]{:S(2)}) collective-permute-start(bf16[384,384]{1,0:T(8,128)(2,1)S(1)} %pad_maximum_fusion.7), channel_id=1, source_target_pairs={{0,4},{1,5},{2,6},{3,7},{4,8},{5,9},{6,10},{7,11},{8,12},{9,13},{1... | collective-permute-start | bytes 884744 | tf_op jit(solution)/shard_map/w_up/ppermute | solution.py:27
  12.9 15.0 %collective-permute-start.4 = (bf16[384,384]{1,0:T(8,128)(2,1)S(1)}, bf16[384,384]{1,0:T(8,128)(2,1)S(1)}, u32[]{:S(2)}, u32[]{:S(2)}) collective-permute-start(bf16[384,384]{1,0:T(8,128)(2,1)S(1)} %pad_maximum_fusion.7), channel_id=1, source_target_pairs={{0,12},{1,13},{2,14},{3,15},{4,0},{5,1},{6,2},{7,3},{8,4},{9,5},{1... | collective-permute-start | bytes 884744 | tf_op jit(solution)/shard_map/w_down/ppermute | solution.py:27
  15.3 27.6 %collective-permute-start.8 = (bf16[4,2,128,512]{3,2,1,0:T(8,128)(2,1)S(1)}, bf16[4,2,128,512]{3,2,1,0:T(8,128)(2,1)S(1)}, u32[]{:S(2)}, u32[]{:S(2)}) collective-permute-start(bf16[4,2,128,512]{3,2,1,0:T(8,128)(2,1)S(1)} %pad_maximum_fusion.1), channel_id=1, source_target_pairs={{0,2},{1,3},{2,0},{3,1},{4,6},{5,7},{6,4},{7,5},{8,10},{9,11},{10,... | collective-permute-start | bytes 3145736 | tf_op jit(solution)/shard_map/kv_y1/ppermute | solution.py:27
  15.7 49.6 %collective-permute-start.10 = (bf16[4,2,128,512]{3,2,1,0:T(8,128)(2,1)S(1)}, bf16[4,2,128,512]{3,2,1,0:T(8,128)(2,1)S(1)}, u32[]{:S(2)}, u32[]{:S(2)}) collective-permute-start(bf16[4,2,128,512]{3,2,1,0:T(8,128)(2,1)S(1)} %pad_maximum_fusion.2), channel_id=1, source_target_pairs={{0,2},{1,3},{2,0},{3,1},{4,6},{5,7},{6,4},{7,5},{8,10},{9,11},{10,... | collective-permute-start | bytes 3145736 | tf_op jit(solution)/shard_map/kv_y2/ppermute | solution.py:27
  28.0 11.7 %collective-permute-start.6 = (bf16[384,384]{1,0:T(8,128)(2,1)S(1)}, bf16[384,384]{1,0:T(8,128)(2,1)S(1)}, u32[]{:S(2)}, u32[]{:S(2)}) collective-permute-start(bf16[384,384]{1,0:T(8,128)(2,1)S(1)} %collective-permute-done.3), channel_id=1, source_target_pairs={{0,4},{1,5},{2,6},{3,7},{4,8},{5,9},{6,10},{7,11},{8,12},{9,13},{1... | collective-permute-start | bytes 884744 | tf_op jit(solution)/shard_map/w_up2/ppermute | solution.py:27
  29.1 20.2 %collective-permute-start.9 = (bf16[4,2,128,256]{3,2,1,0:T(8,128)(2,1)}, bf16[4,2,128,256]{3,2,1,0:T(8,128)(2,1)S(1)}, u32[]{:S(2)}, u32[]{:S(2)}) collective-permute-start(bf16[4,2,128,256]{3,2,1,0:T(8,128)(2,1)} %collective-permute-done.5.a_ref.b_ref), channel_id=1, source_target_pairs={{0,4},{1,5},{2,14},{3,15},{4,8},{5,9},{6,2},{7,3},{8,12},{9,13},{1... | collective-permute-start | bytes 1572872 | tf_op jit(solution)/shard_map/kv_z0/ppermute | solution.py:27
  40.6 50.7 %collective-permute-start.14 = (bf16[2,384,384]{2,1,0:T(8,128)(2,1)}, bf16[2,384,384]{2,1,0:T(8,128)(2,1)}, u32[]{:S(2)}, u32[]{:S(2)}) collective-permute-start(bf16[2,384,384]{2,1,0:T(8,128)(2,1)} %pad_maximum_fusion.3), channel_id=1, source_target_pairs={{0,2},{1,3},{2,0},{3,1},{4,6},{5,7},{6,4},{7,5},{8,10},{9,11},{10,... | collective-permute-start | bytes 1769480 | tf_op jit(solution)/shard_map/w_yx/ppermute | solution.py:27
  42.9 48.4 %copy-start.3 = (bf16[4,2,128,512]{3,2,1,0:T(8,128)(2,1)}, bf16[4,2,128,512]{3,2,1,0:T(8,128)(2,1)S(1)}, u32[]{:S(2)}) copy-start(bf16[4,2,128,512]{3,2,1,0:T(8,128)(2,1)S(1)} %collective-permute-done.8.a_ref.b_ref) | copy-start | bytes 3145732
  44.3 47.2 %collective-permute-start.15 = (bf16[4,384,384]{2,1,0:T(8,128)(2,1)}, bf16[4,384,384]{2,1,0:T(8,128)(2,1)}, u32[]{:S(2)}, u32[]{:S(2)}) collective-permute-start(bf16[4,384,384]{2,1,0:T(8,128)(2,1)} %pad_maximum_fusion.refs_0_), channel_id=1, source_target_pairs={{0,16},{1,17},{2,18},{3,19},{4,20},{5,21},{6,22},{7,23},{8,24},{9,... | collective-permute-start | bytes 3538952 | tf_op jit(solution)/shard_map/w_x1/ppermute | solution.py:37
  46.2 25.7 %collective-permute-start.11 = (bf16[4,2,128,512]{3,2,1,0:T(8,128)(2,1)S(1)}, bf16[4,2,128,512]{3,2,1,0:T(8,128)(2,1)S(1)}, u32[]{:S(2)}, u32[]{:S(2)}) collective-permute-start(bf16[4,2,128,512]{3,2,1,0:T(8,128)(2,1)S(1)} %collective-permute-done.8.a_ref.b_ref), channel_id=1, source_target_pairs={{0,4},{1,5},{2,14},{3,15},{4,8},{5,9},{6,2},{7,3},{8,12},{9,13},{1... | collective-permute-start | bytes 3145736 | tf_op jit(solution)/shard_map/kv_z1/ppermute | solution.py:27
  49.3 39.9 %collective-permute-start.7 = (bf16[4,2,128,256]{3,2,1,0:T(8,128)(2,1)}, bf16[4,2,128,256]{3,2,1,0:T(8,128)(2,1)S(1)}, u32[]{:S(2)}, u32[]{:S(2)}) collective-permute-start(bf16[4,2,128,256]{3,2,1,0:T(8,128)(2,1)} %pad_maximum_fusion.5), channel_id=1, source_target_pairs={{0,2},{1,3},{2,0},{3,1},{4,6},{5,7},{6,4},{7,5},{8,10},{9,11},{10,... | collective-permute-start | bytes 1572872 | tf_op jit(solution)/shard_map/kv_y3/ppermute | solution.py:27
  65.3 46.4 %copy-start.2 = (bf16[4,2,128,512]{3,2,1,0:T(8,128)(2,1)}, bf16[4,2,128,512]{3,2,1,0:T(8,128)(2,1)S(1)}, u32[]{:S(2)}) copy-start(bf16[4,2,128,512]{3,2,1,0:T(8,128)(2,1)S(1)} %collective-permute-done.10.a_ref.b_ref) | copy-start | bytes 3145732
  65.3 46.5 %collective-permute-start.18 = (bf16[2,384,384]{2,1,0:T(8,128)(2,1)}, bf16[2,384,384]{2,1,0:T(8,128)(2,1)}, u32[]{:S(2)}, u32[]{:S(2)}) collective-permute-start(bf16[2,384,384]{2,1,0:T(8,128)(2,1)} %pad_maximum_fusion.4), channel_id=1, source_target_pairs={{0,2},{1,3},{2,0},{3,1},{4,6},{5,7},{6,4},{7,5},{8,10},{9,11},{10,... | collective-permute-start | bytes 1769480 | tf_op jit(solution)/shard_map/w_yy/ppermute | solution.py:27
  71.9 1.9 %collective-permute-start.12 = (bf16[4,2,128,256]{3,2,1,0:T(8,128)(2,1)S(1)}, bf16[4,2,128,256]{3,2,1,0:T(8,128)(2,1)S(1)}, u32[]{:S(2)}, u32[]{:S(2)}) collective-permute-start(bf16[4,2,128,256]{3,2,1,0:T(8,128)(2,1)S(1)} %broadcast_select_fusion.3), channel_id=1, source_target_pairs={{0,1},{1,0},{2,3},{3,2},{4,5},{5,4},{6,7},{7,6},{8,9},{9,8},{10,11... | collective-permute-start | bytes 1572872 | tf_op jit(solution)/shard_map/kv_g0/ppermute | solution.py:27
  74.6 27.9 %collective-permute-start.16 = (bf16[4,2,128,512]{3,2,1,0:T(8,128)(2,1)S(1)}, bf16[4,2,128,512]{3,2,1,0:T(8,128)(2,1)}, u32[]{:S(2)}, u32[]{:S(2)}) collective-permute-start(bf16[4,2,128,512]{3,2,1,0:T(8,128)(2,1)S(1)} %collective-permute-done.10.a_ref.b_ref), channel_id=1, source_target_pairs={{0,4},{1,5},{2,14},{3,15},{4,8},{5,9},{6,2},{7,3},{8,12},{9,13},{1... | collective-permute-start | bytes 3145736 | tf_op jit(solution)/shard_map/kv_z2/ppermute | solution.py:27
  89.2 36.1 %copy-start.5 = (bf16[4,2,128,256]{3,2,1,0:T(8,128)(2,1)}, bf16[4,2,128,256]{3,2,1,0:T(8,128)(2,1)S(1)}, u32[]{:S(2)}) copy-start(bf16[4,2,128,256]{3,2,1,0:T(8,128)(2,1)S(1)} %collective-permute-done.7.a_ref.b_ref) | copy-start | bytes 1572868
  89.2 36.1 %collective-permute-start.13 = (bf16[4,2,128,256]{3,2,1,0:T(8,128)(2,1)S(1)}, bf16[4,2,128,256]{3,2,1,0:T(8,128)(2,1)}, u32[]{:S(2)}, u32[]{:S(2)}) collective-permute-start(bf16[4,2,128,256]{3,2,1,0:T(8,128)(2,1)S(1)} %collective-permute-done.7.a_ref.b_ref), channel_id=1, source_target_pairs={{0,4},{1,5},{2,14},{3,15},{4,8},{5,9},{6,2},{7,3},{8,12},{9,13},{1... | collective-permute-start | bytes 1572872 | tf_op jit(solution)/shard_map/kv_z3/ppermute | solution.py:27
  91.4 11.1 %collective-permute-start.17 = (bf16[4,2,128,512]{3,2,1,0:T(8,128)(2,1)S(1)}, bf16[4,2,128,512]{3,2,1,0:T(8,128)(2,1)}, u32[]{:S(2)}, u32[]{:S(2)}) collective-permute-start(bf16[4,2,128,512]{3,2,1,0:T(8,128)(2,1)S(1)} %broadcast_select_fusion.1), channel_id=1, source_target_pairs={{0,1},{1,0},{2,3},{3,2},{4,5},{5,4},{6,7},{7,6},{8,9},{9,8},{10,11... | collective-permute-start | bytes 3145736 | tf_op jit(solution)/shard_map/kv_g1/ppermute | solution.py:27
  91.5 21.8 %collective-permute-start.19 = (bf16[2,384,384]{2,1,0:T(8,128)(2,1)}, bf16[2,384,384]{2,1,0:T(8,128)(2,1)S(1)}, u32[]{:S(2)}, u32[]{:S(2)}) collective-permute-start(bf16[2,384,384]{2,1,0:T(8,128)(2,1)} %collective-permute-done.14.refs_4_), channel_id=1, source_target_pairs={{0,16},{1,17},{2,18},{3,19},{4,20},{5,21},{6,22},{7,23},{8,24},{9,... | collective-permute-start | bytes 1769480 | tf_op jit(solution)/shard_map/w_x2x/ppermute | solution.py:37
  102.5 33.2 %collective-permute-start.23 = (bf16[4,384,384]{2,1,0:T(8,128)(2,1)}, bf16[4,384,384]{2,1,0:T(8,128)(2,1)S(1)}, u32[]{:S(2)}, u32[]{:S(2)}) collective-permute-start(bf16[4,384,384]{2,1,0:T(8,128)(2,1)} %collective-permute-done.15.refs_1_), channel_id=1, source_target_pairs={{0,1},{1,0},{2,3},{3,2},{4,5},{5,4},{6,7},{7,6},{8,9},{9,8},{10,11... | collective-permute-start | bytes 3538952 | tf_op jit(solution)/shard_map/w_d1/ppermute | solution.py:27
  102.5 26.4 %collective-permute-start.22 = (bf16[4,384,384]{2,1,0:T(8,128)(2,1)}, bf16[4,384,384]{2,1,0:T(8,128)(2,1)}, u32[]{:S(2)}, u32[]{:S(2)}) collective-permute-start(bf16[4,384,384]{2,1,0:T(8,128)(2,1)} %pad_maximum_fusion.refs_0_), channel_id=1, source_target_pairs={{0,1},{1,0},{2,3},{3,2},{4,5},{5,4},{6,7},{7,6},{8,9},{9,8},{10,11... | collective-permute-start | bytes 3538952 | tf_op jit(solution)/shard_map/w_c1/ppermute | solution.py:27
  111.9 3.6 %collective-permute-start.20 = (bf16[4,2,128,512]{3,2,1,0:T(8,128)(2,1)S(1)}, bf16[4,2,128,512]{3,2,1,0:T(8,128)(2,1)S(1)}, u32[]{:S(2)}, u32[]{:S(2)}) collective-permute-start(bf16[4,2,128,512]{3,2,1,0:T(8,128)(2,1)S(1)} %broadcast_select_fusion), channel_id=1, source_target_pairs={{0,1},{1,0},{2,3},{3,2},{4,5},{5,4},{6,7},{7,6},{8,9},{9,8},{10,11... | collective-permute-start | bytes 3145736 | tf_op jit(solution)/shard_map/kv_g2/ppermute | solution.py:27
  113.3 15.6 %collective-permute-start.26 = (bf16[2,384,384]{2,1,0:T(8,128)(2,1)}, bf16[2,384,384]{2,1,0:T(8,128)(2,1)}, u32[]{:S(2)}, u32[]{:S(2)}) collective-permute-start(bf16[2,384,384]{2,1,0:T(8,128)(2,1)} %collective-permute-done.18.refs_8_), channel_id=1, source_target_pairs={{0,16},{1,17},{2,18},{3,19},{4,20},{5,21},{6,22},{7,23},{8,24},{9,... | collective-permute-start | bytes 1769480 | tf_op jit(solution)/shard_map/w_x2y/ppermute | solution.py:37
  125.4 4.0 %collective-permute-start.21 = (bf16[4,2,128,256]{3,2,1,0:T(8,128)(2,1)S(1)}, bf16[4,2,128,256]{3,2,1,0:T(8,128)(2,1)}, u32[]{:S(2)}, u32[]{:S(2)}) collective-permute-start(bf16[4,2,128,256]{3,2,1,0:T(8,128)(2,1)S(1)} %broadcast_select_fusion.2), channel_id=1, source_target_pairs={{0,1},{1,0},{2,3},{3,2},{4,5},{5,4},{6,7},{7,6},{8,9},{9,8},{10,11... | collective-permute-start | bytes 1572872 | tf_op jit(solution)/shard_map/kv_g3/ppermute | solution.py:27
  126.8 8.9 %collective-permute-start.24 = (bf16[2,384,384]{2,1,0:T(8,128)(2,1)}, bf16[2,384,384]{2,1,0:T(8,128)(2,1)S(1)}, u32[]{:S(2)}, u32[]{:S(2)}) collective-permute-start(bf16[2,384,384]{2,1,0:T(8,128)(2,1)} %collective-permute-done.14.refs_4_), channel_id=1, source_target_pairs={{0,1},{1,0},{2,3},{3,2},{4,5},{5,4},{6,7},{7,6},{8,9},{9,8},{10,11... | collective-permute-start | bytes 1769480 | tf_op jit(solution)/shard_map/w_c2x/ppermute | solution.py:27
  128.9 6.9 %collective-permute-start.25 = (bf16[2,384,384]{2,1,0:T(8,128)(2,1)S(1)}, bf16[2,384,384]{2,1,0:T(8,128)(2,1)S(1)}, u32[]{:S(2)}, u32[]{:S(2)}) collective-permute-start(bf16[2,384,384]{2,1,0:T(8,128)(2,1)S(1)} %collective-permute-done.19.refs_5_), channel_id=1, source_target_pairs={{0,1},{1,0},{2,3},{3,2},{4,5},{5,4},{6,7},{7,6},{8,9},{9,8},{10,11... | collective-permute-start | bytes 1769480 | tf_op jit(solution)/shard_map/w_d2x/ppermute | solution.py:27
  128.9 6.9 %collective-permute-start.28 = (bf16[2,384,384]{2,1,0:T(8,128)(2,1)}, bf16[2,384,384]{2,1,0:T(8,128)(2,1)}, u32[]{:S(2)}, u32[]{:S(2)}) collective-permute-start(bf16[2,384,384]{2,1,0:T(8,128)(2,1)} %collective-permute-done.26.refs_9_), channel_id=1, source_target_pairs={{0,1},{1,0},{2,3},{3,2},{4,5},{5,4},{6,7},{7,6},{8,9},{9,8},{10,11... | collective-permute-start | bytes 1769480 | tf_op jit(solution)/shard_map/w_d2y/ppermute | solution.py:27
  129.4 6.4 %collective-permute-start.27 = (bf16[2,384,384]{2,1,0:T(8,128)(2,1)}, bf16[2,384,384]{2,1,0:T(8,128)(2,1)}, u32[]{:S(2)}, u32[]{:S(2)}) collective-permute-start(bf16[2,384,384]{2,1,0:T(8,128)(2,1)} %collective-permute-done.18.refs_8_), channel_id=1, source_target_pairs={{0,1},{1,0},{2,3},{3,2},{4,5},{5,4},{6,7},{7,6},{8,9},{9,8},{10,11... | collective-permute-start | bytes 1769480 | tf_op jit(solution)/shard_map/w_c2y/ppermute | solution.py:27
  (11 other events, 74.6 us)
